TPU v7x, 32 devices: a whole 2x2x4 slice. The times are simulated.
32 devices in a mesh: island: 8 (over z, x), tensor: 4 (over y, core).
Axes of the slice: x: 2, y: 2, z: 4, core: 2. Of those that a mesh axis runs over, the one named last changes fastest.
Arguments:
- hidden: bfloat16 [8, 512, 14336], P('island', None, 'tensor'), may hold values from -6 to 6
- island_weights: bfloat16 [8, 4096, 14336], P('island', None, 'tensor'), may hold values from -6 to 6
- targets: bfloat16 [8, 4096, 512], P('island', 'tensor'), may hold values from -6 to 6
- global_weights: float32 [1024, 14336], P('island', 'tensor'), may hold values from -6 to 6
- momentum: float32 [1024, 14336], P('island', 'tensor'), may hold values from -3 to 3
Outputs:
- mixed: bfloat16 [8, 1024, 14336], P('island', None, 'tensor')
- new_global: float32 [1024, 14336], P('island', 'tensor')
- new_momentum: float32 [1024, 14336], P('island', 'tensor')
- grad_hidden: bfloat16 [8, 512, 14336], P('island', None, 'tensor')
All inputs are finite; a program needn't handle non-finite values.
Results may differ from a plain program's by a relative error of at most 0.015.
Values may be sent and summed in bfloat16 or wider, within the bound.
No kernel may reach another device: no remote copies, remote signals or barrier semaphores. Data moves between devices by JAX's collectives and lax.ppermute only.
A program may use at most 192 MiB of HBM per device.

v0:
```python
import math

import jax
import jax.numpy as jnp
from jax import lax
from jax.sharding import PartitionSpec as P

FF = 14336
FRAG = 1024


inner_rate = 0.3
outer_rate = 0.7
outer_beta = 0.9
mix_share = 0.5


def shards(hidden, island_weights, targets, global_weights, momentum):
    activations = hidden[0]
    weights = island_weights[0]
    goals = targets[0]
    scale = 1.0 / math.sqrt(FF)
    outputs = lax.psum_scatter(
        (
            lax.dot_general(
                weights, activations, (((1,), (1,)), ((), ())), preferred_element_type=jnp.float32
            )
            * scale
        ).astype(jnp.bfloat16),
        "tensor",
        scatter_dimension=0,
        tiled=True,
    ).astype(jnp.float32)
    residue = (outputs - goals.astype(jnp.float32)).astype(jnp.bfloat16)
    full_residue = lax.all_gather(residue, "tensor", axis=0, tiled=True)
    back = (
        lax.dot_general(
            full_residue, weights, (((0,), (0,)), ((), ())), preferred_element_type=jnp.float32
        )
        * scale
    )
    grad_hidden = back.astype(jnp.bfloat16)
    part_residue = lax.slice_in_dim(full_residue, 0, FRAG, axis=0)
    grad = jnp.dot(part_residue, activations, preferred_element_type=jnp.float32) * scale
    base = lax.slice_in_dim(weights, 0, FRAG, axis=0).astype(jnp.float32)
    stored = base - inner_rate * grad
    islands = lax.axis_size("island")
    total = lax.psum(stored.astype(jnp.bfloat16), "island").astype(jnp.float32)
    full_global, full_momentum = (
        lax.all_gather(global_weights.astype(jnp.bfloat16), "island", axis=0, tiled=True).astype(
            global_weights.dtype
        ),
        lax.all_gather(momentum.astype(jnp.bfloat16), "island", axis=0, tiled=True).astype(
            momentum.dtype
        ),
    )
    pseudo = full_global - total / islands
    momentum_all = outer_beta * full_momentum + pseudo
    global_all = full_global - outer_rate * (pseudo + outer_beta * momentum_all)
    mixed = (mix_share * stored + (1.0 - mix_share) * global_all).astype(jnp.bfloat16)
    row_count = global_weights.shape[0]
    offset = lax.axis_index("island") * row_count
    new_global = lax.dynamic_slice_in_dim(global_all, offset, row_count, 0)
    new_momentum = lax.dynamic_slice_in_dim(momentum_all, offset, row_count, 0)
    return (mixed[None], new_global, new_momentum, grad_hidden[None])


def solution(mesh):
    return jax.shard_map(
        shards,
        mesh=mesh,
        in_specs=(
            P("island", None, "tensor"),
            P("island", None, "tensor"),
            P("island", "tensor", None),
            P("island", "tensor"),
            P("island", "tensor"),
        ),
        out_specs=(
            P("island", None, "tensor"),
            P("island", "tensor"),
            P("island", "tensor"),
            P("island", None, "tensor"),
        ),
        check_vma=False,
    )
```

profile of v0, /device:TPU:0, one launch (start us, length us, event | category | flops | bytes accessed | tf_op | source)
XLA Modules:
  0.0 618.2 jit_solution(15736938271436173029)
XLA Ops:
  7.2 0.0 copy-start.1
  7.2 0.0 reduce-scatter.2.cloned.1.call-start
  7.2 22.0 %multiply_convert_fusion.1 = bf16[4096,512]{1,0:T(8,128)(2,1)} fusion(bf16[1,4096,3584]{2,1,0:T(8,128)(2,1)} %param.6, bf16[1,512,3584]{2,1,0:T(8,128)(2,1)} %param.5), kind=kOutput, calls=%fused_computation.10 | convolution fusion | flops 15036579840 | bytes 37224448 | tf_op jit(solution)/shard_map/dot_general | solution.py:25
  29.2 0.0 copy-start
  29.2 0.0 reduce-scatter.2.cloned.1.call-update
  29.2 0.0 all-gather.4.cloned.1.call-start
  29.3 47.3 %reduce-scatter.2.cloned.1.call-done = bf16[1024,512]{1,0:T(8,128)(2,1)} async-done(((bf16[4096,512]{1,0:T(8,128)(2,1)}), bf16[1024,512]{1,0:T(8,128)(2,1)}) %reduce-scatter.2.cloned.1.call-update) | async-done | bytes 1048592 | tf_op jit(solution)/shard_map/reduce_scatter | solution.py:23
  76.6 0.0 copy-done.1
  76.6 2.5 fusion.16
  79.1 0.0 all-gather.4.cloned.1.call-update
  79.1 0.0 all-gather.6.cloned.1.call-start
  79.2 0.0 copy-done
  79.2 1.0 convert_element_type.52
  80.2 0.0 all-gather.6.cloned.1.call-update
  80.3 0.0 all-gather.8.cloned.1.call-start
  80.3 2.5 convert_element_type.56
  82.8 0.0 all-gather.8.cloned.1.call-update
  82.8 0.0 all-reduce.2.cloned.1.call-start
  82.9 30.9 %all-gather.4.cloned.1.call-done = bf16[4096,512]{1,0:T(8,128)(2,1)} async-done(((bf16[1024,512]{1,0:T(8,128)(2,1)}), bf16[4096,512]{1,0:T(8,128)(2,1)}) %all-gather.4.cloned.1.call-update) | async-done | bytes 4194320 | tf_op jit(solution)/shard_map/all_gather | solution.py:35
  113.7 16.5 %fusion.4 = (bf16[1024,3584]{1,0:T(8,128)(2,1)}, f32[1024,3584]{1,0:T(8,128)}) fusion(bf16[1,4096,3584]{2,1,0:T(8,128)(2,1)} %param.6, bf16[1,512,3584]{2,1,0:T(8,128)(2,1)} %param.5, bf16[4096,512]{1,0:T(8,128)(2,1)} %all-gather.4.cloned.1.call-done), kind=kOutput, calls=%fused_computation.9 | convolution fusion | flops 3772776448 | bytes 34078720 | tf_op jit(solution)/shard_map/dot_general | solution.py:44
  130.2 0.0 all-reduce.2.cloned.1.call-update
  130.2 23.6 %fusion.10 = bf16[1,512,3584]{2,1,0:T(8,128)(2,1)} fusion(bf16[4096,512]{1,0:T(8,128)(2,1)} %all-gather.4.cloned.1.call-done, bf16[1,4096,3584]{2,1,0:T(8,128)(2,1)} %param.6), kind=kOutput, calls=%fused_computation.13 | convolution fusion | flops 15036055552 | bytes 37224448 | tf_op jit(solution)/shard_map/dot_general | solution.py:37
  153.9 74.3 %all-gather.6.cloned.1.call-done = bf16[1024,3584]{1,0:T(8,128)(2,1)} async-done(((bf16[128,3584]{1,0:T(8,128)(2,1)}), bf16[1024,3584]{1,0:T(8,128)(2,1)}) %all-gather.6.cloned.1.call-update) | async-done | bytes 7340048 | tf_op jit(solution)/shard_map/all_gather | solution.py:50
  228.2 113.1 %all-gather.8.cloned.1.call-done = bf16[1024,3584]{1,0:T(8,128)(2,1)} async-done(((bf16[128,3584]{1,0:T(8,128)(2,1)}), bf16[1024,3584]{1,0:T(8,128)(2,1)}) %all-gather.8.cloned.1.call-update) | async-done | bytes 7340048 | tf_op jit(solution)/shard_map/all_gather | solution.py:53
  341.3 244.6 %all-reduce.2.cloned.1.call-done = bf16[1024,3584]{1,0:T(8,128)(2,1)} async-done(((bf16[1024,3584]{1,0:T(8,128)(2,1)}), bf16[1024,3584]{1,0:T(8,128)(2,1)}) %all-reduce.2.cloned.1.call-update) | async-done | bytes 7340048 | tf_op jit(solution)/shard_map/psum | solution.py:48
  585.9 22.1 %fusion.5 = (bf16[1,1024,3584]{2,1,0:T(8,128)(2,1)}, f32[1024,3584]{1,0:T(8,128)S(1)}, f32[1024,3584]{1,0:T(8,128)}) fusion(f32[1024,3584]{1,0:T(8,128)} %get-tuple-element.8, bf16[1,4096,3584]{2,1,0:T(8,128)(2,1)} %param.6, bf16[1024,3584]{1,0:T(8,128)(2,1)} %all-gather.8.cloned.1.call-done, bf16[1024,3584]{1,0:T(8,128)(2,1)} %all-reduce.2.cloned.1.call-done, ...), kind=kLoop, calls=%fused_computation.11 | loop fusion | flops 62390272 | bytes 80740352 | tf_op jit(solution)/shard_map/broadcast_in_dim | solution.py:65
  608.0 3.7 constant_dynamic-slice_fusion
Async XLA Ops:
  7.2 69.5 %copy-start.1 = (bf16[1,1024,512]{2,1,0:T(8,128)(2,1)S(1)}, bf16[1,1024,512]{2,1,0:T(8,128)(2,1)}, u32[]{:S(2)}) copy-start(bf16[1,1024,512]{2,1,0:T(8,128)(2,1)} %param.7) | copy-start | bytes 3145732
  7.2 69.4 %reduce-scatter.2.cloned.1.call-start = ((), (), s32[]{:S(2)}) async-start(), calls=%async_computation.1 | async-start | bytes 5242880 | tf_op jit(solution)/shard_map/reduce_scatter | solution.py:23
  29.2 50.0 %copy-start = (f32[128,3584]{1,0:T(8,128)S(1)}, f32[128,3584]{1,0:T(8,128)}, u32[]{:S(2)}) copy-start(f32[128,3584]{1,0:T(8,128)} %param.8) | copy-start | bytes 5505028
  29.2 84.5 %all-gather.4.cloned.1.call-start = ((), (), s32[]{:S(2)}) async-start(), calls=%async_computation.2 | async-start | bytes 5242880 | tf_op jit(solution)/shard_map/all_gather | solution.py:35
  79.1 149.1 %all-gather.6.cloned.1.call-start = ((), (), s32[]{:S(2)}) async-start(), calls=%async_computation.3 | async-start | bytes 8257536 | tf_op jit(solution)/shard_map/all_gather | solution.py:50
  80.3 261.0 %all-gather.8.cloned.1.call-start = ((), (), s32[]{:S(2)}) async-start(), calls=%async_computation.5 | async-start | bytes 8257536 | tf_op jit(solution)/shard_map/all_gather | solution.py:53
  82.8 503.0 %all-reduce.2.cloned.1.call-start = ((), (), s32[]{:S(2)}) async-start(), calls=%async_computation.4 | async-start | bytes 14680064 | tf_op jit(solution)/shard_map/psum | solution.py:48
Sparse Core Ops, SparseCore 0:
  29.4 47.2 reduce-scatter.1
  79.2 34.4 all-gather.3
  116.2 111.9 all-gather.5
  231.1 110.1 all-gather.7
  346.1 239.7 all-reduce.1
where the time goes:
time: 618 us
  waiting for transfers between devices  510 us (83%)
  matrix products  62.1 us (10%)
  other arithmetic  28.1 us (5%)
  between operations  13.8 us (2%)
    psum x1, waiting for transfers between devices, shards(): total = lax.psum(stored.astype(jnp.bfloat16), 'island').astype(jnp.float32)  245 us
    all_gather x1, waiting for transfers between devices, shards(): lax.all_gather(momentum.astype(jnp.bfloat16), 'island', axis=0, tiled=True)  113 us
    all_gather x1, waiting for transfers between devices, shards(): lax.all_gather(global_weights.astype(jnp.bfloat16), 'island', axis=0, til...  74.3 us
    reduce_scatter x1, waiting for transfers between devices, shards(): lax.psum_scatter((lax.dot_general(weights, activations, (((1,), (1,)), ((...  47.3 us
    all_gather x1, waiting for transfers between devices, shards(): full_residue = lax.all_gather(residue, 'tensor', axis=0, tiled=True)  30.9 us
    dot_general x1, matrix products, shards(): lax.dot_general(full_residue, weights, (((0,), (0,)), ((), ())), preferre...  23.6 us
    broadcast_in_dim x1, other arithmetic, shards(): return (mixed[None], new_global, new_momentum, grad_hidden[None])  22.1 us
    dot_general x1, matrix products, shards(): lax.dot_general(weights, activations, (((1,), (1,)), ((), ())), preferred...  22 us
  transfers between devices with their start and end apart: 5, of which 5 were waited for; matrix products, arithmetic and copies ran while one was open for 7% of the time, Pallas kernels for 0%

commit v1 on v0

v1 whole, which is shorter than its diff:
```python
import math

import jax
import jax.numpy as jnp
from jax import lax
from jax.experimental import pallas as pl
from jax.experimental.pallas import tpu as pltpu
from jax.sharding import PartitionSpec as P

inner_rate = 0.3
outer_rate = 0.7
outer_beta = 0.9
mix_share = 0.5


VMEM_LIMIT = 54 * 2**20
ANY = pl.BlockSpec(memory_space=pl.ANY)
F32 = jnp.float32
BF16 = jnp.bfloat16


def matmul_nt(a, b):
    return lax.dot_general(a, b, (((1,), (1,)), ((), ())), preferred_element_type=F32)


def add(a, b):
    return (a.astype(F32) + b.astype(F32)).astype(BF16)


def like(x):
    return jax.ShapeDtypeStruct(x.shape, x.dtype)


def options():
    return dict(
        compiler_params=pltpu.CompilerParams(vmem_limit_bytes=VMEM_LIMIT),
        cost_estimate=pl.CostEstimate(flops=1, bytes_accessed=1, transcendentals=0),
    )


def grid_of(grid, ins, outs, scratch=()):
    return pltpu.PrefetchScalarGridSpec(
        num_scalar_prefetch=1, grid=grid, in_specs=ins, out_specs=outs, scratch_shapes=list(scratch)
    )


def swapped(count, bit):
    return [(i, i ^ bit) for i in range(count)]


def across(x, count, bit):
    return lax.ppermute(x, "tensor", swapped(count, bit))


def terms_of(x, count, when=None):
    bit = 4
    while bit < count:
        x = add(x, across(x, count, bit))
        bit *= 2
    terms = [x]
    if count > 2:
        terms.append(across(x, count, 2))
    if when is not None:
        terms = list(join(terms, *when))
    if count > 1:
        terms += [across(term, count, 1) for term in terms]
    return terms


def total_of(values):
    total = values[0].astype(F32)
    for value in values[1:]:
        total += value.astype(F32)
    return total.astype(BF16)


def join(values, *others):
    def kernel(*refs):
        pass

    return pl.pallas_call(
        kernel,
        in_specs=[ANY] * (len(values) + len(others)),
        out_specs=[ANY] * len(values),
        out_shape=[like(x) for x in values],
        input_output_aliases={n: n for n in range(len(values))},
        name="join",
        cost_estimate=pl.CostEstimate(flops=1, bytes_accessed=1, transcendentals=0),
    )(*values, *others)


class Table:
    def __init__(self, pairs, tensor, size, per):
        rows = [r for pair in pairs for r in pair]
        self.count = len(rows)
        self.size = size
        self.values = jnp.stack(
            [lax.div(r, size) for r in rows]
            + [lax.div(lax.rem(r, per), size) for r in rows]
            + [(lax.div(r, per) == tensor).astype(jnp.int32) for r in rows]
            + [tensor]
        )

    def block(self, t, s, n):
        return t[2 * s + n]

    def row(self, t, s, n):
        return pl.multiple_of(t[2 * s + n] * self.size, self.size)

    def goal_row(self, t, s, n):
        return pl.multiple_of(t[self.count + 2 * s + n] * self.size, self.size)

    def goal_here(self, t, s, n):
        return t[2 * self.count + 2 * s + n] == 1

    def tensor(self, t):
        return t[3 * self.count]


def partial_blocks(w, h, goals, first, count, table, scale, when=(), held=()):
    size = table.size
    tokens, width = h.shape
    chunks = next(n for n in (4, 2, 1) if width % (n * 128) == 0)
    span = width // chunks
    blocks = [(first + m, n) for m in range(count) for n in range(2)]
    extra = len(when) + len(held)
    total_rows = len(blocks) * size

    def kernel(t, w_ref, h_ref, *refs):
        g_ref, out = refs[0], refs[1 + extra]
        right, left, goal, w_sem, h_sem, g_sem, o_sem = refs[-7:]

        def goal_copy(at):
            rows = pl.ds(table.goal_row(t, *blocks[at]), size)
            return pltpu.make_async_copy(g_ref.at[rows, :], goal.at[pl.ds(at * size, size), :], g_sem.at[at])

        def copies(c):
            columns = pl.ds(c * span, span)
            yield pltpu.make_async_copy(h_ref.at[:, columns], right.at[:, columns], h_sem.at[c])
            for at, block in enumerate(blocks):
                to = left.at[pl.ds(at * size, size), columns]
                yield pltpu.make_async_copy(w_ref.at[pl.ds(table.row(t, *block), size), columns], to, w_sem.at[c, at])

        for c in range(chunks):
            for copy in copies(c):
                copy.start()
        for at in range(len(blocks)):
            goal_copy(at).start()
        total = None
        for c in range(chunks):
            for copy in copies(c):
                copy.wait()
            columns = pl.ds(c * span, span)
            prod = matmul_nt(left[:, columns], right[:, columns])
            total = prod if total is None else total + prod
        for at, block in enumerate(blocks):
            goal_copy(at).wait()
            rows = pl.ds(at * size, size)
            mine = jnp.where(table.goal_here(t, *block), goal[rows, :].astype(F32), 0.0)
            goal[rows, :] = (total[at * size : (at + 1) * size] * scale - mine).astype(BF16)
        result = pltpu.make_async_copy(goal, out, o_sem)
        result.start()
        result.wait()

    out = pl.pallas_call(
        kernel,
        grid_spec=grid_of(
            (1,),
            [ANY] * (3 + extra),
            [ANY] * (1 + len(held)),
            [
                pltpu.VMEM((tokens, width), BF16),
                pltpu.VMEM((len(blocks) * size, width), BF16),
                pltpu.VMEM((len(blocks) * size, tokens), BF16),
                pltpu.SemaphoreType.DMA((chunks, len(blocks))),
                pltpu.SemaphoreType.DMA((chunks,)),
                pltpu.SemaphoreType.DMA((len(blocks),)),
                pltpu.SemaphoreType.DMA,
            ],
        ),
        out_shape=[jax.ShapeDtypeStruct((total_rows, tokens), BF16)] + [like(x) for x in held],
        input_output_aliases={4 + len(when) + n: 1 + n for n in range(len(held))},
        name="partial_blocks",
        **options(),
    )(table.values, w, h, goals, *when, *held)
    return list(out[:1]), list(out[1:])


def stepped_blocks(w, h, terms, first, count, table, rate, when, split):
    size = table.size
    tokens, width = h.shape
    chunks = next(n for n in (4, 2, 1) if width % (n * 128) == 0)
    span = width // chunks
    blocks = [(first + m, n) for m in range(count) for n in range(2)]
    rows = len(blocks) * size
    parts = 3 if split else 1

    def kernel(t, w_ref, h_ref, *refs):
        t_refs, refs = refs[: len(terms)], refs[len(terms) + len(when) :]
        outs = refs[:parts]
        r_out, right, base, left, more, result, w_sem, h_sem, r_sem, o_sem = refs[parts:]

        def copies(c):
            columns = pl.ds(c * span, span)
            yield pltpu.make_async_copy(h_ref.at[:, columns], right.at[:, columns], h_sem.at[c])
            for at, block in enumerate(blocks):
                to = base.at[pl.ds(at * size, size), columns]
                yield pltpu.make_async_copy(w_ref.at[pl.ds(table.row(t, *block), size), columns], to, w_sem.at[c, at])

        def results(c):
            columns = pl.ds(c * span, span)
            yield pltpu.make_async_copy(result.at[:, columns], outs[0].at[:, columns], o_sem.at[c, 0])
            for n, out in enumerate(outs[1:]):
                part = result.at[pl.ds(n * size, size), columns]
                yield pltpu.make_async_copy(part, out.at[:, columns], o_sem.at[c, 1 + n])

        reads = [pltpu.make_async_copy(ref, more.at[n], r_sem.at[n]) for n, ref in enumerate(t_refs)]
        for copy in reads:
            copy.start()
        for c in range(chunks):
            for copy in copies(c):
                copy.start()
        for copy in reads:
            copy.wait()
        left[...] = total_of([more[n] for n in range(len(terms))])
        keep = pltpu.make_async_copy(left, r_out, r_sem.at[len(terms)])
        keep.start()
        for c in range(chunks):
            for copy in copies(c):
                copy.wait()
            columns = pl.ds(c * span, span)
            step = rate * jnp.dot(left[...], right[:, columns], preferred_element_type=F32)
            result[:, columns] = (base[:, columns].astype(F32) - step).astype(BF16)
            for copy in results(c):
                copy.start()
        for c in range(chunks):
            for copy in results(c):
                copy.wait()
        keep.wait()

    out = pl.pallas_call(
        kernel,
        grid_spec=grid_of(
            (1,),
            [ANY] * (2 + len(terms) + len(when)),
            [ANY] * (parts + 1),
            [
                pltpu.VMEM((tokens, width), BF16),
                pltpu.VMEM((rows, width), BF16),
                pltpu.VMEM((rows, tokens), BF16),
                pltpu.VMEM((len(terms), rows, tokens), BF16),
                pltpu.VMEM((rows, width), BF16),
                pltpu.SemaphoreType.DMA((chunks, len(blocks))),
                pltpu.SemaphoreType.DMA((chunks,)),
                pltpu.SemaphoreType.DMA((len(terms) + 1,)),
                pltpu.SemaphoreType.DMA((chunks, parts)),
            ],
        ),
        out_shape=[jax.ShapeDtypeStruct((rows, width), BF16)]
        + [jax.ShapeDtypeStruct((size, width), BF16)] * (parts - 1)
        + [jax.ShapeDtypeStruct((rows, tokens), BF16)],
        name="stepped_blocks",
        **options(),
    )(table.values, w, h, *terms, *when)
    return list(out[:parts]), out[parts]


def tail_rows(w, h, goals, first, count, tile, table, scale, when, held, blank):
    tokens, width = h.shape
    per = goals.shape[0]
    base = first // tile

    def kernel(t, w_ref, g_ref, h_ref, *refs):
        out, goal = refs[len(when) + len(held)], refs[-1]
        here = lax.div((base + pl.program_id(0)) * tile, per) == table.tensor(t)

        @pl.when(here)
        def _():
            goal[...] = g_ref[...].T

        @pl.when(jnp.logical_not(here))
        def _():
            goal[...] = jnp.zeros_like(goal)

        value = matmul_nt(h_ref[...], w_ref[...]) * scale
        out[...] = (value - goal[...].astype(F32)).astype(BF16)

    out = pl.pallas_call(
        kernel,
        grid_spec=grid_of(
            (count // tile,),
            [
                pl.BlockSpec((tile, width), lambda i, t: (base + i, 0)),
                pl.BlockSpec((tile, tokens), lambda i, t: (lax.rem(base + i, per // tile), 0)),
                pl.BlockSpec((tokens, width), lambda i, t: (0, 0)),
            ]
            + [ANY] * (len(when) + len(held)),
            [pl.BlockSpec((tokens, tile), lambda i, t: (0, i))] + [ANY] * (len(held) + len(blank)),
            [pltpu.VMEM((tokens, tile), BF16)],
        ),
        out_shape=[jax.ShapeDtypeStruct((tokens, count), BF16)]
        + [like(x) for x in held]
        + list(blank),
        input_output_aliases={4 + len(when) + n: 1 + n for n in range(len(held))},
        name="tail_rows",
        **options(),
    )(table.values, w, goals, h, *when, *held)
    return out[0], list(out[1 : 1 + len(held)]), list(out[1 + len(held) :])


def first_features(heads, features, when):
    tokens = heads[0].shape[1]
    frag = sum(x.shape[0] for x in heads)

    def kernel(*refs):
        out, flipped, sem = refs[-3:]
        column = 0
        for ref in refs[: len(heads)]:
            flipped[:, pl.ds(column, ref.shape[0])] = ref[...].T
            column += ref.shape[0]
        copy = pltpu.make_async_copy(flipped, out.at[:, pl.ds(0, frag)], sem)
        copy.start()
        copy.wait()

    return pl.pallas_call(
        kernel,
        grid=(1,),
        in_specs=[pl.BlockSpec(x.shape, lambda i: (0, 0)) for x in heads] + [ANY] * len(when),
        out_specs=ANY,
        out_shape=jax.ShapeDtypeStruct((tokens, features), BF16),
        scratch_shapes=[pltpu.VMEM((tokens, frag), BF16), pltpu.SemaphoreType.DMA],
        name="first_features",
        **options(),
    )(*heads, *when)


def more_features(left, column, terms, when):
    tokens, count = terms[0].shape
    step = count // 2

    def kernel(*refs):
        refs[-1][...] = total_of([ref[...] for ref in refs[: len(terms)]])

    return pl.pallas_call(
        kernel,
        grid=(2,),
        in_specs=[pl.BlockSpec((tokens, step), lambda i: (0, i))] * len(terms) + [ANY] * (1 + len(when)),
        out_specs=pl.BlockSpec((tokens, step), lambda i: (0, column // step + i)),
        out_shape=like(left),
        input_output_aliases={len(terms): 0},
        name="more_features",
        **options(),
    )(*terms, left, *when)


def outer_update(base, moment, total, islands):
    pseudo = base - total / islands
    new_momentum = outer_beta * moment + pseudo
    return base - outer_rate * (pseudo + outer_beta * new_momentum), new_momentum


def outer_step(table, s, got, stored, at, global_weights, momentum, mixed, islands, when):
    size = table.size
    rows, width = global_weights.shape

    steps = next(n for n in (4, 2, 1) if width % (n * 128) == 0)
    span = width // steps

    def kernel(t, a_ref, b_ref, s_ref, g_ref, m_ref, held, *refs):
        g_out, m_out, target, buffer, sems = refs[len(when) :]
        i = pl.program_id(0)

        def copy(i, n):
            part = pl.ds(pl.multiple_of(i * span, span), span)
            to = target.at[pl.ds(table.row(t, s, n), size), part]
            return pltpu.make_async_copy(buffer.at[pl.ds(n * size, size), part], to, sems.at[i, n])

        for n, ref in enumerate((a_ref, b_ref)):
            rows = pl.ds(n * size, size)
            own = s_ref[rows, :].astype(F32)
            new_global, new_momentum = outer_update(g_ref[rows, :], m_ref[rows, :], ref[...].astype(F32) + own, islands)
            g_out[rows, :] = new_global
            m_out[rows, :] = new_momentum
            value = mix_share * own + (1.0 - mix_share) * new_global.astype(BF16).astype(F32)
            buffer[rows, pl.ds(pl.multiple_of(i * span, span), span)] = value.astype(BF16)
            copy(i, n).start()

        @pl.when(i == steps - 1)
        def _():
            for j in range(steps):
                for n in range(2):
                    copy(j, n).wait()

    half = pl.BlockSpec((size, span), lambda i, t: (0, i))
    full = pl.BlockSpec((rows, span), lambda i, t: (0, i))
    return pl.pallas_call(
        kernel,
        grid_spec=grid_of(
            (steps,),
            [half, half, pl.BlockSpec((rows, span), lambda i, t: (at, i)), full, full, ANY] + [ANY] * len(when),
            [full, full, ANY],
            [pltpu.VMEM((rows, width), BF16), pltpu.SemaphoreType.DMA((steps, 2))],
        ),
        out_shape=[like(global_weights), like(momentum), like(mixed)],
        input_output_aliases={6: 2},
        name="outer_step",
        **options(),
    )(table.values, *got, stored, global_weights, momentum, mixed, *when)


def mix_pair(table, s, got, stored, at, mixed):
    size = table.size
    width = mixed.shape[1]

    def kernel(t, a_ref, b_ref, s_ref, held, target, buffer, sems):
        for n, ref in enumerate((a_ref, b_ref)):
            rows = pl.ds(n * size, size)
            value = mix_share * s_ref[rows, :].astype(F32) + (1.0 - mix_share) * ref[...].astype(F32)
            buffer[rows, :] = value.astype(BF16)
        copies = [
            pltpu.make_async_copy(
                buffer.at[pl.ds(n * size, size), :], target.at[pl.ds(table.row(t, s, n), size), :], sems.at[n]
            )
            for n in range(2)
        ]
        for copy in copies:
            copy.start()
        for copy in copies:
            copy.wait()

    return pl.pallas_call(
        kernel,
        grid_spec=grid_of(
            (1,),
            [pl.BlockSpec((size, width), lambda i, t: (0, 0))] * 2
            + [pl.BlockSpec((2 * size, width), lambda i, t: (at, 0)), ANY],
            ANY,
            [pltpu.VMEM((2 * size, width), BF16), pltpu.SemaphoreType.DMA((2,))],
        ),
        out_shape=like(mixed),
        input_output_aliases={4: 0},
        name="mix_pair",
        **options(),
    )(table.values, *got, stored, mixed)


def mix_and_back(w, left, pairs, table, first, count, tile, scale, s, got, stored, at, grad_hidden, mixed):
    size = table.size
    tokens, features = left.shape
    width = w.shape[1]
    blocks = [(m, n) for m in range(pairs) for n in range(2)]
    frag = len(blocks) * size
    more = [mixed] + ([] if grad_hidden is None else [grad_hidden])

    def kernel(t, l_ref, a_ref, b_ref, s_ref, *refs):
        i = pl.program_id(0)
        out, target = refs[len(blocks) + 1 + len(more) : len(blocks) + 3 + len(more)]
        buffer, sems = refs[-2:]

        def copy(n):
            to = target.at[pl.ds(table.row(t, s, n), size), :]
            return pltpu.make_async_copy(buffer.at[pl.ds(n * size, size), :], to, sems.at[n])

        @pl.when(i == 0)
        def _():
            for n, ref in enumerate((a_ref, b_ref)):
                rows = pl.ds(n * size, size)
                value = mix_share * s_ref[rows, :].astype(F32) + (1.0 - mix_share) * ref[...].astype(F32)
                buffer[rows, :] = value.astype(BF16)
                copy(n).start()

        parts = jnp.concatenate([p[...] for p in refs[: len(blocks)]], axis=0)
        total = jnp.dot(l_ref[:, :frag], parts, preferred_element_type=F32)
        total += jnp.dot(l_ref[:, frag:], refs[len(blocks)][...], preferred_element_type=F32)
        out[...] = (total * scale).astype(BF16)

        @pl.when(i == count - 1)
        def _():
            copy(0).wait()
            copy(1).wait()

    operands = 5 + len(blocks) + 1
    aliases = {operands: 1}
    if grad_hidden is not None:
        aliases[operands + 1] = 0

    def block_spec(m, n):
        return pl.BlockSpec((size, tile), lambda i, t: (table.block(t, m, n), first + i))

    rest = pl.BlockSpec((pl.Element(features - frag), pl.Element(tile)), lambda i, t: (frag, (first + i) * tile))
    return pl.pallas_call(
        kernel,
        grid_spec=grid_of(
            (count,),
            [pl.BlockSpec((tokens, features), lambda i, t: (0, 0))]
            + [pl.BlockSpec((size, width), lambda i, t: (0, 0))] * 2
            + [pl.BlockSpec((2 * size, width), lambda i, t: (at, 0))]
            + [block_spec(*x) for x in blocks]
            + [rest]
            + [ANY] * len(more),
            [pl.BlockSpec((tokens, tile), lambda i, t: (0, first + i)), ANY],
            [pltpu.VMEM((2 * size, width), BF16), pltpu.SemaphoreType.DMA((2,))],
        ),
        out_shape=[jax.ShapeDtypeStruct((tokens, width), BF16), like(mixed)],
        input_output_aliases=aliases,
        name="mix_and_back",
        **options(),
    )(table.values, left, *got, stored, *([w] * (len(blocks) + 1)), *more)


def shards(hidden, island_weights, targets, global_weights, momentum):
    h = hidden[0]
    w = island_weights[0]
    goals = targets[0]
    islands = lax.axis_size("island")
    tensors = lax.axis_size("tensor")
    island = lax.axis_index("island")
    tensor = lax.axis_index("tensor")
    rows = global_weights.shape[0]
    size = rows // 2
    frag = rows * islands
    width = w.shape[1]
    scale = 1.0 / math.sqrt(width * tensors)
    rate = inner_rate * scale
    per = goals.shape[0]

    def island_at(k):
        return jnp.where(k < islands // 2, 2 * k, 2 * (islands - 1 - k) + 1)

    def number_at(k):
        return 2 * k if k < islands // 2 else 2 * (islands - 1 - k) + 1

    place = jnp.where(island % 2 == 0, island // 2, islands - 1 - island // 2)
    ahead = [(number_at(k), number_at((k + 1) % islands)) for k in range(islands)]
    back = [(b, a) for a, b in ahead]
    starts = [island_at(lax.rem(place + k, islands)) * rows for k in range(islands)]

    pairs = [(starts[(-s - 1) % islands], starts[(s + 1) % islands] + size) for s in range(islands)]
    table = Table(pairs, tensor, size, per)

    early = 3
    (x,), _ = partial_blocks(w, h, goals, 0, 1, table, scale)
    bit = tensors // 2
    while bit > 1:
        x = add(x, across(x, tensors, bit))
        bit //= 2
    first_terms = [x, across(x, tensors, 1)]
    (x,), _ = partial_blocks(w, h, goals, 1, early, table, scale)
    next_terms = terms_of(x, tensors)
    (first_store, *acc), first_residue = stepped_blocks(w, h, first_terms, 0, 1, table, rate, [], True)

    tile = min(512, per)
    tail_rest = w.shape[0] - frag
    calls = next(n for n in (3, 1) if tail_rest % (n * tile) == 0)
    tail_at = {1: 0, 3: 1, 4: 2}
    tail_due = {5: [0], 6: [1]}
    chips_due = {3: 0, 5: 1}
    tails = []
    mixed = None
    store = {}

    for s in range(islands - 1):
        got = [lax.ppermute(acc[0], "island", ahead), lax.ppermute(acc[1], "island", back)]
        name, at = ("next", s) if s < early else ("last", s - early)
        order = acc
        if s == 0:
            (x,), _ = partial_blocks(w, h, goals, 1 + early, islands - 1 - early, table, scale, order)
            last_terms = terms_of(x, tensors)
            order = [x]
            (store["next"],), next_residue = stepped_blocks(
                w, h, next_terms, 1, early, table, rate, order, False
            )
        if s == early - 1:
            (store["last"],), last_residue = stepped_blocks(
                w, h, last_terms, 1 + early, islands - 1 - early, table, rate, order, False
            )
            order = [last_residue]
        if tail_at.get(s, calls) < calls:
            count = tail_rest // calls
            blank = [jax.ShapeDtypeStruct((frag, width), BF16)] if mixed is None else []
            x, _, fresh = tail_rows(
                w, h, goals, frag + tail_at[s] * count, count, tile, table, scale, order, [], blank
            )
            mixed = fresh[0] if fresh else mixed
            tails.append(terms_of(x, tensors))
            order = [x]
            last_tail = x
        if s == 5:
            left = first_features([first_residue, next_residue, last_residue], w.shape[0], order)
            order = [left]
        for n in tail_due.get(s, []):
            left = more_features(left, frag + n * tails[n][0].shape[1], tails[n], [] if s == 5 else order)
            order = [left]
        if order is not acc and s > 0:
            due = [tails[chips_due[s]][1]] if chips_due.get(s, len(tails)) < len(tails) else []
            (store[name],) = join([store[name]], *order, *due)
        own = [lax.slice_in_dim(store[name], (2 * at + n) * size, (2 * at + n + 1) * size, axis=0) for n in range(2)]
        if s < islands - 2:
            acc = [add(got[i], own[i]) for i in range(2)]
    send = []
    for n in range(2):
        base, moment = (lax.slice_in_dim(x, n * size, (n + 1) * size, axis=0) for x in (global_weights, momentum))
        send.append(outer_update(base, moment, got[n].astype(F32) + own[n].astype(F32), islands)[0].astype(BF16))

    def stored(s):
        if s == 0:
            return first_store, 0
        return (store["next"], s - 1) if s <= early else (store["last"], s - 1 - early)

    wide = 256 if width % 256 == 0 else 128
    tiles = width // wide
    pieces = min(5, tiles, islands - 3)
    cuts = [-(-tiles * n // pieces) for n in range(pieces + 1)]
    grad_hidden = None

    new_global, new_momentum, mixed = outer_step(
        table, islands - 1, got, *stored(islands - 1), global_weights, momentum, mixed, islands, send
    )
    later = range(sum(len(x) for x in tail_due.values()), len(tails))
    waiting = []
    for s in range(islands - 1):
        send = [lax.ppermute(send[0], "island", ahead), lax.ppermute(send[1], "island", back)]
        if s == 0:
            send = join(send, mixed)
        if waiting:
            send = join(send, *waiting)
        piece = s - (islands - 2 - pieces)
        if 0 <= piece < pieces:
            grad_hidden, mixed = mix_and_back(
                w, left, islands, table, cuts[piece], cuts[piece + 1] - cuts[piece], wide, scale, s, send, *stored(s),
                grad_hidden, mixed,
            )
            waiting = [mixed]
        else:
            mixed = mix_pair(table, s, send, *stored(s), mixed)
        if s == 0 and later:
            terms = terms_of(last_tail, tensors, send)
            for n in later:
                left = more_features(left, frag + n * terms[0].shape[1], terms, [mixed])
            waiting = [mixed, left]
    return (mixed[None], new_global, new_momentum, grad_hidden[None])


def solution(mesh):
    return jax.shard_map(
        shards,
        mesh=mesh,
        in_specs=(
            P("island", None, "tensor"),
            P("island", None, "tensor"),
            P("island", "tensor", None),
            P("island", "tensor"),
            P("island", "tensor"),
        ),
        out_specs=(
            P("island", None, "tensor"),
            P("island", "tensor"),
            P("island", "tensor"),
            P("island", None, "tensor"),
        ),
        check_vma=False,
    )
```

time: 618 us -> 237 us (0.38)
  waiting for transfers between devices: 510 us -> 26.6 us
  Pallas kernels: 0 us -> 140 us
  matrix products: 62.1 us -> 0 us
  starting transfers between devices: 0.21 us -> 37.3 us
  between operations: 13.8 us -> 1.97 us
  other arithmetic: 28.1 us -> 16.4 us
  local copies, waits for them, and re-layouts: 3.69 us -> 13.5 us
    psum x1 -> x0, waiting for transfers between devices: 245 us -> none  [shards(): total = lax.psum(stored.astype(jnp.bfloat16), 'island').astype(jnp.float32)]
    all_gather x3 -> x0, waiting for transfers between devices: 218 us -> none  [the longest x1 113 us: shards(): lax.all_gather(momentum.astype(jnp.bfloat16), 'island', axis=0, tiled=True)]
    pallas_call x0 -> x35, Pallas kernels: none -> 140 us  [the longest x5 47.2 us: mix_and_back(): pl.pallas_call(kernel, grid_spec=grid_of((count,), [pl.BlockSpec((tokens,...]
    dot_general x3 -> x0, matrix products: 62.1 us -> none  [the longest x1 23.6 us: shards(): lax.dot_general(full_residue, weights, (((0,), (0,)), ((), ())), preferre...]
    reduce_scatter x1 -> x0, waiting for transfers between devices: 47.3 us -> none  [shards(): lax.psum_scatter((lax.dot_general(weights, activations, (((1,), (1,)), ((...]
    ppermute x0 -> x45, starting transfers between devices: none -> 37.3 us  [the longest x7 12.1 us: shards(): lax.ppermute(send[1], 'island', back)]
    ppermute x0 -> x45, waiting for transfers between devices: none -> 26.6 us  [the longest x17 7.91 us: across(): return lax.ppermute(x, 'tensor', swapped(count, bit))]
    broadcast_in_dim x1 -> x0, other arithmetic: 22.1 us -> none  [shards(): return (mixed[None], new_global, new_momentum, grad_hidden[None])]
  transfers between devices with their start and end apart: 5 -> 45, of which waited for: 5 -> 16; matrix products, arithmetic and copies ran while one was open for 7% -> 6% of each run, Pallas kernels for 0% -> 56%
where the time goes in v1:
time: 237 us; the launch traced here: 236 us
  Pallas kernels  140 us (59%)
  starting transfers between devices  37.3 us (16%)
  waiting for transfers between devices  26.6 us (11%)
  other arithmetic  16.4 us (7%)
  local copies, waits for them, and re-layouts  13.5 us (6%)
    pallas_call x5, Pallas kernels, mix_and_back(): pl.pallas_call(kernel, grid_spec=grid_of((count,), [pl.BlockSpec((tokens,...  47.2 us
    pallas_call x3, Pallas kernels, tail_rows(): pl.pallas_call(kernel, grid_spec=grid_of((count // tile,), [pl.BlockSpec(...  27.4 us
    pallas_call x3, Pallas kernels, stepped_blocks(): pl.pallas_call(kernel, grid_spec=grid_of((1,), [ANY] * (2 + len(terms) +...  21.4 us
    pallas_call x3, Pallas kernels, partial_blocks(): pl.pallas_call(kernel, grid_spec=grid_of((1,), [ANY] * (3 + extra), [ANY]...  18.2 us
    convert_element_type x7, other arithmetic, add(): return (a.astype(F32) + b.astype(F32)).astype(BF16)  13.9 us
    unnamed x76, local copies, waits for them, and re-layouts  12.8 us
    ppermute x7, starting transfers between devices, shards(): lax.ppermute(send[1], 'island', back)  12.1 us
    ppermute x7, starting transfers between devices, shards(): lax.ppermute(acc[1], 'island', back)  10.2 us
  transfers between devices with their start and end apart: 45, of which 16 were waited for; matrix products, arithmetic and copies ran while one was open for 6% of the time, Pallas kernels for 56%

profile of v1, /device:TPU:0, one launch (start us, length us, event | category | flops | bytes accessed | tf_op | source)
XLA Modules:
  0.0 236.0 jit_solution(3208685518540661780)
XLA Ops:
  2.0 4.6 %partial_blocks.3 = bf16[128,512]{1,0:T(8,128)(2,1)} custom-call(s32[49]{0:T(128)} %stack.263.t, bf16[4096,3584]{1,0:T(8,128)(2,1)} %bitcast.54, bf16[512,3584]{1,0:T(8,128)(2,1)} %bitcast.149, bf16[1024,512]{1,0:T(8,128)(2,1)} %bitcast.159), custom_call_target="tpu_custom_call" | custom-call | flops 1 | bytes 1 | tf_op jit(solution)/shard_map/partial_blocks/pallas_call | solution.py:165
  6.6 3.0 %collective-permute-start = (bf16[128,512]{1,0:T(8,128)(2,1)}, bf16[128,512]{1,0:T(8,128)(2,1)S(1)}, u32[]{:S(2)}, u32[]{:S(2)}) collective-permute-start(bf16[128,512]{1,0:T(8,128)(2,1)} %partial_blocks.3), channel_id=1, source_target_pairs={{0,2},{1,3},{2,0},{3,1},{4,6},{5,7},{6,4},{7,5},{8,10},{9,11},{10,... | collective-permute-start | bytes 393224 | tf_op jit(solution)/shard_map/ppermute | solution.py:52
  9.6 6.3 %partial_blocks.4.refs_0_ = bf16[384,512]{1,0:T(8,128)(2,1)} custom-call(s32[49]{0:T(128)} %stack.263.t, bf16[4096,3584]{1,0:T(8,128)(2,1)} %bitcast.55, bf16[512,3584]{1,0:T(8,128)(2,1)} %bitcast.150, bf16[1024,512]{1,0:T(8,128)(2,1)} %bitcast.160), custom_call_target="tpu_custom_call" | custom-call | flops 1 | bytes 1 | tf_op jit(solution)/shard_map/partial_blocks/pallas_call | solution.py:165
  18.1 5.1 %stepped_blocks.3 = (bf16[128,3584]{1,0:T(8,128)(2,1)}, bf16[64,3584]{1,0:T(8,128)(2,1)}, bf16[64,3584]{1,0:T(8,128)(2,1)}, bf16[128,512]{1,0:T(8,128)(2,1)}) custom-call(s32[49]{0:T(128)} %stack.263.t, bf16[4096,3584]{1,0:T(8,128)(2,1)} %bitcast.56, bf16[512,3584]{1,0:T(8,128)(2,1)} %bitcast.151, bf16[128,512]{1,0:T(8,128)(2,1)} %copy-done.31, ...), custom_call_target="tpu_custom_call" | custom-call | flops 1 | bytes 1 | tf_op jit(solution)/shard_map/stepped_blocks/pallas_call | solution.py:241
  23.2 2.1 collective-permute-start.2
  26.7 7.3 %partial_blocks.5.refs_4_.refs_0_ = bf16[512,512]{1,0:T(8,128)(2,1)} custom-call(s32[49]{0:T(128)} %stack.263.t, bf16[4096,3584]{1,0:T(8,128)(2,1)} %bitcast.57, bf16[512,3584]{1,0:T(8,128)(2,1)} %bitcast.152, bf16[1024,512]{1,0:T(8,128)(2,1)} %bitcast.161, bf16[64,3584]{1,0:T(8,128)(2,1)} %get-tuple-element.43.refs_1_, ...), custom_call_target="tpu_custom_call" | custom-call | flops 1 | bytes 1 | tf_op jit(solution)/shard_map/partial_blocks/pallas_call | solution.py:165
  36.7 7.5 %stepped_blocks.4 = (bf16[384,3584]{1,0:T(8,128)(2,1)}, bf16[384,512]{1,0:T(8,128)(2,1)}) custom-call(s32[49]{0:T(128)} %stack.263.t, bf16[4096,3584]{1,0:T(8,128)(2,1)} %bitcast.58, bf16[512,3584]{1,0:T(8,128)(2,1)} %bitcast.153, bf16[384,512]{1,0:T(8,128)(2,1)} %partial_blocks.4.refs_0_, bf16[384,512]{1,0:T(8,128)(2,1)} %copy-done.34, ...), custom_call_target="tpu_custom_call" | custom-call | flops 1 | bytes 1 | tf_op jit(solution)/shard_map/stepped_blocks/pallas_call | solution.py:241
  48.8 9.1 %tail_rows.3 = (bf16[512,1024]{1,0:T(8,128)(2,1)}, bf16[1024,3584]{1,0:T(8,128)(2,1)}) custom-call(s32[49]{0:T(128)} %stack.263.t, bf16[4096,3584]{1,0:T(8,128)(2,1)} %bitcast.59, bf16[1024,512]{1,0:T(8,128)(2,1)} %bitcast.162, bf16[512,3584]{1,0:T(8,128)(2,1)} %bitcast.154, bf16[64,3584]{1,0:T(8,128)(2,1)} %copy-done.10, bf16[64,3584]{1,0:T(8,128)(2,1)} %copy-done.11), custom_call_target="tpu_custom_call" | custom-call | flops 1 | bytes 1 | tf_op jit(solution)/shard_map/tail_rows/pallas_call | solution.py:288
  59.2 2.4 %add_convert_fusion.8 = (bf16[64,3584]{1,0:T(8,128)(2,1)}, bf16[64,3584]{1,0:T(8,128)(2,1)S(1)}) fusion(bf16[64,3584]{1,0:T(8,128)(2,1)} %copy-done.33, bf16[384,3584]{1,0:T(8,128)(2,1)} %join.14.refs_0_, bf16[64,3584]{1,0:T(8,128)(2,1)} %collective-permute-done.6), kind=kLoop, calls=%fused_computation.10 | loop fusion | flops 1835008 | bytes 2752512 | tf_op jit(solution)/shard_map/convert_element_type | solution.py:27
  61.6 1.6 collective-permute-start.14
  65.1 8.8 %stepped_blocks.5 = (bf16[512,3584]{1,0:T(8,128)(2,1)}, bf16[512,512]{1,0:T(8,128)(2,1)}) custom-call(s32[49]{0:T(128)} %stack.263.t, bf16[4096,3584]{1,0:T(8,128)(2,1)} %bitcast.60, bf16[512,3584]{1,0:T(8,128)(2,1)} %bitcast.155, bf16[512,512]{1,0:T(8,128)(2,1)} %partial_blocks.5.refs_4_.refs_0_, bf16[512,512]{1,0:T(8,128)(2,1)} %collective-permute-done.9.refs_1_, ...), custom_call_target="tpu_custom_call" | custom-call | flops 1 | bytes 1 | tf_op jit(solution)/shard_map/stepped_blocks/pallas_call | solution.py:241
  75.6 2.4 %add_convert_fusion.6 = (bf16[64,3584]{1,0:T(8,128)(2,1)}, bf16[64,3584]{1,0:T(8,128)(2,1)S(1)}) fusion(bf16[64,3584]{1,0:T(8,128)(2,1)} %collective-permute-done.14, bf16[384,3584]{1,0:T(8,128)(2,1)} %join.15.s_ref, bf16[64,3584]{1,0:T(8,128)(2,1)} %collective-permute-done.8), kind=kLoop, calls=%fused_computation.8 | loop fusion | flops 1835008 | bytes 2752512 | tf_op jit(solution)/shard_map/convert_element_type | solution.py:27
  78.0 1.6 collective-permute-start.17
  80.1 9.1 %tail_rows.4.refs_1_.refs_0_ = bf16[512,1024]{1,0:T(8,128)(2,1)} custom-call(s32[49]{0:T(128)} %stack.263.t, bf16[4096,3584]{1,0:T(8,128)(2,1)} %bitcast.61, bf16[1024,512]{1,0:T(8,128)(2,1)} %bitcast.163, bf16[512,3584]{1,0:T(8,128)(2,1)} %bitcast.156, bf16[64,3584]{1,0:T(8,128)(2,1)} %copy-done.12, bf16[64,3584]{1,0:T(8,128)(2,1)} %get-tuple-element.90.refs_1_), custom_call_target="tpu_custom_call" | custom-call | flops 1 | bytes 1 | tf_op jit(solution)/shard_map/tail_rows/pallas_call | solution.py:288
  90.9 2.6 %add_convert_fusion.4 = (bf16[64,3584]{1,0:T(8,128)(2,1)}, bf16[64,3584]{1,0:T(8,128)(2,1)}) fusion(bf16[64,3584]{1,0:T(8,128)(2,1)} %collective-permute-done.17, bf16[512,3584]{1,0:T(8,128)(2,1)} %join.16.refs_0_, bf16[64,3584]{1,0:T(8,128)(2,1)} %collective-permute-done.13), kind=kLoop, calls=%fused_computation.6 | loop fusion | flops 1835008 | bytes 2752512 | tf_op jit(solution)/shard_map/convert_element_type | solution.py:27
  93.5 2.1 collective-permute-start.21
  95.7 9.3 %tail_rows.5.refs_1_.refs_0_ = bf16[512,1024]{1,0:T(8,128)(2,1)} custom-call(s32[49]{0:T(128)} %stack.263.t, bf16[4096,3584]{1,0:T(8,128)(2,1)} %bitcast.62, bf16[1024,512]{1,0:T(8,128)(2,1)} %bitcast.164, bf16[512,3584]{1,0:T(8,128)(2,1)} %bitcast.157, bf16[64,3584]{1,0:T(8,128)(2,1)} %get-tuple-element.89.refs_0_, bf16[64,3584]{1,0:T(8,128)(2,1)} %get-tuple-element.88.refs_1_), custom_call_target="tpu_custom_call" | custom-call | flops 1 | bytes 1 | tf_op jit(solution)/shard_map/tail_rows/pallas_call | solution.py:288
  106.5 2.6 %add_convert_fusion.2 = (bf16[64,3584]{1,0:T(8,128)(2,1)}, bf16[64,3584]{1,0:T(8,128)(2,1)}) fusion(bf16[64,3584]{1,0:T(8,128)(2,1)} %collective-permute-done.21, bf16[512,3584]{1,0:T(8,128)(2,1)} %join.17.refs_0_, bf16[64,3584]{1,0:T(8,128)(2,1)} %collective-permute-done.16), kind=kLoop, calls=%fused_computation.4 | loop fusion | flops 1835008 | bytes 2752512 | tf_op jit(solution)/shard_map/convert_element_type | solution.py:27
  109.1 1.7 collective-permute-start.26
  111.1 2.6 %first_features.1.refs_4_ = bf16[512,4096]{1,0:T(8,128)(2,1)} custom-call(bf16[128,512]{1,0:T(8,128)(2,1)} %get-tuple-element.49.refs_0_, bf16[384,512]{1,0:T(8,128)(2,1)} %get-tuple-element.50.refs_1_, bf16[512,512]{1,0:T(8,128)(2,1)} %get-tuple-element.47.refs_1_.refs_2_, bf16[64,3584]{1,0:T(8,128)(2,1)} %get-tuple-element.87.refs_3_, ...), custom_call_target="tpu_custom_call" | custom-call | flops 1 | bytes 1 | tf_op jit(solution)/shard_map/first_features/pallas_call | solution.py:325
  113.8 3.3 %more_features.3.refs_1_.refs_4_ = bf16[512,4096]{1,0:T(8,128)(2,1)} custom-call(bf16[512,1024]{1,0:T(8,128)(2,1)} %get-tuple-element.46.refs_1_.refs_0_, bf16[512,1024]{1,0:T(8,128)(2,1)} %copy-done.5, bf16[512,1024]{1,0:T(8,128)(2,1)} %collective-permute-done.19.refs_2_, ...), custom_call_target="tpu_custom_call", output_to_operand_aliasing={{}: (4, {})} | custom-call | flops 1 | bytes 1 | tf_op jit(solution)/shard_map/more_features/pallas_call | solution.py:344
  117.2 4.1 %collective-permute-done.22.refs_2_.refs_1_ = bf16[512,1024]{1,0:T(8,128)(2,1)} collective-permute-done((bf16[512,1024]{1,0:T(8,128)(2,1)S(1)}, bf16[512,1024]{1,0:T(8,128)(2,1)}, u32[]{:S(2)}, u32[]{:S(2)}) %collective-permute-start.22) | collective-permute-done | bytes 1048608 | tf_op jit(solution)/shard_map/ppermute | solution.py:52
  122.4 2.6 %add_convert_fusion = (bf16[64,3584]{1,0:T(8,128)(2,1)}, bf16[64,3584]{1,0:T(8,128)(2,1)}) fusion(bf16[64,3584]{1,0:T(8,128)(2,1)} %collective-permute-done.26, bf16[512,3584]{1,0:T(8,128)(2,1)} %join.18.refs_0_, bf16[64,3584]{1,0:T(8,128)(2,1)} %collective-permute-done.18), kind=kLoop, calls=%fused_computation.2 | loop fusion | flops 1835008 | bytes 2752512 | tf_op jit(solution)/shard_map/convert_element_type | solution.py:27
  125.0 1.6 collective-permute-start.28
  127.0 3.3 %more_features.4.refs_1_.refs_4_ = bf16[512,4096]{1,0:T(8,128)(2,1)} custom-call(bf16[512,1024]{1,0:T(8,128)(2,1)} %tail_rows.4.refs_1_.refs_0_, bf16[512,1024]{1,0:T(8,128)(2,1)} %collective-permute-done.22.refs_2_.refs_1_, bf16[512,1024]{1,0:T(8,128)(2,1)} %collective-permute-done.24.refs_2_, ...), custom_call_target="tpu_custom_call", output_to_operand_aliasing={{}: (4, {})} | custom-call | flops 1 | bytes 1 | tf_op jit(solution)/shard_map/more_features/pallas_call | solution.py:344
  130.3 2.0 collective-permute-start.32
  132.3 4.7 %collective-permute-done.28.b_ref = bf16[64,3584]{1,0:T(8,128)(2,1)S(1)} collective-permute-done((bf16[64,3584]{1,0:T(8,128)(2,1)}, bf16[64,3584]{1,0:T(8,128)(2,1)S(1)}, u32[]{:S(2)}, u32[]{:S(2)}) %collective-permute-start.28) | collective-permute-done | bytes 458784 | tf_op jit(solution)/shard_map/ppermute | solution.py:563
  137.0 1.8 collective-permute-done.23.a_ref
  138.8 2.5 %subtract_convert_fusion = (bf16[64,3584]{1,0:T(8,128)(2,1)S(1)}, bf16[64,3584]{1,0:T(8,128)(2,1)S(1)}) fusion(f32[128,3584]{1,0:T(8,128)S(1)} %copy-done.2, bf16[64,3584]{1,0:T(8,128)(2,1)S(1)} %collective-permute-done.28.b_ref, f32[128,3584]{1,0:T(8,128)} %g_ref.1, bf16[512,3584]{1,0:T(8,128)(2,1)} %join.19.s_ref, ...), kind=kLoop, calls=%fused_computation | loop fusion | flops 5505024 | bytes 6422528 | tf_op jit(solution)/shard_map/convert_element_type | solution.py:603
  141.4 1.8 collective-permute-start.29
  143.5 6.8 %outer_step.1 = (f32[128,3584]{1,0:T(8,128)}, f32[128,3584]{1,0:T(8,128)}, bf16[1024,3584]{1,0:T(8,128)(2,1)}) custom-call(s32[49]{0:T(128)} %stack.263.t, bf16[64,3584]{1,0:T(8,128)(2,1)} %collective-permute-done.23.a_ref, bf16[64,3584]{1,0:T(8,128)(2,1)} %copy-done.17, bf16[512,3584]{1,0:T(8,128)(2,1)} %join.19.s_ref, ...), custom_call_target="tpu_custom_call", output_to_operand_aliasing={{2}: (6, {})} | custom-call | flops 1 | bytes 1 | tf_op jit(solution)/shard_map/outer_step/pallas_call | solution.py:396
  150.3 2.2 collective-permute-done.29.refs_1_
  152.5 2.2 collective-permute-done.27.refs_0_
  156.3 1.7 collective-permute-start.31
  158.1 3.4 %mix_pair.2.refs_5_.refs_2_.refs_17_ = bf16[1024,3584]{1,0:T(8,128)(2,1)} custom-call(s32[49]{0:T(128)} %stack.263.t, bf16[64,3584]{1,0:T(8,128)(2,1)} %get-tuple-element.53.a_ref.refs_2_, bf16[64,3584]{1,0:T(8,128)(2,1)} %get-tuple-element.54.b_ref.refs_3_, bf16[128,3584]{1,0:T(8,128)(2,1)} %get-tuple-element.55.s_ref, ...), custom_call_target="tpu_custom_call", output_to_operand_aliasing={{}: (4, {})} | custom-call | flops 1 | bytes 1 | tf_op jit(solution)/shard_map/mix_pair/pallas_call | solution.py:431
  163.4 3.2 %more_features.5.refs_3_.l_ref = bf16[512,4096]{1,0:T(8,128)(2,1)} custom-call(bf16[512,1024]{1,0:T(8,128)(2,1)} %get-tuple-element.56.refs_0_, bf16[512,1024]{1,0:T(8,128)(2,1)} %get-tuple-element.57.refs_1_, bf16[512,1024]{1,0:T(8,128)(2,1)} %copy-done.29, bf16[512,1024]{1,0:T(8,128)(2,1)} %copy-done.30, ...), custom_call_target="tpu_custom_call", output_to_operand_aliasing={{}: (4, {})} | custom-call | flops 1 | bytes 1 | tf_op jit(solution)/shard_map/more_features/pallas_call | solution.py:344
  166.6 2.1 collective-permute-done.30.refs_0_
  170.6 1.7 collective-permute-start.36
  172.3 9.7 %mix_and_back.5 = (bf16[512,3584]{1,0:T(8,128)(2,1)}, bf16[1024,3584]{1,0:T(8,128)(2,1)}) custom-call(s32[49]{0:T(128)} %stack.263.t, bf16[512,4096]{1,0:T(8,128)(2,1)} %more_features.5.refs_3_.l_ref, bf16[64,3584]{1,0:T(8,128)(2,1)} %get-tuple-element.58.a_ref, bf16[64,3584]{1,0:T(8,128)(2,1)} %get-tuple-element.59.b_ref, ...), custom_call_target="tpu_custom_call", output_to_operand_aliasing={{1}: (22, {})} | custom-call | flops 1 | bytes 1 | tf_op jit(solution)/shard_map/mix_and_back/pallas_call | solution.py:491
  183.5 1.7 collective-permute-start.38
  185.2 9.8 %mix_and_back.6 = (bf16[512,3584]{1,0:T(8,128)(2,1)}, bf16[1024,3584]{1,0:T(8,128)(2,1)}) custom-call(s32[49]{0:T(128)} %stack.263.t, bf16[512,4096]{1,0:T(8,128)(2,1)} %more_features.5.refs_3_.l_ref, bf16[64,3584]{1,0:T(8,128)(2,1)} %get-tuple-element.61.a_ref, ...), custom_call_target="tpu_custom_call", output_to_operand_aliasing={{1}: (22, {}), {0}: (23, {})} | custom-call | flops 1 | bytes 1 | tf_op jit(solution)/shard_map/mix_and_back/pallas_call | solution.py:491
  196.2 1.7 collective-permute-start.40
  197.9 9.8 %mix_and_back.7 = (bf16[512,3584]{1,0:T(8,128)(2,1)}, bf16[1024,3584]{1,0:T(8,128)(2,1)}) custom-call(s32[49]{0:T(128)} %stack.263.t, bf16[512,4096]{1,0:T(8,128)(2,1)} %more_features.5.refs_3_.l_ref, bf16[64,3584]{1,0:T(8,128)(2,1)} %get-tuple-element.65.a_ref, ...), custom_call_target="tpu_custom_call", output_to_operand_aliasing={{1}: (22, {}), {0}: (23, {})} | custom-call | flops 1 | bytes 1 | tf_op jit(solution)/shard_map/mix_and_back/pallas_call | solution.py:491
  209.0 1.7 collective-permute-start.42
  210.7 9.8 %mix_and_back.8 = (bf16[512,3584]{1,0:T(8,128)(2,1)}, bf16[1024,3584]{1,0:T(8,128)(2,1)}) custom-call(s32[49]{0:T(128)} %stack.263.t, bf16[512,4096]{1,0:T(8,128)(2,1)} %more_features.5.refs_3_.l_ref, bf16[64,3584]{1,0:T(8,128)(2,1)} %get-tuple-element.69.a_ref, ...), custom_call_target="tpu_custom_call", output_to_operand_aliasing={{1}: (22, {}), {0}: (23, {})} | custom-call | flops 1 | bytes 1 | tf_op jit(solution)/shard_map/mix_and_back/pallas_call | solution.py:491
  221.7 1.7 collective-permute-start.44
  223.4 8.1 %mix_and_back.9 = (bf16[512,3584]{1,0:T(8,128)(2,1)}, bf16[1024,3584]{1,0:T(8,128)(2,1)}) custom-call(s32[49]{0:T(128)} %stack.263.t, bf16[512,4096]{1,0:T(8,128)(2,1)} %more_features.5.refs_3_.l_ref, bf16[64,3584]{1,0:T(8,128)(2,1)} %get-tuple-element.73.a_ref, ...), custom_call_target="tpu_custom_call", output_to_operand_aliasing={{1}: (22, {}), {0}: (23, {})} | custom-call | flops 1 | bytes 1 | tf_op jit(solution)/shard_map/mix_and_back/pallas_call | solution.py:491
  232.5 3.4 %mix_pair.3 = bf16[1024,3584]{1,0:T(8,128)(2,1)} custom-call(s32[49]{0:T(128)} %stack.263.t, bf16[64,3584]{1,0:T(8,128)(2,1)} %get-tuple-element.77.a_ref, bf16[64,3584]{1,0:T(8,128)(2,1)} %get-tuple-element.78.b_ref, bf16[512,3584]{1,0:T(8,128)(2,1)} %join.19.s_ref, bf16[1024,3584]{1,0:T(8,128)(2,1)} %get-tuple-element.76.refs_2_.held), custom_call_target="tpu_custom_call", output_to_operand_aliasing={{}: (4, {})} | custom-call | flops 1 | bytes 1 | tf_op jit(solution)/shard_map/mix_pair/pallas_call | solution.py:431
  (162 shorter events, 33.8 us)
Async XLA Ops:
  6.6 9.4 %copy-start.32 = (bf16[128,512]{1,0:T(8,128)(2,1)S(1)}, bf16[128,512]{1,0:T(8,128)(2,1)}, u32[]{:S(2)}) copy-start(bf16[128,512]{1,0:T(8,128)(2,1)} %partial_blocks.3) | copy-start | bytes 393220
  6.6 9.4 %collective-permute-start = (bf16[128,512]{1,0:T(8,128)(2,1)}, bf16[128,512]{1,0:T(8,128)(2,1)S(1)}, u32[]{:S(2)}, u32[]{:S(2)}) collective-permute-start(bf16[128,512]{1,0:T(8,128)(2,1)} %partial_blocks.3), channel_id=1, source_target_pairs={{0,2},{1,3},{2,0},{3,1},{4,6},{5,7},{6,4},{7,5},{8,10},{9,11},{10,... | collective-permute-start | bytes 393224 | tf_op jit(solution)/shard_map/ppermute | solution.py:52
  15.9 10.8 %collective-permute-start.3 = (bf16[384,512]{1,0:T(8,128)(2,1)}, bf16[384,512]{1,0:T(8,128)(2,1)S(1)}, u32[]{:S(2)}, u32[]{:S(2)}) collective-permute-start(bf16[384,512]{1,0:T(8,128)(2,1)} %partial_blocks.4.refs_0_), channel_id=1, source_target_pairs={{0,2},{1,3},{2,0},{3,1},{4,6},{5,7},{6,4},{7,5},{8,10},{9,11},{10,... | collective-permute-start | bytes 1179656 | tf_op jit(solution)/shard_map/ppermute | solution.py:52
  16.0 1.4 collective-permute-start.1
  23.2 21.0 %collective-permute-start.2 = (bf16[64,3584]{1,0:T(8,128)(2,1)}, bf16[64,3584]{1,0:T(8,128)(2,1)S(1)}, u32[]{:S(2)}, u32[]{:S(2)}) collective-permute-start(bf16[64,3584]{1,0:T(8,128)(2,1)} %get-tuple-element.43.refs_1_), channel_id=1, source_target_pairs={{0,8},{8,16},{16,24},{24,28},{28,20},{20,12},{12,4},{4,0},{1,9},{9... | collective-permute-start | bytes 1376264 | tf_op jit(solution)/shard_map/ppermute | solution.py:563
  25.3 18.9 %collective-permute-start.7 = (bf16[64,3584]{1,0:T(8,128)(2,1)}, bf16[64,3584]{1,0:T(8,128)(2,1)S(1)}, u32[]{:S(2)}, u32[]{:S(2)}) collective-permute-start(bf16[64,3584]{1,0:T(8,128)(2,1)} %get-tuple-element.44.refs_2_), channel_id=1, source_target_pairs={{8,0},{16,8},{24,16},{28,24},{20,28},{12,20},{4,12},{0,4},{9,1},{1... | collective-permute-start | bytes 1376264 | tf_op jit(solution)/shard_map/ppermute | solution.py:563
  25.3 9.9 %collective-permute-start.4 = (bf16[384,512]{1,0:T(8,128)(2,1)S(1)}, bf16[384,512]{1,0:T(8,128)(2,1)S(1)}, u32[]{:S(2)}, u32[]{:S(2)}) collective-permute-start(bf16[384,512]{1,0:T(8,128)(2,1)S(1)} %copy-done.28), channel_id=1, source_target_pairs={{0,1},{1,0},{2,3},{3,2},{4,5},{5,4},{6,7},{7,6},{8,9},{9,8},{10,11... | collective-permute-start | bytes 1179656 | tf_op jit(solution)/shard_map/ppermute | solution.py:52
  26.7 8.5 %collective-permute-start.5 = (bf16[384,512]{1,0:T(8,128)(2,1)S(1)}, bf16[384,512]{1,0:T(8,128)(2,1)S(1)}, u32[]{:S(2)}, u32[]{:S(2)}) collective-permute-start(bf16[384,512]{1,0:T(8,128)(2,1)S(1)} %collective-permute-done.3.refs_1_), channel_id=1, source_target_pairs={{0,1},{1,0},{2,3},{3,2},{4,5},{5,4},{6,7},{7,6},{8,9},{9,8},{10,11... | collective-permute-start | bytes 1179656 | tf_op jit(solution)/shard_map/ppermute | solution.py:52
  34.0 13.7 %copy-start.3 = (bf16[512,512]{1,0:T(8,128)(2,1)S(1)}, bf16[512,512]{1,0:T(8,128)(2,1)}, u32[]{:S(2)}) copy-start(bf16[512,512]{1,0:T(8,128)(2,1)} %partial_blocks.5.refs_4_.refs_0_) | copy-start | bytes 1572868
  34.1 14.7 %collective-permute-start.9 = (bf16[512,512]{1,0:T(8,128)(2,1)}, bf16[512,512]{1,0:T(8,128)(2,1)}, u32[]{:S(2)}, u32[]{:S(2)}) collective-permute-start(bf16[512,512]{1,0:T(8,128)(2,1)} %partial_blocks.5.refs_4_.refs_0_), channel_id=1, source_target_pairs={{0,2},{1,3},{2,0},{3,1},{4,6},{5,7},{6,4},{7,5},{8,10},{9,11},{10,... | collective-permute-start | bytes 1572872 | tf_op jit(solution)/shard_map/ppermute | solution.py:52
  45.6 12.3 %collective-permute-start.12 = (bf16[64,3584]{1,0:T(8,128)(2,1)S(1)}, bf16[64,3584]{1,0:T(8,128)(2,1)S(1)}, u32[]{:S(2)}, u32[]{:S(2)}) collective-permute-start(bf16[64,3584]{1,0:T(8,128)(2,1)S(1)} %get-tuple-element.94.refs_1_), channel_id=1, source_target_pairs={{8,0},{16,8},{24,16},{28,24},{20,28},{12,20},{4,12},{0,4},{9,1},{1... | collective-permute-start | bytes 1376264 | tf_op jit(solution)/shard_map/ppermute | solution.py:563
  47.2 12.1 %collective-permute-start.6 = (bf16[64,3584]{1,0:T(8,128)(2,1)S(1)}, bf16[64,3584]{1,0:T(8,128)(2,1)}, u32[]{:S(2)}, u32[]{:S(2)}) collective-permute-start(bf16[64,3584]{1,0:T(8,128)(2,1)S(1)} %get-tuple-element.95.refs_0_), channel_id=1, source_target_pairs={{0,8},{8,16},{16,24},{24,28},{28,20},{20,12},{12,4},{4,0},{1,9},{9... | collective-permute-start | bytes 1376264 | tf_op jit(solution)/shard_map/ppermute | solution.py:563
  47.7 17.4 %collective-permute-start.10 = (bf16[512,512]{1,0:T(8,128)(2,1)S(1)}, bf16[512,512]{1,0:T(8,128)(2,1)}, u32[]{:S(2)}, u32[]{:S(2)}) collective-permute-start(bf16[512,512]{1,0:T(8,128)(2,1)S(1)} %copy-done.3), channel_id=1, source_target_pairs={{0,1},{1,0},{2,3},{3,2},{4,5},{5,4},{6,7},{7,6},{8,9},{9,8},{10,11... | collective-permute-start | bytes 1572872 | tf_op jit(solution)/shard_map/ppermute | solution.py:52
  48.8 16.3 %collective-permute-start.11 = (bf16[512,512]{1,0:T(8,128)(2,1)}, bf16[512,512]{1,0:T(8,128)(2,1)}, u32[]{:S(2)}, u32[]{:S(2)}) collective-permute-start(bf16[512,512]{1,0:T(8,128)(2,1)} %collective-permute-done.9.refs_1_), channel_id=1, source_target_pairs={{0,1},{1,0},{2,3},{3,2},{4,5},{5,4},{6,7},{7,6},{8,9},{9,8},{10,11... | collective-permute-start | bytes 1572872 | tf_op jit(solution)/shard_map/ppermute | solution.py:52
  61.6 13.0 %collective-permute-start.14 = (bf16[64,3584]{1,0:T(8,128)(2,1)}, bf16[64,3584]{1,0:T(8,128)(2,1)}, u32[]{:S(2)}, u32[]{:S(2)}) collective-permute-start(bf16[64,3584]{1,0:T(8,128)(2,1)} %get-tuple-element.92.refs_5_), channel_id=1, source_target_pairs={{8,0},{16,8},{24,16},{28,24},{20,28},{12,20},{4,12},{0,4},{9,1},{1... | collective-permute-start | bytes 1376264 | tf_op jit(solution)/shard_map/ppermute | solution.py:563
  63.2 12.4 %collective-permute-start.8 = (bf16[64,3584]{1,0:T(8,128)(2,1)S(1)}, bf16[64,3584]{1,0:T(8,128)(2,1)}, u32[]{:S(2)}, u32[]{:S(2)}) collective-permute-start(bf16[64,3584]{1,0:T(8,128)(2,1)S(1)} %get-tuple-element.93.refs_4_), channel_id=1, source_target_pairs={{0,8},{8,16},{16,24},{24,28},{28,20},{20,12},{12,4},{4,0},{1,9},{9... | collective-permute-start | bytes 1376264 | tf_op jit(solution)/shard_map/ppermute | solution.py:563
  63.7 25.5 %collective-permute-start.15 = (bf16[512,1024]{1,0:T(8,128)(2,1)S(1)}, bf16[512,1024]{1,0:T(8,128)(2,1)S(1)}, u32[]{:S(2)}, u32[]{:S(2)}) collective-permute-start(bf16[512,1024]{1,0:T(8,128)(2,1)S(1)} %copy-done.4), channel_id=1, source_target_pairs={{0,2},{1,3},{2,0},{3,1},{4,6},{5,7},{6,4},{7,5},{8,10},{9,11},{10,... | collective-permute-start | bytes 3145736 | tf_op jit(solution)/shard_map/ppermute | solution.py:52
  78.0 12.1 %collective-permute-start.17 = (bf16[64,3584]{1,0:T(8,128)(2,1)}, bf16[64,3584]{1,0:T(8,128)(2,1)}, u32[]{:S(2)}, u32[]{:S(2)}) collective-permute-start(bf16[64,3584]{1,0:T(8,128)(2,1)} %get-tuple-element.90.refs_1_), channel_id=1, source_target_pairs={{8,0},{16,8},{24,16},{28,24},{20,28},{12,20},{4,12},{0,4},{9,1},{1... | collective-permute-start | bytes 1376264 | tf_op jit(solution)/shard_map/ppermute | solution.py:563
  79.6 11.3 %collective-permute-start.13 = (bf16[64,3584]{1,0:T(8,128)(2,1)S(1)}, bf16[64,3584]{1,0:T(8,128)(2,1)}, u32[]{:S(2)}, u32[]{:S(2)}) collective-permute-start(bf16[64,3584]{1,0:T(8,128)(2,1)S(1)} %get-tuple-element.91.refs_0_), channel_id=1, source_target_pairs={{0,8},{8,16},{16,24},{24,28},{28,20},{20,12},{12,4},{4,0},{1,9},{9... | collective-permute-start | bytes 1376264 | tf_op jit(solution)/shard_map/ppermute | solution.py:563
  93.5 11.8 %collective-permute-start.21 = (bf16[64,3584]{1,0:T(8,128)(2,1)}, bf16[64,3584]{1,0:T(8,128)(2,1)}, u32[]{:S(2)}, u32[]{:S(2)}) collective-permute-start(bf16[64,3584]{1,0:T(8,128)(2,1)} %get-tuple-element.88.refs_1_), channel_id=1, source_target_pairs={{8,0},{16,8},{24,16},{28,24},{20,28},{12,20},{4,12},{0,4},{9,1},{1... | collective-permute-start | bytes 1376264 | tf_op jit(solution)/shard_map/ppermute | solution.py:563
  95.6 9.4 %copy-start.6 = (bf16[512,1024]{1,0:T(8,128)(2,1)S(1)}, bf16[512,1024]{1,0:T(8,128)(2,1)}, u32[]{:S(2)}) copy-start(bf16[512,1024]{1,0:T(8,128)(2,1)} %copy-done.5) | copy-start | bytes 3145732
  95.6 11.0 %collective-permute-start.16 = (bf16[64,3584]{1,0:T(8,128)(2,1)}, bf16[64,3584]{1,0:T(8,128)(2,1)}, u32[]{:S(2)}, u32[]{:S(2)}) collective-permute-start(bf16[64,3584]{1,0:T(8,128)(2,1)} %get-tuple-element.89.refs_0_), channel_id=1, source_target_pairs={{0,8},{8,16},{16,24},{24,28},{28,20},{20,12},{12,4},{4,0},{1,9},{9... | collective-permute-start | bytes 1376264 | tf_op jit(solution)/shard_map/ppermute | solution.py:563
  95.6 18.2 %collective-permute-start.19 = (bf16[512,1024]{1,0:T(8,128)(2,1)S(1)}, bf16[512,1024]{1,0:T(8,128)(2,1)}, u32[]{:S(2)}, u32[]{:S(2)}) collective-permute-start(bf16[512,1024]{1,0:T(8,128)(2,1)S(1)} %copy-done.4), channel_id=1, source_target_pairs={{0,1},{1,0},{2,3},{3,2},{4,5},{5,4},{6,7},{7,6},{8,9},{9,8},{10,11... | collective-permute-start | bytes 3145736 | tf_op jit(solution)/shard_map/ppermute | solution.py:52
  95.6 25.7 %collective-permute-start.22 = (bf16[512,1024]{1,0:T(8,128)(2,1)S(1)}, bf16[512,1024]{1,0:T(8,128)(2,1)}, u32[]{:S(2)}, u32[]{:S(2)}) collective-permute-start(bf16[512,1024]{1,0:T(8,128)(2,1)S(1)} %copy-done.1), channel_id=1, source_target_pairs={{0,2},{1,3},{2,0},{3,1},{4,6},{5,7},{6,4},{7,5},{8,10},{9,11},{10,... | collective-permute-start | bytes 3145736 | tf_op jit(solution)/shard_map/ppermute | solution.py:52
  104.9 8.9 %collective-permute-start.20 = (bf16[512,1024]{1,0:T(8,128)(2,1)S(1)}, bf16[512,1024]{1,0:T(8,128)(2,1)}, u32[]{:S(2)}, u32[]{:S(2)}) collective-permute-start(bf16[512,1024]{1,0:T(8,128)(2,1)S(1)} %copy-done.6), channel_id=1, source_target_pairs={{0,1},{1,0},{2,3},{3,2},{4,5},{5,4},{6,7},{7,6},{8,9},{9,8},{10,11... | collective-permute-start | bytes 3145736 | tf_op jit(solution)/shard_map/ppermute | solution.py:52
  109.1 12.2 %collective-permute-start.26 = (bf16[64,3584]{1,0:T(8,128)(2,1)}, bf16[64,3584]{1,0:T(8,128)(2,1)}, u32[]{:S(2)}, u32[]{:S(2)}) collective-permute-start(bf16[64,3584]{1,0:T(8,128)(2,1)} %get-tuple-element.86.refs_4_), channel_id=1, source_target_pairs={{8,0},{16,8},{24,16},{28,24},{20,28},{12,20},{4,12},{0,4},{9,1},{1... | collective-permute-start | bytes 1376264 | tf_op jit(solution)/shard_map/ppermute | solution.py:563
  110.8 11.6 %collective-permute-start.18 = (bf16[64,3584]{1,0:T(8,128)(2,1)}, bf16[64,3584]{1,0:T(8,128)(2,1)}, u32[]{:S(2)}, u32[]{:S(2)}) collective-permute-start(bf16[64,3584]{1,0:T(8,128)(2,1)} %get-tuple-element.87.refs_3_), channel_id=1, source_target_pairs={{0,8},{8,16},{16,24},{24,28},{28,20},{20,12},{12,4},{4,0},{1,9},{9... | collective-permute-start | bytes 1376264 | tf_op jit(solution)/shard_map/ppermute | solution.py:563
  113.8 13.3 %collective-permute-start.24 = (bf16[512,1024]{1,0:T(8,128)(2,1)S(1)}, bf16[512,1024]{1,0:T(8,128)(2,1)}, u32[]{:S(2)}, u32[]{:S(2)}) collective-permute-start(bf16[512,1024]{1,0:T(8,128)(2,1)S(1)} %copy-done.1), channel_id=1, source_target_pairs={{0,1},{1,0},{2,3},{3,2},{4,5},{5,4},{6,7},{7,6},{8,9},{9,8},{10,11... | collective-permute-start | bytes 3145736 | tf_op jit(solution)/shard_map/ppermute | solution.py:52
  121.3 5.7 %collective-permute-start.25 = (bf16[512,1024]{1,0:T(8,128)(2,1)}, bf16[512,1024]{1,0:T(8,128)(2,1)}, u32[]{:S(2)}, u32[]{:S(2)}) collective-permute-start(bf16[512,1024]{1,0:T(8,128)(2,1)} %collective-permute-done.22.refs_2_.refs_1_), channel_id=1, source_target_pairs={{0,1},{1,0},{2,3},{3,2},{4,5},{5,4},{6,7},{7,6},{8,9},{9,8},{10,11... | collective-permute-start | bytes 3145736 | tf_op jit(solution)/shard_map/ppermute | solution.py:52
  125.0 12.0 %collective-permute-start.28 = (bf16[64,3584]{1,0:T(8,128)(2,1)}, bf16[64,3584]{1,0:T(8,128)(2,1)S(1)}, u32[]{:S(2)}, u32[]{:S(2)}) collective-permute-start(bf16[64,3584]{1,0:T(8,128)(2,1)} %get-tuple-element.84.refs_6_), channel_id=1, source_target_pairs={{8,0},{16,8},{24,16},{28,24},{20,28},{12,20},{4,12},{0,4},{9,1},{1... | collective-permute-start | bytes 1376264 | tf_op jit(solution)/shard_map/ppermute | solution.py:563
  126.6 12.2 %collective-permute-start.23 = (bf16[64,3584]{1,0:T(8,128)(2,1)}, bf16[64,3584]{1,0:T(8,128)(2,1)}, u32[]{:S(2)}, u32[]{:S(2)}) collective-permute-start(bf16[64,3584]{1,0:T(8,128)(2,1)} %get-tuple-element.85.refs_5_), channel_id=1, source_target_pairs={{0,8},{8,16},{16,24},{24,28},{28,20},{20,12},{12,4},{4,0},{1,9},{9... | collective-permute-start | bytes 1376264 | tf_op jit(solution)/shard_map/ppermute | solution.py:563
  130.3 25.2 %collective-permute-start.32 = (bf16[512,1024]{1,0:T(8,128)(2,1)S(1)}, bf16[512,1024]{1,0:T(8,128)(2,1)}, u32[]{:S(2)}, u32[]{:S(2)}) collective-permute-start(bf16[512,1024]{1,0:T(8,128)(2,1)S(1)} %copy-done), channel_id=1, source_target_pairs={{0,2},{1,3},{2,0},{3,1},{4,6},{5,7},{6,4},{7,5},{8,10},{9,11},{10,... | collective-permute-start | bytes 3145736 | tf_op jit(solution)/shard_map/ppermute | solution.py:52
  141.4 11.1 %collective-permute-start.29 = (bf16[64,3584]{1,0:T(8,128)(2,1)S(1)}, bf16[64,3584]{1,0:T(8,128)(2,1)S(1)}, u32[]{:S(2)}, u32[]{:S(2)}) collective-permute-start(bf16[64,3584]{1,0:T(8,128)(2,1)S(1)} %get-tuple-element.82.refs_1_), channel_id=1, source_target_pairs={{8,0},{16,8},{24,16},{28,24},{20,28},{12,20},{4,12},{0,4},{9,1},{1... | collective-permute-start | bytes 1376264 | tf_op jit(solution)/shard_map/ppermute | solution.py:622
  143.2 11.5 %collective-permute-start.27 = (bf16[64,3584]{1,0:T(8,128)(2,1)S(1)}, bf16[64,3584]{1,0:T(8,128)(2,1)S(1)}, u32[]{:S(2)}, u32[]{:S(2)}) collective-permute-start(bf16[64,3584]{1,0:T(8,128)(2,1)S(1)} %get-tuple-element.83.refs_0_), channel_id=1, source_target_pairs={{0,8},{8,16},{16,24},{24,28},{28,20},{20,12},{12,4},{4,0},{1,9},{9... | collective-permute-start | bytes 1376264 | tf_op jit(solution)/shard_map/ppermute | solution.py:622
  155.5 5.9 %collective-permute-start.33 = (bf16[512,1024]{1,0:T(8,128)(2,1)}, bf16[512,1024]{1,0:T(8,128)(2,1)S(1)}, u32[]{:S(2)}, u32[]{:S(2)}) collective-permute-start(bf16[512,1024]{1,0:T(8,128)(2,1)} %get-tuple-element.56.refs_0_), channel_id=1, source_target_pairs={{0,1},{1,0},{2,3},{3,2},{4,5},{5,4},{6,7},{7,6},{8,9},{9,8},{10,11... | collective-permute-start | bytes 3145736 | tf_op jit(solution)/shard_map/ppermute | solution.py:52
  155.5 5.9 %collective-permute-start.34 = (bf16[512,1024]{1,0:T(8,128)(2,1)}, bf16[512,1024]{1,0:T(8,128)(2,1)S(1)}, u32[]{:S(2)}, u32[]{:S(2)}) collective-permute-start(bf16[512,1024]{1,0:T(8,128)(2,1)} %get-tuple-element.57.refs_1_), channel_id=1, source_target_pairs={{0,1},{1,0},{2,3},{3,2},{4,5},{5,4},{6,7},{7,6},{8,9},{9,8},{10,11... | collective-permute-start | bytes 3145736 | tf_op jit(solution)/shard_map/ppermute | solution.py:52
  156.0 12.7 %collective-permute-start.30 = (bf16[64,3584]{1,0:T(8,128)(2,1)}, bf16[64,3584]{1,0:T(8,128)(2,1)S(1)}, u32[]{:S(2)}, u32[]{:S(2)}) collective-permute-start(bf16[64,3584]{1,0:T(8,128)(2,1)} %get-tuple-element.53.a_ref.refs_2_), channel_id=1, source_target_pairs={{0,8},{8,16},{16,24},{24,28},{28,20},{20,12},{12,4},{4,0},{1,9},{9... | collective-permute-start | bytes 1376264 | tf_op jit(solution)/shard_map/ppermute | solution.py:622
  156.3 12.4 %collective-permute-start.31 = (bf16[64,3584]{1,0:T(8,128)(2,1)}, bf16[64,3584]{1,0:T(8,128)(2,1)S(1)}, u32[]{:S(2)}, u32[]{:S(2)}) collective-permute-start(bf16[64,3584]{1,0:T(8,128)(2,1)} %get-tuple-element.54.b_ref.refs_3_), channel_id=1, source_target_pairs={{8,0},{16,8},{24,16},{28,24},{20,28},{12,20},{4,12},{0,4},{9,1},{1... | collective-permute-start | bytes 1376264 | tf_op jit(solution)/shard_map/ppermute | solution.py:622
  170.3 11.9 %collective-permute-start.35 = (bf16[64,3584]{1,0:T(8,128)(2,1)}, bf16[64,3584]{1,0:T(8,128)(2,1)S(1)}, u32[]{:S(2)}, u32[]{:S(2)}) collective-permute-start(bf16[64,3584]{1,0:T(8,128)(2,1)} %get-tuple-element.58.a_ref), channel_id=1, source_target_pairs={{0,8},{8,16},{16,24},{24,28},{28,20},{20,12},{12,4},{4,0},{1,9},{9... | collective-permute-start | bytes 1376264 | tf_op jit(solution)/shard_map/ppermute | solution.py:622
  170.6 11.6 %collective-permute-start.36 = (bf16[64,3584]{1,0:T(8,128)(2,1)}, bf16[64,3584]{1,0:T(8,128)(2,1)S(1)}, u32[]{:S(2)}, u32[]{:S(2)}) collective-permute-start(bf16[64,3584]{1,0:T(8,128)(2,1)} %get-tuple-element.59.b_ref), channel_id=1, source_target_pairs={{8,0},{16,8},{24,16},{28,24},{20,28},{12,20},{4,12},{0,4},{9,1},{1... | collective-permute-start | bytes 1376264 | tf_op jit(solution)/shard_map/ppermute | solution.py:622
  183.1 11.8 %collective-permute-start.37 = (bf16[64,3584]{1,0:T(8,128)(2,1)}, bf16[64,3584]{1,0:T(8,128)(2,1)S(1)}, u32[]{:S(2)}, u32[]{:S(2)}) collective-permute-start(bf16[64,3584]{1,0:T(8,128)(2,1)} %get-tuple-element.61.a_ref), channel_id=1, source_target_pairs={{0,8},{8,16},{16,24},{24,28},{28,20},{20,12},{12,4},{4,0},{1,9},{9... | collective-permute-start | bytes 1376264 | tf_op jit(solution)/shard_map/ppermute | solution.py:622
  183.5 11.5 %collective-permute-start.38 = (bf16[64,3584]{1,0:T(8,128)(2,1)}, bf16[64,3584]{1,0:T(8,128)(2,1)S(1)}, u32[]{:S(2)}, u32[]{:S(2)}) collective-permute-start(bf16[64,3584]{1,0:T(8,128)(2,1)} %get-tuple-element.62.b_ref), channel_id=1, source_target_pairs={{8,0},{16,8},{24,16},{28,24},{20,28},{12,20},{4,12},{0,4},{9,1},{1... | collective-permute-start | bytes 1376264 | tf_op jit(solution)/shard_map/ppermute | solution.py:622
  195.9 11.8 %collective-permute-start.39 = (bf16[64,3584]{1,0:T(8,128)(2,1)}, bf16[64,3584]{1,0:T(8,128)(2,1)S(1)}, u32[]{:S(2)}, u32[]{:S(2)}) collective-permute-start(bf16[64,3584]{1,0:T(8,128)(2,1)} %get-tuple-element.65.a_ref), channel_id=1, source_target_pairs={{0,8},{8,16},{16,24},{24,28},{28,20},{20,12},{12,4},{4,0},{1,9},{9... | collective-permute-start | bytes 1376264 | tf_op jit(solution)/shard_map/ppermute | solution.py:622
  196.2 11.5 %collective-permute-start.40 = (bf16[64,3584]{1,0:T(8,128)(2,1)}, bf16[64,3584]{1,0:T(8,128)(2,1)S(1)}, u32[]{:S(2)}, u32[]{:S(2)}) collective-permute-start(bf16[64,3584]{1,0:T(8,128)(2,1)} %get-tuple-element.66.b_ref), channel_id=1, source_target_pairs={{8,0},{16,8},{24,16},{28,24},{20,28},{12,20},{4,12},{0,4},{9,1},{1... | collective-permute-start | bytes 1376264 | tf_op jit(solution)/shard_map/ppermute | solution.py:622
  208.6 11.8 %collective-permute-start.41 = (bf16[64,3584]{1,0:T(8,128)(2,1)}, bf16[64,3584]{1,0:T(8,128)(2,1)S(1)}, u32[]{:S(2)}, u32[]{:S(2)}) collective-permute-start(bf16[64,3584]{1,0:T(8,128)(2,1)} %get-tuple-element.69.a_ref), channel_id=1, source_target_pairs={{0,8},{8,16},{16,24},{24,28},{28,20},{20,12},{12,4},{4,0},{1,9},{9... | collective-permute-start | bytes 1376264 | tf_op jit(solution)/shard_map/ppermute | solution.py:622
  209.0 11.5 %collective-permute-start.42 = (bf16[64,3584]{1,0:T(8,128)(2,1)}, bf16[64,3584]{1,0:T(8,128)(2,1)S(1)}, u32[]{:S(2)}, u32[]{:S(2)}) collective-permute-start(bf16[64,3584]{1,0:T(8,128)(2,1)} %get-tuple-element.70.b_ref), channel_id=1, source_target_pairs={{8,0},{16,8},{24,16},{28,24},{20,28},{12,20},{4,12},{0,4},{9,1},{1... | collective-permute-start | bytes 1376264 | tf_op jit(solution)/shard_map/ppermute | solution.py:622
  221.4 10.2 %collective-permute-start.43 = (bf16[64,3584]{1,0:T(8,128)(2,1)}, bf16[64,3584]{1,0:T(8,128)(2,1)S(1)}, u32[]{:S(2)}, u32[]{:S(2)}) collective-permute-start(bf16[64,3584]{1,0:T(8,128)(2,1)} %get-tuple-element.73.a_ref), channel_id=1, source_target_pairs={{0,8},{8,16},{16,24},{24,28},{28,20},{20,12},{12,4},{4,0},{1,9},{9... | collective-permute-start | bytes 1376264 | tf_op jit(solution)/shard_map/ppermute | solution.py:622
  221.7 9.9 %collective-permute-start.44 = (bf16[64,3584]{1,0:T(8,128)(2,1)}, bf16[64,3584]{1,0:T(8,128)(2,1)S(1)}, u32[]{:S(2)}, u32[]{:S(2)}) collective-permute-start(bf16[64,3584]{1,0:T(8,128)(2,1)} %get-tuple-element.74.b_ref), channel_id=1, source_target_pairs={{8,0},{16,8},{24,16},{28,24},{20,28},{12,20},{4,12},{0,4},{9,1},{1... | collective-permute-start | bytes 1376264 | tf_op jit(solution)/shard_map/ppermute | solution.py:622
  (35 other events, 82.8 us)

commit v2 on v1

--- a/solution.py
+++ b/solution.py
@@ -13,7 +13,7 @@
 mix_share = 0.5
 
 
-VMEM_LIMIT = 54 * 2**20
+MIB = 2**20
 ANY = pl.BlockSpec(memory_space=pl.ANY)
 F32 = jnp.float32
 BF16 = jnp.bfloat16
@@ -31,9 +31,9 @@
     return jax.ShapeDtypeStruct(x.shape, x.dtype)
 
 
-def options():
+def options(limit=50):
     return dict(
-        compiler_params=pltpu.CompilerParams(vmem_limit_bytes=VMEM_LIMIT),
+        compiler_params=pltpu.CompilerParams(vmem_limit_bytes=limit * MIB),
         cost_estimate=pl.CostEstimate(flops=1, bytes_accessed=1, transcendentals=0),
     )
 
@@ -440,7 +440,7 @@
         out_shape=like(mixed),
         input_output_aliases={4: 0},
         name="mix_pair",
-        **options(),
+        **options(58),
     )(table.values, *got, stored, mixed)
 
 
@@ -504,7 +504,7 @@
         out_shape=[jax.ShapeDtypeStruct((tokens, width), BF16), like(mixed)],
         input_output_aliases=aliases,
         name="mix_and_back",
-        **options(),
+        **options(58),
     )(table.values, left, *got, stored, *([w] * (len(blocks) + 1)), *more)
 
 

time: 237 us -> 234 us (0.987)
  Pallas kernels: 140 us -> 130 us
  waiting for transfers between devices: 26.6 us -> 31.5 us
    pallas_call x3, Pallas kernels: 27.4 us -> 24.2 us  [tail_rows(): pl.pallas_call(kernel, grid_spec=grid_of((count // tile,), [pl.BlockSpec(...]
    unnamed x76 -> x62, local copies, waits for them, and re-layouts: 12.8 us -> 15.3 us
  transfers between devices with their start and end apart: 45 -> 45, of which waited for: 16 -> 17; matrix products, arithmetic and copies ran while one was open for 6% -> 6% of each run, Pallas kernels for 56% -> 53%
where the time goes in v2:
time: 234 us
  Pallas kernels  130 us (56%)
  starting transfers between devices  37.3 us (16%)
  waiting for transfers between devices  31.5 us (13%)
  other arithmetic  17.3 us (7%)
  local copies, waits for them, and re-layouts  15.4 us (7%)
    pallas_call x5, Pallas kernels, mix_and_back(): pl.pallas_call(kernel, grid_spec=grid_of((count,), [pl.BlockSpec((tokens,...  47.2 us
    pallas_call x3, Pallas kernels, tail_rows(): pl.pallas_call(kernel, grid_spec=grid_of((count // tile,), [pl.BlockSpec(...  24.2 us
    pallas_call x3, Pallas kernels, stepped_blocks(): pl.pallas_call(kernel, grid_spec=grid_of((1,), [ANY] * (2 + len(terms) +...  19.5 us
    pallas_call x3, Pallas kernels, partial_blocks(): pl.pallas_call(kernel, grid_spec=grid_of((1,), [ANY] * (3 + extra), [ANY]...  15.8 us
    unnamed x62, local copies, waits for them, and re-layouts  15.3 us
    convert_element_type x7, other arithmetic, add(): return (a.astype(F32) + b.astype(F32)).astype(BF16)  14.8 us
    ppermute x7, starting transfers between devices, shards(): lax.ppermute(send[1], 'island', back)  11.9 us
    ppermute x17, waiting for transfers between devices, across(): return lax.ppermute(x, 'tensor', swapped(count, bit))  10.1 us
  transfers between devices with their start and end apart: 45, of which 17 were waited for; matrix products, arithmetic and copies ran while one was open for 6% of the time, Pallas kernels for 53%

profile of v2, /device:TPU:0, one launch (start us, length us, event | category | flops | bytes accessed | tf_op | source)
XLA Modules:
  0.0 233.6 jit_solution(16327260726316763574)
XLA Ops:
  2.6 4.0 %partial_blocks.3 = bf16[128,512]{1,0:T(8,128)(2,1)S(1)} custom-call(s32[49]{0:T(128)S(1)} %stack.263.t, bf16[4096,3584]{1,0:T(8,128)(2,1)} %bitcast.60, bf16[512,3584]{1,0:T(8,128)(2,1)} %bitcast.155, bf16[1024,512]{1,0:T(8,128)(2,1)S(1)} %bitcast.54), custom_call_target="tpu_custom_call" | custom-call | flops 1 | bytes 1 | tf_op jit(solution)/shard_map/partial_blocks/pallas_call | solution.py:165
  6.6 3.0 %collective-permute-start = (bf16[128,512]{1,0:T(8,128)(2,1)S(1)}, bf16[128,512]{1,0:T(8,128)(2,1)S(1)}, u32[]{:S(2)}, u32[]{:S(2)}) collective-permute-start(bf16[128,512]{1,0:T(8,128)(2,1)S(1)} %partial_blocks.3), channel_id=1, source_target_pairs={{0,2},{1,3},{2,0},{3,1},{4,6},{5,7},{6,4},{7,5},{8,10},{9,11},{10,... | collective-permute-start | bytes 393224 | tf_op jit(solution)/shard_map/ppermute | solution.py:52
  9.6 5.5 %partial_blocks.4.refs_0_ = bf16[384,512]{1,0:T(8,128)(2,1)S(1)} custom-call(s32[49]{0:T(128)S(1)} %stack.263.t, bf16[4096,3584]{1,0:T(8,128)(2,1)} %bitcast.61, bf16[512,3584]{1,0:T(8,128)(2,1)} %bitcast.156, bf16[1024,512]{1,0:T(8,128)(2,1)S(1)} %bitcast.55), custom_call_target="tpu_custom_call" | custom-call | flops 1 | bytes 1 | tf_op jit(solution)/shard_map/partial_blocks/pallas_call | solution.py:165
  16.7 4.1 %stepped_blocks.3 = (bf16[128,3584]{1,0:T(8,128)(2,1)S(1)}, bf16[64,3584]{1,0:T(8,128)(2,1)S(1)}, bf16[64,3584]{1,0:T(8,128)(2,1)S(1)}, bf16[128,512]{1,0:T(8,128)(2,1)S(1)}) custom-call(s32[49]{0:T(128)S(1)} %stack.263.t, bf16[4096,3584]{1,0:T(8,128)(2,1)} %bitcast.62, bf16[512,3584]{1,0:T(8,128)(2,1)} %bitcast.157, ...), custom_call_target="tpu_custom_call" | custom-call | flops 1 | bytes 1 | tf_op jit(solution)/shard_map/stepped_blocks/pallas_call | solution.py:241
  22.4 2.1 collective-permute-start.2
  25.8 6.3 %partial_blocks.5.refs_4_.refs_0_ = bf16[512,512]{1,0:T(8,128)(2,1)S(1)} custom-call(s32[49]{0:T(128)S(1)} %stack.263.t, bf16[4096,3584]{1,0:T(8,128)(2,1)} %bitcast.63, bf16[512,3584]{1,0:T(8,128)(2,1)} %bitcast.158, bf16[1024,512]{1,0:T(8,128)(2,1)S(1)} %bitcast.56, bf16[64,3584]{1,0:T(8,128)(2,1)S(1)} %get-tuple-element.43.refs_1_, ...), custom_call_target="tpu_custom_call" | custom-call | flops 1 | bytes 1 | tf_op jit(solution)/shard_map/partial_blocks/pallas_call | solution.py:165
  33.3 6.9 %stepped_blocks.4 = (bf16[384,3584]{1,0:T(8,128)(2,1)}, bf16[384,512]{1,0:T(8,128)(2,1)S(1)}) custom-call(s32[49]{0:T(128)S(1)} %stack.263.t, bf16[4096,3584]{1,0:T(8,128)(2,1)} %bitcast.64, bf16[512,3584]{1,0:T(8,128)(2,1)} %bitcast.159, bf16[384,512]{1,0:T(8,128)(2,1)S(1)} %partial_blocks.4.refs_0_, bf16[384,512]{1,0:T(8,128)(2,1)S(1)} %collective-permute-done.3.refs_1_, ...), custom_call_target="tpu_custom_call" | custom-call | flops 1 | bytes 1 | tf_op jit(solution)/shard_map/stepped_blocks/pallas_call | solution.py:241
  40.3 2.1 add_convert_fusion.10
  44.4 2.2 collective-permute-done.9.refs_1_
  46.7 8.1 %tail_rows.3 = (bf16[512,1024]{1,0:T(8,128)(2,1)S(1)}, bf16[1024,3584]{1,0:T(8,128)(2,1)}) custom-call(s32[49]{0:T(128)S(1)} %stack.263.t, bf16[4096,3584]{1,0:T(8,128)(2,1)} %bitcast.65, bf16[1024,512]{1,0:T(8,128)(2,1)S(1)} %bitcast.57, bf16[512,3584]{1,0:T(8,128)(2,1)} %bitcast.160, bf16[64,3584]{1,0:T(8,128)(2,1)S(1)} %get-tuple-element.95.refs_0_, ...), custom_call_target="tpu_custom_call" | custom-call | flops 1 | bytes 1 | tf_op jit(solution)/shard_map/tail_rows/pallas_call | solution.py:288
  55.9 2.5 %add_convert_fusion.8 = (bf16[64,3584]{1,0:T(8,128)(2,1)}, bf16[64,3584]{1,0:T(8,128)(2,1)S(1)}) fusion(bf16[64,3584]{1,0:T(8,128)(2,1)} %collective-permute-done.12, bf16[384,3584]{1,0:T(8,128)(2,1)} %join.14.refs_0_, bf16[64,3584]{1,0:T(8,128)(2,1)} %collective-permute-done.6), kind=kLoop, calls=%fused_computation.10 | loop fusion | flops 1835008 | bytes 2752512 | tf_op jit(solution)/shard_map/convert_element_type | solution.py:27
  58.3 1.6 collective-permute-start.14
  61.7 8.6 %stepped_blocks.5 = (bf16[512,3584]{1,0:T(8,128)(2,1)}, bf16[512,512]{1,0:T(8,128)(2,1)S(1)}) custom-call(s32[49]{0:T(128)S(1)} %stack.263.t, bf16[4096,3584]{1,0:T(8,128)(2,1)} %bitcast.66, bf16[512,3584]{1,0:T(8,128)(2,1)} %bitcast.161, bf16[512,512]{1,0:T(8,128)(2,1)S(1)} %partial_blocks.5.refs_4_.refs_0_, ...), custom_call_target="tpu_custom_call" | custom-call | flops 1 | bytes 1 | tf_op jit(solution)/shard_map/stepped_blocks/pallas_call | solution.py:241
  72.8 2.6 %add_convert_fusion.6 = (bf16[64,3584]{1,0:T(8,128)(2,1)}, bf16[64,3584]{1,0:T(8,128)(2,1)}) fusion(bf16[64,3584]{1,0:T(8,128)(2,1)} %collective-permute-done.14, bf16[384,3584]{1,0:T(8,128)(2,1)} %join.15.s_ref, bf16[64,3584]{1,0:T(8,128)(2,1)} %collective-permute-done.8), kind=kLoop, calls=%fused_computation.8 | loop fusion | flops 1835008 | bytes 2752512 | tf_op jit(solution)/shard_map/convert_element_type | solution.py:27
  75.4 1.6 collective-permute-start.17
  77.4 8.1 %tail_rows.4.refs_1_.refs_0_ = bf16[512,1024]{1,0:T(8,128)(2,1)S(1)} custom-call(s32[49]{0:T(128)S(1)} %stack.263.t, bf16[4096,3584]{1,0:T(8,128)(2,1)} %bitcast.67, bf16[1024,512]{1,0:T(8,128)(2,1)S(1)} %bitcast.58, bf16[512,3584]{1,0:T(8,128)(2,1)} %bitcast.162, bf16[64,3584]{1,0:T(8,128)(2,1)} %get-tuple-element.91.refs_0_, ...), custom_call_target="tpu_custom_call" | custom-call | flops 1 | bytes 1 | tf_op jit(solution)/shard_map/tail_rows/pallas_call | solution.py:288
  88.9 2.6 %add_convert_fusion.4 = (bf16[64,3584]{1,0:T(8,128)(2,1)}, bf16[64,3584]{1,0:T(8,128)(2,1)}) fusion(bf16[64,3584]{1,0:T(8,128)(2,1)} %collective-permute-done.17, bf16[512,3584]{1,0:T(8,128)(2,1)} %join.16.refs_0_, bf16[64,3584]{1,0:T(8,128)(2,1)} %collective-permute-done.13), kind=kLoop, calls=%fused_computation.6 | loop fusion | flops 1835008 | bytes 2752512 | tf_op jit(solution)/shard_map/convert_element_type | solution.py:27
  91.5 1.7 collective-permute-start.21
  93.5 8.1 %tail_rows.5.refs_1_.refs_0_ = bf16[512,1024]{1,0:T(8,128)(2,1)S(1)} custom-call(s32[49]{0:T(128)S(1)} %stack.263.t, bf16[4096,3584]{1,0:T(8,128)(2,1)} %bitcast.68, bf16[1024,512]{1,0:T(8,128)(2,1)S(1)} %bitcast.59, bf16[512,3584]{1,0:T(8,128)(2,1)} %bitcast.163, bf16[64,3584]{1,0:T(8,128)(2,1)} %get-tuple-element.89.refs_0_, ...), custom_call_target="tpu_custom_call" | custom-call | flops 1 | bytes 1 | tf_op jit(solution)/shard_map/tail_rows/pallas_call | solution.py:288
  104.2 2.4 %add_convert_fusion.2 = (bf16[64,3584]{1,0:T(8,128)(2,1)}, bf16[64,3584]{1,0:T(8,128)(2,1)S(1)}) fusion(bf16[64,3584]{1,0:T(8,128)(2,1)} %collective-permute-done.21, bf16[512,3584]{1,0:T(8,128)(2,1)} %join.17.refs_0_, bf16[64,3584]{1,0:T(8,128)(2,1)} %collective-permute-done.16), kind=kLoop, calls=%fused_computation.4 | loop fusion | flops 1835008 | bytes 2752512 | tf_op jit(solution)/shard_map/convert_element_type | solution.py:27
  106.6 1.7 collective-permute-start.26
  111.1 3.0 %more_features.3.refs_1_.refs_4_ = bf16[512,4096]{1,0:T(8,128)(2,1)} custom-call(bf16[512,1024]{1,0:T(8,128)(2,1)S(1)} %copy-done.9, bf16[512,1024]{1,0:T(8,128)(2,1)} %collective-permute-done.15.refs_2_.refs_1_, bf16[512,1024]{1,0:T(8,128)(2,1)} %collective-permute-done.19.refs_2_, ...), custom_call_target="tpu_custom_call", output_to_operand_aliasing={{}: (4, {})} | custom-call | flops 1 | bytes 1 | tf_op jit(solution)/shard_map/more_features/pallas_call | solution.py:344
  114.1 5.1 %collective-permute-done.22.refs_2_.refs_1_ = bf16[512,1024]{1,0:T(8,128)(2,1)} collective-permute-done((bf16[512,1024]{1,0:T(8,128)(2,1)S(1)}, bf16[512,1024]{1,0:T(8,128)(2,1)}, u32[]{:S(2)}, u32[]{:S(2)}) %collective-permute-start.22) | collective-permute-done | bytes 1048608 | tf_op jit(solution)/shard_map/ppermute | solution.py:52
  119.5 2.6 %add_convert_fusion = (bf16[64,3584]{1,0:T(8,128)(2,1)}, bf16[64,3584]{1,0:T(8,128)(2,1)}) fusion(bf16[64,3584]{1,0:T(8,128)(2,1)} %collective-permute-done.26, bf16[512,3584]{1,0:T(8,128)(2,1)} %join.18.refs_0_, bf16[64,3584]{1,0:T(8,128)(2,1)} %collective-permute-done.18), kind=kLoop, calls=%fused_computation.2 | loop fusion | flops 1835008 | bytes 2752512 | tf_op jit(solution)/shard_map/convert_element_type | solution.py:27
  122.0 1.7 collective-permute-start.28
  124.1 3.0 %more_features.4.refs_1_.refs_4_ = bf16[512,4096]{1,0:T(8,128)(2,1)} custom-call(bf16[512,1024]{1,0:T(8,128)(2,1)S(1)} %copy-done.6, bf16[512,1024]{1,0:T(8,128)(2,1)} %collective-permute-done.22.refs_2_.refs_1_, bf16[512,1024]{1,0:T(8,128)(2,1)} %collective-permute-done.24.refs_2_, ...), custom_call_target="tpu_custom_call", output_to_operand_aliasing={{}: (4, {})} | custom-call | flops 1 | bytes 1 | tf_op jit(solution)/shard_map/more_features/pallas_call | solution.py:344
  127.1 2.0 collective-permute-start.32
  129.1 5.8 %collective-permute-done.28.b_ref = bf16[64,3584]{1,0:T(8,128)(2,1)S(1)} collective-permute-done((bf16[64,3584]{1,0:T(8,128)(2,1)}, bf16[64,3584]{1,0:T(8,128)(2,1)S(1)}, u32[]{:S(2)}, u32[]{:S(2)}) %collective-permute-start.28) | collective-permute-done | bytes 458784 | tf_op jit(solution)/shard_map/ppermute | solution.py:563
  136.4 2.6 %subtract_convert_fusion = (bf16[64,3584]{1,0:T(8,128)(2,1)S(1)}, bf16[64,3584]{1,0:T(8,128)(2,1)S(1)}) fusion(f32[128,3584]{1,0:T(8,128)} %m_ref.1, bf16[64,3584]{1,0:T(8,128)(2,1)S(1)} %collective-permute-done.28.b_ref, f32[128,3584]{1,0:T(8,128)S(1)} %copy-done.7, bf16[512,3584]{1,0:T(8,128)(2,1)} %join.19.s_ref, ...), kind=kLoop, calls=%fused_computation | loop fusion | flops 5505024 | bytes 6422528 | tf_op jit(solution)/shard_map/convert_element_type | solution.py:603
  139.0 1.8 collective-permute-start.29
  141.0 6.3 %outer_step.1 = (f32[128,3584]{1,0:T(8,128)}, f32[128,3584]{1,0:T(8,128)}, bf16[1024,3584]{1,0:T(8,128)(2,1)}) custom-call(s32[49]{0:T(128)S(1)} %stack.263.t, bf16[64,3584]{1,0:T(8,128)(2,1)} %collective-permute-done.23.a_ref, bf16[64,3584]{1,0:T(8,128)(2,1)S(1)} %collective-permute-done.28.b_ref, ...), custom_call_target="tpu_custom_call", output_to_operand_aliasing={{2}: (6, {})} | custom-call | flops 1 | bytes 1 | tf_op jit(solution)/shard_map/outer_step/pallas_call | solution.py:396
  147.4 3.1 %collective-permute-done.29.refs_1_ = bf16[64,3584]{1,0:T(8,128)(2,1)S(1)} collective-permute-done((bf16[64,3584]{1,0:T(8,128)(2,1)S(1)}, bf16[64,3584]{1,0:T(8,128)(2,1)S(1)}, u32[]{:S(2)}, u32[]{:S(2)}) %collective-permute-start.29) | collective-permute-done | bytes 458784 | tf_op jit(solution)/shard_map/ppermute | solution.py:622
  150.4 1.9 collective-permute-done.27.refs_0_
  153.9 1.7 collective-permute-start.31
  155.6 3.5 %mix_pair.2.refs_5_.refs_2_.refs_17_ = bf16[1024,3584]{1,0:T(8,128)(2,1)} custom-call(s32[49]{0:T(128)} %copy-done.13, bf16[64,3584]{1,0:T(8,128)(2,1)} %get-tuple-element.53.a_ref.refs_2_, bf16[64,3584]{1,0:T(8,128)(2,1)} %get-tuple-element.54.b_ref.refs_3_, bf16[128,3584]{1,0:T(8,128)(2,1)} %copy-done.12, ...), custom_call_target="tpu_custom_call", output_to_operand_aliasing={{}: (4, {})} | custom-call | flops 1 | bytes 1 | tf_op jit(solution)/shard_map/mix_pair/pallas_call | solution.py:431
  160.1 2.7 %more_features.5.refs_3_.l_ref = bf16[512,4096]{1,0:T(8,128)(2,1)} custom-call(bf16[512,1024]{1,0:T(8,128)(2,1)S(1)} %copy-done.4, bf16[512,1024]{1,0:T(8,128)(2,1)} %get-tuple-element.57.refs_1_, bf16[512,1024]{1,0:T(8,128)(2,1)S(1)} %collective-permute-done.33.refs_2_, bf16[512,1024]{1,0:T(8,128)(2,1)} %copy-done.30, ...), custom_call_target="tpu_custom_call", output_to_operand_aliasing={{}: (4, {})} | custom-call | flops 1 | bytes 1 | tf_op jit(solution)/shard_map/more_features/pallas_call | solution.py:344
  162.8 3.5 %collective-permute-done.30.refs_0_ = bf16[64,3584]{1,0:T(8,128)(2,1)S(1)} collective-permute-done((bf16[64,3584]{1,0:T(8,128)(2,1)}, bf16[64,3584]{1,0:T(8,128)(2,1)S(1)}, u32[]{:S(2)}, u32[]{:S(2)}) %collective-permute-start.30) | collective-permute-done | bytes 458784 | tf_op jit(solution)/shard_map/ppermute | solution.py:622
  168.1 1.7 collective-permute-start.36
  169.9 9.7 %mix_and_back.5 = (bf16[512,3584]{1,0:T(8,128)(2,1)}, bf16[1024,3584]{1,0:T(8,128)(2,1)}) custom-call(s32[49]{0:T(128)} %copy-done.13, bf16[512,4096]{1,0:T(8,128)(2,1)} %more_features.5.refs_3_.l_ref, bf16[64,3584]{1,0:T(8,128)(2,1)} %get-tuple-element.58.a_ref, bf16[64,3584]{1,0:T(8,128)(2,1)} %get-tuple-element.59.b_ref, ...), custom_call_target="tpu_custom_call", output_to_operand_aliasing={{1}: (22, {})} | custom-call | flops 1 | bytes 1 | tf_op jit(solution)/shard_map/mix_and_back/pallas_call | solution.py:491
  181.1 1.7 collective-permute-start.38
  182.7 9.8 %mix_and_back.6 = (bf16[512,3584]{1,0:T(8,128)(2,1)}, bf16[1024,3584]{1,0:T(8,128)(2,1)}) custom-call(s32[49]{0:T(128)} %copy-done.13, bf16[512,4096]{1,0:T(8,128)(2,1)} %more_features.5.refs_3_.l_ref, bf16[64,3584]{1,0:T(8,128)(2,1)} %get-tuple-element.61.a_ref, ...), custom_call_target="tpu_custom_call", output_to_operand_aliasing={{1}: (22, {}), {0}: (23, {})} | custom-call | flops 1 | bytes 1 | tf_op jit(solution)/shard_map/mix_and_back/pallas_call | solution.py:491
  193.8 1.7 collective-permute-start.40
  195.5 9.8 %mix_and_back.7 = (bf16[512,3584]{1,0:T(8,128)(2,1)}, bf16[1024,3584]{1,0:T(8,128)(2,1)}) custom-call(s32[49]{0:T(128)} %copy-done.13, bf16[512,4096]{1,0:T(8,128)(2,1)} %more_features.5.refs_3_.l_ref, bf16[64,3584]{1,0:T(8,128)(2,1)} %get-tuple-element.65.a_ref, ...), custom_call_target="tpu_custom_call", output_to_operand_aliasing={{1}: (22, {}), {0}: (23, {})} | custom-call | flops 1 | bytes 1 | tf_op jit(solution)/shard_map/mix_and_back/pallas_call | solution.py:491
  206.6 1.7 collective-permute-start.42
  208.2 9.8 %mix_and_back.8 = (bf16[512,3584]{1,0:T(8,128)(2,1)}, bf16[1024,3584]{1,0:T(8,128)(2,1)}) custom-call(s32[49]{0:T(128)} %copy-done.13, bf16[512,4096]{1,0:T(8,128)(2,1)} %more_features.5.refs_3_.l_ref, bf16[64,3584]{1,0:T(8,128)(2,1)} %get-tuple-element.69.a_ref, ...), custom_call_target="tpu_custom_call", output_to_operand_aliasing={{1}: (22, {}), {0}: (23, {})} | custom-call | flops 1 | bytes 1 | tf_op jit(solution)/shard_map/mix_and_back/pallas_call | solution.py:491
  219.3 1.7 collective-permute-start.44
  220.9 8.1 %mix_and_back.9 = (bf16[512,3584]{1,0:T(8,128)(2,1)}, bf16[1024,3584]{1,0:T(8,128)(2,1)}) custom-call(s32[49]{0:T(128)} %copy-done.13, bf16[512,4096]{1,0:T(8,128)(2,1)} %more_features.5.refs_3_.l_ref, bf16[64,3584]{1,0:T(8,128)(2,1)} %get-tuple-element.73.a_ref, ...), custom_call_target="tpu_custom_call", output_to_operand_aliasing={{1}: (22, {}), {0}: (23, {})} | custom-call | flops 1 | bytes 1 | tf_op jit(solution)/shard_map/mix_and_back/pallas_call | solution.py:491
  230.0 3.4 %mix_pair.3 = bf16[1024,3584]{1,0:T(8,128)(2,1)} custom-call(s32[49]{0:T(128)} %copy-done.13, bf16[64,3584]{1,0:T(8,128)(2,1)} %get-tuple-element.77.a_ref, bf16[64,3584]{1,0:T(8,128)(2,1)} %get-tuple-element.78.b_ref, bf16[512,3584]{1,0:T(8,128)(2,1)} %join.19.s_ref, bf16[1024,3584]{1,0:T(8,128)(2,1)} %get-tuple-element.76.refs_2_.held), custom_call_target="tpu_custom_call", output_to_operand_aliasing={{}: (4, {})} | custom-call | flops 1 | bytes 1 | tf_op jit(solution)/shard_map/mix_pair/pallas_call | solution.py:431
  (148 shorter events, 36.8 us)
Async XLA Ops:
  1.4 139.7 %copy-start.13 = (s32[49]{0:T(128)}, s32[49]{0:T(128)S(1)}, u32[]{:S(2)}) copy-start(s32[49]{0:T(128)S(1)} %stack.263.t) | copy-start | bytes 592
  6.6 8.6 %collective-permute-start = (bf16[128,512]{1,0:T(8,128)(2,1)S(1)}, bf16[128,512]{1,0:T(8,128)(2,1)S(1)}, u32[]{:S(2)}, u32[]{:S(2)}) collective-permute-start(bf16[128,512]{1,0:T(8,128)(2,1)S(1)} %partial_blocks.3), channel_id=1, source_target_pairs={{0,2},{1,3},{2,0},{3,1},{4,6},{5,7},{6,4},{7,5},{8,10},{9,11},{10,... | collective-permute-start | bytes 393224 | tf_op jit(solution)/shard_map/ppermute | solution.py:52
  15.2 10.6 %collective-permute-start.3 = (bf16[384,512]{1,0:T(8,128)(2,1)S(1)}, bf16[384,512]{1,0:T(8,128)(2,1)S(1)}, u32[]{:S(2)}, u32[]{:S(2)}) collective-permute-start(bf16[384,512]{1,0:T(8,128)(2,1)S(1)} %partial_blocks.4.refs_0_), channel_id=1, source_target_pairs={{0,2},{1,3},{2,0},{3,1},{4,6},{5,7},{6,4},{7,5},{8,10},{9,11},{10,... | collective-permute-start | bytes 1179656 | tf_op jit(solution)/shard_map/ppermute | solution.py:52
  15.3 10.5 %copy-start.1 = (bf16[1,1024,512]{2,1,0:T(8,128)(2,1)S(1)}, bf16[1,1024,512]{2,1,0:T(8,128)(2,1)}, u32[]{:S(2)}) copy-start(bf16[1,1024,512]{2,1,0:T(8,128)(2,1)} %param.7) | copy-start | bytes 3145732
  15.3 1.4 collective-permute-start.1
  22.4 17.8 %collective-permute-start.2 = (bf16[64,3584]{1,0:T(8,128)(2,1)S(1)}, bf16[64,3584]{1,0:T(8,128)(2,1)S(1)}, u32[]{:S(2)}, u32[]{:S(2)}) collective-permute-start(bf16[64,3584]{1,0:T(8,128)(2,1)S(1)} %get-tuple-element.43.refs_1_), channel_id=1, source_target_pairs={{0,8},{8,16},{16,24},{24,28},{28,20},{20,12},{12,4},{4,0},{1,9},{9... | collective-permute-start | bytes 1376264 | tf_op jit(solution)/shard_map/ppermute | solution.py:563
  24.4 15.8 %collective-permute-start.7 = (bf16[64,3584]{1,0:T(8,128)(2,1)S(1)}, bf16[64,3584]{1,0:T(8,128)(2,1)S(1)}, u32[]{:S(2)}, u32[]{:S(2)}) collective-permute-start(bf16[64,3584]{1,0:T(8,128)(2,1)S(1)} %get-tuple-element.44.refs_2_), channel_id=1, source_target_pairs={{8,0},{16,8},{24,16},{28,24},{20,28},{12,20},{4,12},{0,4},{9,1},{1... | collective-permute-start | bytes 1376264 | tf_op jit(solution)/shard_map/ppermute | solution.py:563
  24.5 8.9 %collective-permute-start.4 = (bf16[384,512]{1,0:T(8,128)(2,1)S(1)}, bf16[384,512]{1,0:T(8,128)(2,1)S(1)}, u32[]{:S(2)}, u32[]{:S(2)}) collective-permute-start(bf16[384,512]{1,0:T(8,128)(2,1)S(1)} %partial_blocks.4.refs_0_), channel_id=1, source_target_pairs={{0,1},{1,0},{2,3},{3,2},{4,5},{5,4},{6,7},{7,6},{8,9},{9,8},{10,11... | collective-permute-start | bytes 1179656 | tf_op jit(solution)/shard_map/ppermute | solution.py:52
  25.8 7.6 %collective-permute-start.5 = (bf16[384,512]{1,0:T(8,128)(2,1)S(1)}, bf16[384,512]{1,0:T(8,128)(2,1)S(1)}, u32[]{:S(2)}, u32[]{:S(2)}) collective-permute-start(bf16[384,512]{1,0:T(8,128)(2,1)S(1)} %collective-permute-done.3.refs_1_), channel_id=1, source_target_pairs={{0,1},{1,0},{2,3},{3,2},{4,5},{5,4},{6,7},{7,6},{8,9},{9,8},{10,11... | collective-permute-start | bytes 1179656 | tf_op jit(solution)/shard_map/ppermute | solution.py:52
  32.2 14.5 %collective-permute-start.9 = (bf16[512,512]{1,0:T(8,128)(2,1)S(1)}, bf16[512,512]{1,0:T(8,128)(2,1)}, u32[]{:S(2)}, u32[]{:S(2)}) collective-permute-start(bf16[512,512]{1,0:T(8,128)(2,1)S(1)} %partial_blocks.5.refs_4_.refs_0_), channel_id=1, source_target_pairs={{0,2},{1,3},{2,0},{3,1},{4,6},{5,7},{6,4},{7,5},{8,10},{9,11},{10,... | collective-permute-start | bytes 1572872 | tf_op jit(solution)/shard_map/ppermute | solution.py:52
  42.4 13.3 %collective-permute-start.12 = (bf16[64,3584]{1,0:T(8,128)(2,1)}, bf16[64,3584]{1,0:T(8,128)(2,1)}, u32[]{:S(2)}, u32[]{:S(2)}) collective-permute-start(bf16[64,3584]{1,0:T(8,128)(2,1)} %get-tuple-element.94.refs_1_), channel_id=1, source_target_pairs={{8,0},{16,8},{24,16},{28,24},{20,28},{12,20},{4,12},{0,4},{9,1},{1... | collective-permute-start | bytes 1376264 | tf_op jit(solution)/shard_map/ppermute | solution.py:563
  43.9 12.0 %collective-permute-start.6 = (bf16[64,3584]{1,0:T(8,128)(2,1)S(1)}, bf16[64,3584]{1,0:T(8,128)(2,1)}, u32[]{:S(2)}, u32[]{:S(2)}) collective-permute-start(bf16[64,3584]{1,0:T(8,128)(2,1)S(1)} %get-tuple-element.95.refs_0_), channel_id=1, source_target_pairs={{0,8},{8,16},{16,24},{24,28},{28,20},{20,12},{12,4},{4,0},{1,9},{9... | collective-permute-start | bytes 1376264 | tf_op jit(solution)/shard_map/ppermute | solution.py:563
  44.4 17.3 %collective-permute-start.10 = (bf16[512,512]{1,0:T(8,128)(2,1)S(1)}, bf16[512,512]{1,0:T(8,128)(2,1)}, u32[]{:S(2)}, u32[]{:S(2)}) collective-permute-start(bf16[512,512]{1,0:T(8,128)(2,1)S(1)} %partial_blocks.5.refs_4_.refs_0_), channel_id=1, source_target_pairs={{0,1},{1,0},{2,3},{3,2},{4,5},{5,4},{6,7},{7,6},{8,9},{9,8},{10,11... | collective-permute-start | bytes 1572872 | tf_op jit(solution)/shard_map/ppermute | solution.py:52
  46.7 15.1 %collective-permute-start.11 = (bf16[512,512]{1,0:T(8,128)(2,1)}, bf16[512,512]{1,0:T(8,128)(2,1)}, u32[]{:S(2)}, u32[]{:S(2)}) collective-permute-start(bf16[512,512]{1,0:T(8,128)(2,1)} %collective-permute-done.9.refs_1_), channel_id=1, source_target_pairs={{0,1},{1,0},{2,3},{3,2},{4,5},{5,4},{6,7},{7,6},{8,9},{9,8},{10,11... | collective-permute-start | bytes 1572872 | tf_op jit(solution)/shard_map/ppermute | solution.py:52
  58.3 13.4 %collective-permute-start.14 = (bf16[64,3584]{1,0:T(8,128)(2,1)}, bf16[64,3584]{1,0:T(8,128)(2,1)}, u32[]{:S(2)}, u32[]{:S(2)}) collective-permute-start(bf16[64,3584]{1,0:T(8,128)(2,1)} %get-tuple-element.92.refs_5_), channel_id=1, source_target_pairs={{8,0},{16,8},{24,16},{28,24},{20,28},{12,20},{4,12},{0,4},{9,1},{1... | collective-permute-start | bytes 1376264 | tf_op jit(solution)/shard_map/ppermute | solution.py:563
  59.9 12.8 %collective-permute-start.8 = (bf16[64,3584]{1,0:T(8,128)(2,1)S(1)}, bf16[64,3584]{1,0:T(8,128)(2,1)}, u32[]{:S(2)}, u32[]{:S(2)}) collective-permute-start(bf16[64,3584]{1,0:T(8,128)(2,1)S(1)} %get-tuple-element.93.refs_4_), channel_id=1, source_target_pairs={{0,8},{8,16},{16,24},{24,28},{28,20},{20,12},{12,4},{4,0},{1,9},{9... | collective-permute-start | bytes 1376264 | tf_op jit(solution)/shard_map/ppermute | solution.py:563
  60.4 26.1 %collective-permute-start.15 = (bf16[512,1024]{1,0:T(8,128)(2,1)S(1)}, bf16[512,1024]{1,0:T(8,128)(2,1)}, u32[]{:S(2)}, u32[]{:S(2)}) collective-permute-start(bf16[512,1024]{1,0:T(8,128)(2,1)S(1)} %copy-done.9), channel_id=1, source_target_pairs={{0,2},{1,3},{2,0},{3,1},{4,6},{5,7},{6,4},{7,5},{8,10},{9,11},{10,... | collective-permute-start | bytes 3145736 | tf_op jit(solution)/shard_map/ppermute | solution.py:52
  75.4 12.2 %collective-permute-start.17 = (bf16[64,3584]{1,0:T(8,128)(2,1)}, bf16[64,3584]{1,0:T(8,128)(2,1)}, u32[]{:S(2)}, u32[]{:S(2)}) collective-permute-start(bf16[64,3584]{1,0:T(8,128)(2,1)} %get-tuple-element.90.refs_1_), channel_id=1, source_target_pairs={{8,0},{16,8},{24,16},{28,24},{20,28},{12,20},{4,12},{0,4},{9,1},{1... | collective-permute-start | bytes 1376264 | tf_op jit(solution)/shard_map/ppermute | solution.py:563
  76.9 12.0 %collective-permute-start.13 = (bf16[64,3584]{1,0:T(8,128)(2,1)}, bf16[64,3584]{1,0:T(8,128)(2,1)}, u32[]{:S(2)}, u32[]{:S(2)}) collective-permute-start(bf16[64,3584]{1,0:T(8,128)(2,1)} %get-tuple-element.91.refs_0_), channel_id=1, source_target_pairs={{0,8},{8,16},{16,24},{24,28},{28,20},{20,12},{12,4},{4,0},{1,9},{9... | collective-permute-start | bytes 1376264 | tf_op jit(solution)/shard_map/ppermute | solution.py:563
  91.5 11.6 %collective-permute-start.21 = (bf16[64,3584]{1,0:T(8,128)(2,1)}, bf16[64,3584]{1,0:T(8,128)(2,1)}, u32[]{:S(2)}, u32[]{:S(2)}) collective-permute-start(bf16[64,3584]{1,0:T(8,128)(2,1)} %get-tuple-element.88.refs_1_), channel_id=1, source_target_pairs={{8,0},{16,8},{24,16},{28,24},{20,28},{12,20},{4,12},{0,4},{9,1},{1... | collective-permute-start | bytes 1376264 | tf_op jit(solution)/shard_map/ppermute | solution.py:563
  93.1 11.0 %collective-permute-start.16 = (bf16[64,3584]{1,0:T(8,128)(2,1)}, bf16[64,3584]{1,0:T(8,128)(2,1)}, u32[]{:S(2)}, u32[]{:S(2)}) collective-permute-start(bf16[64,3584]{1,0:T(8,128)(2,1)} %get-tuple-element.89.refs_0_), channel_id=1, source_target_pairs={{0,8},{8,16},{16,24},{24,28},{28,20},{20,12},{12,4},{4,0},{1,9},{9... | collective-permute-start | bytes 1376264 | tf_op jit(solution)/shard_map/ppermute | solution.py:563
  93.5 17.5 %collective-permute-start.19 = (bf16[512,1024]{1,0:T(8,128)(2,1)S(1)}, bf16[512,1024]{1,0:T(8,128)(2,1)}, u32[]{:S(2)}, u32[]{:S(2)}) collective-permute-start(bf16[512,1024]{1,0:T(8,128)(2,1)S(1)} %copy-done.9), channel_id=1, source_target_pairs={{0,1},{1,0},{2,3},{3,2},{4,5},{5,4},{6,7},{7,6},{8,9},{9,8},{10,11... | collective-permute-start | bytes 3145736 | tf_op jit(solution)/shard_map/ppermute | solution.py:52
  93.5 25.7 %collective-permute-start.22 = (bf16[512,1024]{1,0:T(8,128)(2,1)S(1)}, bf16[512,1024]{1,0:T(8,128)(2,1)}, u32[]{:S(2)}, u32[]{:S(2)}) collective-permute-start(bf16[512,1024]{1,0:T(8,128)(2,1)S(1)} %copy-done.6), channel_id=1, source_target_pairs={{0,2},{1,3},{2,0},{3,1},{4,6},{5,7},{6,4},{7,5},{8,10},{9,11},{10,... | collective-permute-start | bytes 3145736 | tf_op jit(solution)/shard_map/ppermute | solution.py:52
  102.6 8.5 %collective-permute-start.20 = (bf16[512,1024]{1,0:T(8,128)(2,1)}, bf16[512,1024]{1,0:T(8,128)(2,1)}, u32[]{:S(2)}, u32[]{:S(2)}) collective-permute-start(bf16[512,1024]{1,0:T(8,128)(2,1)} %collective-permute-done.15.refs_2_.refs_1_), channel_id=1, source_target_pairs={{0,1},{1,0},{2,3},{3,2},{4,5},{5,4},{6,7},{7,6},{8,9},{9,8},{10,11... | collective-permute-start | bytes 3145736 | tf_op jit(solution)/shard_map/ppermute | solution.py:52
  106.6 12.6 %collective-permute-start.26 = (bf16[64,3584]{1,0:T(8,128)(2,1)}, bf16[64,3584]{1,0:T(8,128)(2,1)}, u32[]{:S(2)}, u32[]{:S(2)}) collective-permute-start(bf16[64,3584]{1,0:T(8,128)(2,1)} %get-tuple-element.86.refs_4_), channel_id=1, source_target_pairs={{8,0},{16,8},{24,16},{28,24},{20,28},{12,20},{4,12},{0,4},{9,1},{1... | collective-permute-start | bytes 1376264 | tf_op jit(solution)/shard_map/ppermute | solution.py:563
  108.3 11.2 %collective-permute-start.18 = (bf16[64,3584]{1,0:T(8,128)(2,1)S(1)}, bf16[64,3584]{1,0:T(8,128)(2,1)}, u32[]{:S(2)}, u32[]{:S(2)}) collective-permute-start(bf16[64,3584]{1,0:T(8,128)(2,1)S(1)} %get-tuple-element.87.refs_3_), channel_id=1, source_target_pairs={{0,8},{8,16},{16,24},{24,28},{28,20},{20,12},{12,4},{4,0},{1,9},{9... | collective-permute-start | bytes 1376264 | tf_op jit(solution)/shard_map/ppermute | solution.py:563
  111.0 13.1 %collective-permute-start.24 = (bf16[512,1024]{1,0:T(8,128)(2,1)S(1)}, bf16[512,1024]{1,0:T(8,128)(2,1)}, u32[]{:S(2)}, u32[]{:S(2)}) collective-permute-start(bf16[512,1024]{1,0:T(8,128)(2,1)S(1)} %copy-done.6), channel_id=1, source_target_pairs={{0,1},{1,0},{2,3},{3,2},{4,5},{5,4},{6,7},{7,6},{8,9},{9,8},{10,11... | collective-permute-start | bytes 3145736 | tf_op jit(solution)/shard_map/ppermute | solution.py:52
  119.2 4.9 %collective-permute-start.25 = (bf16[512,1024]{1,0:T(8,128)(2,1)}, bf16[512,1024]{1,0:T(8,128)(2,1)}, u32[]{:S(2)}, u32[]{:S(2)}) collective-permute-start(bf16[512,1024]{1,0:T(8,128)(2,1)} %collective-permute-done.22.refs_2_.refs_1_), channel_id=1, source_target_pairs={{0,1},{1,0},{2,3},{3,2},{4,5},{5,4},{6,7},{7,6},{8,9},{9,8},{10,11... | collective-permute-start | bytes 3145736 | tf_op jit(solution)/shard_map/ppermute | solution.py:52
  122.0 12.9 %collective-permute-start.28 = (bf16[64,3584]{1,0:T(8,128)(2,1)}, bf16[64,3584]{1,0:T(8,128)(2,1)S(1)}, u32[]{:S(2)}, u32[]{:S(2)}) collective-permute-start(bf16[64,3584]{1,0:T(8,128)(2,1)} %get-tuple-element.84.refs_6_), channel_id=1, source_target_pairs={{8,0},{16,8},{24,16},{28,24},{20,28},{12,20},{4,12},{0,4},{9,1},{1... | collective-permute-start | bytes 1376264 | tf_op jit(solution)/shard_map/ppermute | solution.py:563
  123.8 12.6 %collective-permute-start.23 = (bf16[64,3584]{1,0:T(8,128)(2,1)}, bf16[64,3584]{1,0:T(8,128)(2,1)}, u32[]{:S(2)}, u32[]{:S(2)}) collective-permute-start(bf16[64,3584]{1,0:T(8,128)(2,1)} %get-tuple-element.85.refs_5_), channel_id=1, source_target_pairs={{0,8},{8,16},{16,24},{24,28},{28,20},{20,12},{12,4},{4,0},{1,9},{9... | collective-permute-start | bytes 1376264 | tf_op jit(solution)/shard_map/ppermute | solution.py:563
  127.1 9.3 %copy-start.7 = (f32[128,3584]{1,0:T(8,128)S(1)}, f32[128,3584]{1,0:T(8,128)}, u32[]{:S(2)}) copy-start(f32[128,3584]{1,0:T(8,128)} %g_ref.1) | copy-start | bytes 5505028
  127.1 26.0 %collective-permute-start.32 = (bf16[512,1024]{1,0:T(8,128)(2,1)S(1)}, bf16[512,1024]{1,0:T(8,128)(2,1)}, u32[]{:S(2)}, u32[]{:S(2)}) collective-permute-start(bf16[512,1024]{1,0:T(8,128)(2,1)S(1)} %copy-done.3), channel_id=1, source_target_pairs={{0,2},{1,3},{2,0},{3,1},{4,6},{5,7},{6,4},{7,5},{8,10},{9,11},{10,... | collective-permute-start | bytes 3145736 | tf_op jit(solution)/shard_map/ppermute | solution.py:52
  139.0 11.5 %collective-permute-start.29 = (bf16[64,3584]{1,0:T(8,128)(2,1)S(1)}, bf16[64,3584]{1,0:T(8,128)(2,1)S(1)}, u32[]{:S(2)}, u32[]{:S(2)}) collective-permute-start(bf16[64,3584]{1,0:T(8,128)(2,1)S(1)} %get-tuple-element.82.refs_1_), channel_id=1, source_target_pairs={{8,0},{16,8},{24,16},{28,24},{20,28},{12,20},{4,12},{0,4},{9,1},{1... | collective-permute-start | bytes 1376264 | tf_op jit(solution)/shard_map/ppermute | solution.py:622
  140.8 11.5 %collective-permute-start.27 = (bf16[64,3584]{1,0:T(8,128)(2,1)S(1)}, bf16[64,3584]{1,0:T(8,128)(2,1)S(1)}, u32[]{:S(2)}, u32[]{:S(2)}) collective-permute-start(bf16[64,3584]{1,0:T(8,128)(2,1)S(1)} %get-tuple-element.83.refs_0_), channel_id=1, source_target_pairs={{0,8},{8,16},{16,24},{24,28},{28,20},{20,12},{12,4},{4,0},{1,9},{9... | collective-permute-start | bytes 1376264 | tf_op jit(solution)/shard_map/ppermute | solution.py:622
  153.1 6.1 %collective-permute-start.33 = (bf16[512,1024]{1,0:T(8,128)(2,1)}, bf16[512,1024]{1,0:T(8,128)(2,1)S(1)}, u32[]{:S(2)}, u32[]{:S(2)}) collective-permute-start(bf16[512,1024]{1,0:T(8,128)(2,1)} %get-tuple-element.56.refs_0_), channel_id=1, source_target_pairs={{0,1},{1,0},{2,3},{3,2},{4,5},{5,4},{6,7},{7,6},{8,9},{9,8},{10,11... | collective-permute-start | bytes 3145736 | tf_op jit(solution)/shard_map/ppermute | solution.py:52
  153.1 6.1 %collective-permute-start.34 = (bf16[512,1024]{1,0:T(8,128)(2,1)}, bf16[512,1024]{1,0:T(8,128)(2,1)S(1)}, u32[]{:S(2)}, u32[]{:S(2)}) collective-permute-start(bf16[512,1024]{1,0:T(8,128)(2,1)} %get-tuple-element.57.refs_1_), channel_id=1, source_target_pairs={{0,1},{1,0},{2,3},{3,2},{4,5},{5,4},{6,7},{7,6},{8,9},{9,8},{10,11... | collective-permute-start | bytes 3145736 | tf_op jit(solution)/shard_map/ppermute | solution.py:52
  153.6 12.7 %collective-permute-start.30 = (bf16[64,3584]{1,0:T(8,128)(2,1)}, bf16[64,3584]{1,0:T(8,128)(2,1)S(1)}, u32[]{:S(2)}, u32[]{:S(2)}) collective-permute-start(bf16[64,3584]{1,0:T(8,128)(2,1)} %get-tuple-element.53.a_ref.refs_2_), channel_id=1, source_target_pairs={{0,8},{8,16},{16,24},{24,28},{28,20},{20,12},{12,4},{4,0},{1,9},{9... | collective-permute-start | bytes 1376264 | tf_op jit(solution)/shard_map/ppermute | solution.py:622
  153.9 12.4 %collective-permute-start.31 = (bf16[64,3584]{1,0:T(8,128)(2,1)}, bf16[64,3584]{1,0:T(8,128)(2,1)S(1)}, u32[]{:S(2)}, u32[]{:S(2)}) collective-permute-start(bf16[64,3584]{1,0:T(8,128)(2,1)} %get-tuple-element.54.b_ref.refs_3_), channel_id=1, source_target_pairs={{8,0},{16,8},{24,16},{28,24},{20,28},{12,20},{4,12},{0,4},{9,1},{1... | collective-permute-start | bytes 1376264 | tf_op jit(solution)/shard_map/ppermute | solution.py:622
  167.9 11.9 %collective-permute-start.35 = (bf16[64,3584]{1,0:T(8,128)(2,1)}, bf16[64,3584]{1,0:T(8,128)(2,1)S(1)}, u32[]{:S(2)}, u32[]{:S(2)}) collective-permute-start(bf16[64,3584]{1,0:T(8,128)(2,1)} %get-tuple-element.58.a_ref), channel_id=1, source_target_pairs={{0,8},{8,16},{16,24},{24,28},{28,20},{20,12},{12,4},{4,0},{1,9},{9... | collective-permute-start | bytes 1376264 | tf_op jit(solution)/shard_map/ppermute | solution.py:622
  168.1 11.6 %collective-permute-start.36 = (bf16[64,3584]{1,0:T(8,128)(2,1)}, bf16[64,3584]{1,0:T(8,128)(2,1)S(1)}, u32[]{:S(2)}, u32[]{:S(2)}) collective-permute-start(bf16[64,3584]{1,0:T(8,128)(2,1)} %get-tuple-element.59.b_ref), channel_id=1, source_target_pairs={{8,0},{16,8},{24,16},{28,24},{20,28},{12,20},{4,12},{0,4},{9,1},{1... | collective-permute-start | bytes 1376264 | tf_op jit(solution)/shard_map/ppermute | solution.py:622
  180.7 11.8 %collective-permute-start.37 = (bf16[64,3584]{1,0:T(8,128)(2,1)}, bf16[64,3584]{1,0:T(8,128)(2,1)S(1)}, u32[]{:S(2)}, u32[]{:S(2)}) collective-permute-start(bf16[64,3584]{1,0:T(8,128)(2,1)} %get-tuple-element.61.a_ref), channel_id=1, source_target_pairs={{0,8},{8,16},{16,24},{24,28},{28,20},{20,12},{12,4},{4,0},{1,9},{9... | collective-permute-start | bytes 1376264 | tf_op jit(solution)/shard_map/ppermute | solution.py:622
  181.1 11.4 %collective-permute-start.38 = (bf16[64,3584]{1,0:T(8,128)(2,1)}, bf16[64,3584]{1,0:T(8,128)(2,1)S(1)}, u32[]{:S(2)}, u32[]{:S(2)}) collective-permute-start(bf16[64,3584]{1,0:T(8,128)(2,1)} %get-tuple-element.62.b_ref), channel_id=1, source_target_pairs={{8,0},{16,8},{24,16},{28,24},{20,28},{12,20},{4,12},{0,4},{9,1},{1... | collective-permute-start | bytes 1376264 | tf_op jit(solution)/shard_map/ppermute | solution.py:622
  193.5 11.8 %collective-permute-start.39 = (bf16[64,3584]{1,0:T(8,128)(2,1)}, bf16[64,3584]{1,0:T(8,128)(2,1)S(1)}, u32[]{:S(2)}, u32[]{:S(2)}) collective-permute-start(bf16[64,3584]{1,0:T(8,128)(2,1)} %get-tuple-element.65.a_ref), channel_id=1, source_target_pairs={{0,8},{8,16},{16,24},{24,28},{28,20},{20,12},{12,4},{4,0},{1,9},{9... | collective-permute-start | bytes 1376264 | tf_op jit(solution)/shard_map/ppermute | solution.py:622
  193.8 11.4 %collective-permute-start.40 = (bf16[64,3584]{1,0:T(8,128)(2,1)}, bf16[64,3584]{1,0:T(8,128)(2,1)S(1)}, u32[]{:S(2)}, u32[]{:S(2)}) collective-permute-start(bf16[64,3584]{1,0:T(8,128)(2,1)} %get-tuple-element.66.b_ref), channel_id=1, source_target_pairs={{8,0},{16,8},{24,16},{28,24},{20,28},{12,20},{4,12},{0,4},{9,1},{1... | collective-permute-start | bytes 1376264 | tf_op jit(solution)/shard_map/ppermute | solution.py:622
  206.2 11.8 %collective-permute-start.41 = (bf16[64,3584]{1,0:T(8,128)(2,1)}, bf16[64,3584]{1,0:T(8,128)(2,1)S(1)}, u32[]{:S(2)}, u32[]{:S(2)}) collective-permute-start(bf16[64,3584]{1,0:T(8,128)(2,1)} %get-tuple-element.69.a_ref), channel_id=1, source_target_pairs={{0,8},{8,16},{16,24},{24,28},{28,20},{20,12},{12,4},{4,0},{1,9},{9... | collective-permute-start | bytes 1376264 | tf_op jit(solution)/shard_map/ppermute | solution.py:622
  206.6 11.4 %collective-permute-start.42 = (bf16[64,3584]{1,0:T(8,128)(2,1)}, bf16[64,3584]{1,0:T(8,128)(2,1)S(1)}, u32[]{:S(2)}, u32[]{:S(2)}) collective-permute-start(bf16[64,3584]{1,0:T(8,128)(2,1)} %get-tuple-element.70.b_ref), channel_id=1, source_target_pairs={{8,0},{16,8},{24,16},{28,24},{20,28},{12,20},{4,12},{0,4},{9,1},{1... | collective-permute-start | bytes 1376264 | tf_op jit(solution)/shard_map/ppermute | solution.py:622
  218.9 10.2 %collective-permute-start.43 = (bf16[64,3584]{1,0:T(8,128)(2,1)}, bf16[64,3584]{1,0:T(8,128)(2,1)S(1)}, u32[]{:S(2)}, u32[]{:S(2)}) collective-permute-start(bf16[64,3584]{1,0:T(8,128)(2,1)} %get-tuple-element.73.a_ref), channel_id=1, source_target_pairs={{0,8},{8,16},{16,24},{24,28},{28,20},{20,12},{12,4},{4,0},{1,9},{9... | collective-permute-start | bytes 1376264 | tf_op jit(solution)/shard_map/ppermute | solution.py:622
  219.3 9.8 %collective-permute-start.44 = (bf16[64,3584]{1,0:T(8,128)(2,1)}, bf16[64,3584]{1,0:T(8,128)(2,1)S(1)}, u32[]{:S(2)}, u32[]{:S(2)}) collective-permute-start(bf16[64,3584]{1,0:T(8,128)(2,1)} %get-tuple-element.74.b_ref), channel_id=1, source_target_pairs={{8,0},{16,8},{24,16},{28,24},{20,28},{12,20},{4,12},{0,4},{9,1},{1... | collective-permute-start | bytes 1376264 | tf_op jit(solution)/shard_map/ppermute | solution.py:622
  (28 other events, 46.6 us)

commit v3 on v2

--- a/solution.py
+++ b/solution.py
@@ -623,7 +623,7 @@
         if s == 0:
             send = join(send, mixed)
         if waiting:
-            send = join(send, *waiting)
+            send = [*join(send[:1], *waiting), send[1]]
         piece = s - (islands - 2 - pieces)
         if 0 <= piece < pieces:
             grad_hidden, mixed = mix_and_back(

time: 234 us -> 233 us (level)
    ppermute x7, starting transfers between devices: 2.33 us -> 10 us  [shards(): lax.ppermute(send[0], 'island', ahead)]
    ppermute x7, starting transfers between devices: 11.9 us -> 4.19 us  [shards(): lax.ppermute(send[1], 'island', back)]
    ppermute x7, starting transfers between devices: 9.81 us -> 5.91 us  [shards(): lax.ppermute(acc[1], 'island', back)]
    ppermute x7, starting transfers between devices: 4.4 us -> 8.3 us  [shards(): lax.ppermute(acc[0], 'island', ahead)]
    ppermute x7, waiting for transfers between devices: 7.66 us -> 4.24 us  [shards(): lax.ppermute(acc[1], 'island', back)]
    ppermute x7, waiting for transfers between devices: 5.27 us -> 8.06 us  [shards(): lax.ppermute(acc[0], 'island', ahead)]
where the time goes in v3:
time: 233 us
  Pallas kernels  130 us (56%)
  starting transfers between devices  37.3 us (16%)
  waiting for transfers between devices  30.6 us (13%)
  other arithmetic  17.3 us (7%)
  local copies, waits for them, and re-layouts  15.4 us (7%)
    pallas_call x5, Pallas kernels, mix_and_back(): pl.pallas_call(kernel, grid_spec=grid_of((count,), [pl.BlockSpec((tokens,...  47.2 us
    pallas_call x3, Pallas kernels, tail_rows(): pl.pallas_call(kernel, grid_spec=grid_of((count // tile,), [pl.BlockSpec(...  24.2 us
    pallas_call x3, Pallas kernels, stepped_blocks(): pl.pallas_call(kernel, grid_spec=grid_of((1,), [ANY] * (2 + len(terms) +...  19.5 us
    pallas_call x3, Pallas kernels, partial_blocks(): pl.pallas_call(kernel, grid_spec=grid_of((1,), [ANY] * (3 + extra), [ANY]...  15.8 us
    unnamed x62, local copies, waits for them, and re-layouts  15.2 us
    convert_element_type x7, other arithmetic, add(): return (a.astype(F32) + b.astype(F32)).astype(BF16)  14.8 us
    ppermute x7, starting transfers between devices, shards(): lax.ppermute(send[0], 'island', ahead)  10 us
    ppermute x17, waiting for transfers between devices, across(): return lax.ppermute(x, 'tensor', swapped(count, bit))  10 us
  transfers between devices with their start and end apart: 45, of which 17 were waited for; matrix products, arithmetic and copies ran while one was open for 6% of the time, Pallas kernels for 53%

profile of v3, /device:TPU:0, one launch (start us, length us, event | category | flops | bytes accessed | tf_op | source)
XLA Modules:
  0.0 232.6 jit_solution(5997983403477584955)
XLA Ops:
  2.6 4.0 %partial_blocks.3 = bf16[128,512]{1,0:T(8,128)(2,1)S(1)} custom-call(s32[49]{0:T(128)S(1)} %stack.263.t, bf16[4096,3584]{1,0:T(8,128)(2,1)} %bitcast.60, bf16[512,3584]{1,0:T(8,128)(2,1)} %bitcast.155, bf16[1024,512]{1,0:T(8,128)(2,1)S(1)} %bitcast.54), custom_call_target="tpu_custom_call" | custom-call | flops 1 | bytes 1 | tf_op jit(solution)/shard_map/partial_blocks/pallas_call | solution.py:165
  6.6 3.0 %collective-permute-start = (bf16[128,512]{1,0:T(8,128)(2,1)S(1)}, bf16[128,512]{1,0:T(8,128)(2,1)S(1)}, u32[]{:S(2)}, u32[]{:S(2)}) collective-permute-start(bf16[128,512]{1,0:T(8,128)(2,1)S(1)} %partial_blocks.3), channel_id=1, source_target_pairs={{0,2},{1,3},{2,0},{3,1},{4,6},{5,7},{6,4},{7,5},{8,10},{9,11},{10,... | collective-permute-start | bytes 393224 | tf_op jit(solution)/shard_map/ppermute | solution.py:52
  9.7 5.5 %partial_blocks.4.refs_0_ = bf16[384,512]{1,0:T(8,128)(2,1)S(1)} custom-call(s32[49]{0:T(128)S(1)} %stack.263.t, bf16[4096,3584]{1,0:T(8,128)(2,1)} %bitcast.61, bf16[512,3584]{1,0:T(8,128)(2,1)} %bitcast.156, bf16[1024,512]{1,0:T(8,128)(2,1)S(1)} %bitcast.55), custom_call_target="tpu_custom_call" | custom-call | flops 1 | bytes 1 | tf_op jit(solution)/shard_map/partial_blocks/pallas_call | solution.py:165
  16.7 4.1 %stepped_blocks.3 = (bf16[128,3584]{1,0:T(8,128)(2,1)S(1)}, bf16[64,3584]{1,0:T(8,128)(2,1)S(1)}, bf16[64,3584]{1,0:T(8,128)(2,1)S(1)}, bf16[128,512]{1,0:T(8,128)(2,1)S(1)}) custom-call(s32[49]{0:T(128)S(1)} %stack.263.t, bf16[4096,3584]{1,0:T(8,128)(2,1)} %bitcast.62, bf16[512,3584]{1,0:T(8,128)(2,1)} %bitcast.157, ...), custom_call_target="tpu_custom_call" | custom-call | flops 1 | bytes 1 | tf_op jit(solution)/shard_map/stepped_blocks/pallas_call | solution.py:241
  22.4 2.0 collective-permute-start.2
  25.8 6.3 %partial_blocks.5.refs_4_.refs_0_ = bf16[512,512]{1,0:T(8,128)(2,1)S(1)} custom-call(s32[49]{0:T(128)S(1)} %stack.263.t, bf16[4096,3584]{1,0:T(8,128)(2,1)} %bitcast.63, bf16[512,3584]{1,0:T(8,128)(2,1)} %bitcast.158, bf16[1024,512]{1,0:T(8,128)(2,1)S(1)} %bitcast.56, bf16[64,3584]{1,0:T(8,128)(2,1)S(1)} %get-tuple-element.31.refs_1_, ...), custom_call_target="tpu_custom_call" | custom-call | flops 1 | bytes 1 | tf_op jit(solution)/shard_map/partial_blocks/pallas_call | solution.py:165
  33.4 6.9 %stepped_blocks.4 = (bf16[384,3584]{1,0:T(8,128)(2,1)}, bf16[384,512]{1,0:T(8,128)(2,1)S(1)}) custom-call(s32[49]{0:T(128)S(1)} %stack.263.t, bf16[4096,3584]{1,0:T(8,128)(2,1)} %bitcast.64, bf16[512,3584]{1,0:T(8,128)(2,1)} %bitcast.159, bf16[384,512]{1,0:T(8,128)(2,1)S(1)} %partial_blocks.4.refs_0_, bf16[384,512]{1,0:T(8,128)(2,1)S(1)} %collective-permute-done.3.refs_1_, ...), custom_call_target="tpu_custom_call" | custom-call | flops 1 | bytes 1 | tf_op jit(solution)/shard_map/stepped_blocks/pallas_call | solution.py:241
  40.3 2.1 add_convert_fusion.10
  42.4 1.5 collective-permute-start.12
  44.4 2.3 collective-permute-done.9.refs_1_
  46.7 8.1 %tail_rows.3 = (bf16[512,1024]{1,0:T(8,128)(2,1)S(1)}, bf16[1024,3584]{1,0:T(8,128)(2,1)}) custom-call(s32[49]{0:T(128)S(1)} %stack.263.t, bf16[4096,3584]{1,0:T(8,128)(2,1)} %bitcast.65, bf16[1024,512]{1,0:T(8,128)(2,1)S(1)} %bitcast.57, bf16[512,3584]{1,0:T(8,128)(2,1)} %bitcast.160, bf16[64,3584]{1,0:T(8,128)(2,1)S(1)} %get-tuple-element.71.refs_0_, ...), custom_call_target="tpu_custom_call" | custom-call | flops 1 | bytes 1 | tf_op jit(solution)/shard_map/tail_rows/pallas_call | solution.py:288
  55.8 2.5 %add_convert_fusion.8 = (bf16[64,3584]{1,0:T(8,128)(2,1)}, bf16[64,3584]{1,0:T(8,128)(2,1)S(1)}) fusion(bf16[64,3584]{1,0:T(8,128)(2,1)} %collective-permute-done.12, bf16[384,3584]{1,0:T(8,128)(2,1)} %join.14.refs_0_, bf16[64,3584]{1,0:T(8,128)(2,1)} %collective-permute-done.6), kind=kLoop, calls=%fused_computation.10 | loop fusion | flops 1835008 | bytes 2752512 | tf_op jit(solution)/shard_map/convert_element_type | solution.py:27
  58.3 1.6 collective-permute-start.14
  60.4 1.4 collective-permute-start.15
  61.7 8.6 %stepped_blocks.5 = (bf16[512,3584]{1,0:T(8,128)(2,1)}, bf16[512,512]{1,0:T(8,128)(2,1)S(1)}) custom-call(s32[49]{0:T(128)S(1)} %stack.263.t, bf16[4096,3584]{1,0:T(8,128)(2,1)} %bitcast.66, bf16[512,3584]{1,0:T(8,128)(2,1)} %bitcast.161, bf16[512,512]{1,0:T(8,128)(2,1)S(1)} %partial_blocks.5.refs_4_.refs_0_, ...), custom_call_target="tpu_custom_call" | custom-call | flops 1 | bytes 1 | tf_op jit(solution)/shard_map/stepped_blocks/pallas_call | solution.py:241
  72.8 2.6 %add_convert_fusion.6 = (bf16[64,3584]{1,0:T(8,128)(2,1)}, bf16[64,3584]{1,0:T(8,128)(2,1)}) fusion(bf16[64,3584]{1,0:T(8,128)(2,1)} %collective-permute-done.14, bf16[384,3584]{1,0:T(8,128)(2,1)} %join.15.s_ref, bf16[64,3584]{1,0:T(8,128)(2,1)} %collective-permute-done.8), kind=kLoop, calls=%fused_computation.8 | loop fusion | flops 1835008 | bytes 2752512 | tf_op jit(solution)/shard_map/convert_element_type | solution.py:27
  76.0 1.5 collective-permute-start.17
  77.4 8.1 %tail_rows.4.refs_1_.refs_0_ = bf16[512,1024]{1,0:T(8,128)(2,1)S(1)} custom-call(s32[49]{0:T(128)S(1)} %stack.263.t, bf16[4096,3584]{1,0:T(8,128)(2,1)} %bitcast.67, bf16[1024,512]{1,0:T(8,128)(2,1)S(1)} %bitcast.58, bf16[512,3584]{1,0:T(8,128)(2,1)} %bitcast.162, bf16[64,3584]{1,0:T(8,128)(2,1)} %get-tuple-element.67.refs_0_, ...), custom_call_target="tpu_custom_call" | custom-call | flops 1 | bytes 1 | tf_op jit(solution)/shard_map/tail_rows/pallas_call | solution.py:288
  88.4 2.6 %add_convert_fusion.4 = (bf16[64,3584]{1,0:T(8,128)(2,1)}, bf16[64,3584]{1,0:T(8,128)(2,1)}) fusion(bf16[64,3584]{1,0:T(8,128)(2,1)} %collective-permute-done.17, bf16[512,3584]{1,0:T(8,128)(2,1)} %join.16.refs_0_, bf16[64,3584]{1,0:T(8,128)(2,1)} %collective-permute-done.13), kind=kLoop, calls=%fused_computation.6 | loop fusion | flops 1835008 | bytes 2752512 | tf_op jit(solution)/shard_map/convert_element_type | solution.py:27
  91.0 1.6 collective-permute-start.16
  93.1 8.1 %tail_rows.5.refs_1_.refs_0_ = bf16[512,1024]{1,0:T(8,128)(2,1)S(1)} custom-call(s32[49]{0:T(128)S(1)} %stack.263.t, bf16[4096,3584]{1,0:T(8,128)(2,1)} %bitcast.68, bf16[1024,512]{1,0:T(8,128)(2,1)S(1)} %bitcast.59, bf16[512,3584]{1,0:T(8,128)(2,1)} %bitcast.163, bf16[64,3584]{1,0:T(8,128)(2,1)} %get-tuple-element.65.refs_0_, ...), custom_call_target="tpu_custom_call" | custom-call | flops 1 | bytes 1 | tf_op jit(solution)/shard_map/tail_rows/pallas_call | solution.py:288
  103.8 2.4 %add_convert_fusion.2 = (bf16[64,3584]{1,0:T(8,128)(2,1)S(1)}, bf16[64,3584]{1,0:T(8,128)(2,1)}) fusion(bf16[64,3584]{1,0:T(8,128)(2,1)} %collective-permute-done.21, bf16[512,3584]{1,0:T(8,128)(2,1)} %join.17.refs_0_, bf16[64,3584]{1,0:T(8,128)(2,1)} %collective-permute-done.16), kind=kLoop, calls=%fused_computation.4 | loop fusion | flops 1835008 | bytes 2752512 | tf_op jit(solution)/shard_map/convert_element_type | solution.py:27
  106.2 1.6 collective-permute-start.18
  109.1 1.4 first_features.1.refs_4_
  110.6 3.0 %more_features.3.refs_1_.refs_4_ = bf16[512,4096]{1,0:T(8,128)(2,1)} custom-call(bf16[512,1024]{1,0:T(8,128)(2,1)S(1)} %copy-done.9, bf16[512,1024]{1,0:T(8,128)(2,1)} %collective-permute-done.15.refs_2_.refs_1_, bf16[512,1024]{1,0:T(8,128)(2,1)} %collective-permute-done.19.refs_2_, ...), custom_call_target="tpu_custom_call", output_to_operand_aliasing={{}: (4, {})} | custom-call | flops 1 | bytes 1 | tf_op jit(solution)/shard_map/more_features/pallas_call | solution.py:344
  113.7 5.0 %collective-permute-done.22.refs_2_.refs_1_ = bf16[512,1024]{1,0:T(8,128)(2,1)} collective-permute-done((bf16[512,1024]{1,0:T(8,128)(2,1)S(1)}, bf16[512,1024]{1,0:T(8,128)(2,1)}, u32[]{:S(2)}, u32[]{:S(2)}) %collective-permute-start.22) | collective-permute-done | bytes 1048608 | tf_op jit(solution)/shard_map/ppermute | solution.py:52
  118.9 2.6 %add_convert_fusion = (bf16[64,3584]{1,0:T(8,128)(2,1)}, bf16[64,3584]{1,0:T(8,128)(2,1)}) fusion(bf16[64,3584]{1,0:T(8,128)(2,1)} %collective-permute-done.26, bf16[512,3584]{1,0:T(8,128)(2,1)} %join.18.refs_0_, bf16[64,3584]{1,0:T(8,128)(2,1)} %collective-permute-done.18), kind=kLoop, calls=%fused_computation.2 | loop fusion | flops 1835008 | bytes 2752512 | tf_op jit(solution)/shard_map/convert_element_type | solution.py:27
  121.5 1.6 collective-permute-start.23
  123.5 3.1 %more_features.4.refs_1_.refs_4_ = bf16[512,4096]{1,0:T(8,128)(2,1)} custom-call(bf16[512,1024]{1,0:T(8,128)(2,1)S(1)} %copy-done.6, bf16[512,1024]{1,0:T(8,128)(2,1)} %collective-permute-done.22.refs_2_.refs_1_, bf16[512,1024]{1,0:T(8,128)(2,1)} %collective-permute-done.24.refs_2_, ...), custom_call_target="tpu_custom_call", output_to_operand_aliasing={{}: (4, {})} | custom-call | flops 1 | bytes 1 | tf_op jit(solution)/shard_map/more_features/pallas_call | solution.py:344
  126.6 2.0 collective-permute-start.31
  128.6 5.8 %collective-permute-done.23.a_ref = bf16[64,3584]{1,0:T(8,128)(2,1)S(1)} collective-permute-done((bf16[64,3584]{1,0:T(8,128)(2,1)}, bf16[64,3584]{1,0:T(8,128)(2,1)S(1)}, u32[]{:S(2)}, u32[]{:S(2)}) %collective-permute-start.23) | collective-permute-done | bytes 458784 | tf_op jit(solution)/shard_map/ppermute | solution.py:563
  134.4 1.4 collective-permute-done.28.b_ref
  135.8 2.6 %subtract_convert_fusion = (bf16[64,3584]{1,0:T(8,128)(2,1)S(1)}, bf16[64,3584]{1,0:T(8,128)(2,1)S(1)}) fusion(f32[128,3584]{1,0:T(8,128)} %m_ref.1, bf16[64,3584]{1,0:T(8,128)(2,1)} %collective-permute-done.28.b_ref, f32[128,3584]{1,0:T(8,128)S(1)} %copy-done.7, bf16[512,3584]{1,0:T(8,128)(2,1)} %join.19.s_ref, ...), kind=kLoop, calls=%fused_computation | loop fusion | flops 5505024 | bytes 6422528 | tf_op jit(solution)/shard_map/convert_element_type | solution.py:603
  138.4 1.6 collective-permute-start.27
  140.4 6.3 %outer_step.1 = (f32[128,3584]{1,0:T(8,128)}, f32[128,3584]{1,0:T(8,128)}, bf16[1024,3584]{1,0:T(8,128)(2,1)}) custom-call(s32[49]{0:T(128)S(1)} %stack.263.t, bf16[64,3584]{1,0:T(8,128)(2,1)S(1)} %collective-permute-done.23.a_ref, bf16[64,3584]{1,0:T(8,128)(2,1)} %collective-permute-done.28.b_ref, ...), custom_call_target="tpu_custom_call", output_to_operand_aliasing={{2}: (6, {})} | custom-call | flops 1 | bytes 1 | tf_op jit(solution)/shard_map/outer_step/pallas_call | solution.py:396
  146.8 3.2 %collective-permute-done.27.refs_0_ = bf16[64,3584]{1,0:T(8,128)(2,1)S(1)} collective-permute-done((bf16[64,3584]{1,0:T(8,128)(2,1)S(1)}, bf16[64,3584]{1,0:T(8,128)(2,1)S(1)}, u32[]{:S(2)}, u32[]{:S(2)}) %collective-permute-start.27) | collective-permute-done | bytes 458784 | tf_op jit(solution)/shard_map/ppermute | solution.py:622
  150.0 1.4 collective-permute-done.29.refs_1_
  152.7 1.7 collective-permute-start.30
  154.7 3.5 %mix_pair.2.refs_5_.refs_1_.refs_17_ = bf16[1024,3584]{1,0:T(8,128)(2,1)} custom-call(s32[49]{0:T(128)} %copy-done.13, bf16[64,3584]{1,0:T(8,128)(2,1)} %get-tuple-element.41.a_ref.refs_2_, bf16[64,3584]{1,0:T(8,128)(2,1)} %get-tuple-element.42.b_ref.refs_3_, bf16[128,3584]{1,0:T(8,128)(2,1)} %copy-done.12, ...), custom_call_target="tpu_custom_call", output_to_operand_aliasing={{}: (4, {})} | custom-call | flops 1 | bytes 1 | tf_op jit(solution)/shard_map/mix_pair/pallas_call | solution.py:431
  159.2 2.7 %more_features.5.refs_2_.l_ref = bf16[512,4096]{1,0:T(8,128)(2,1)} custom-call(bf16[512,1024]{1,0:T(8,128)(2,1)S(1)} %copy-done.4, bf16[512,1024]{1,0:T(8,128)(2,1)} %get-tuple-element.45.refs_1_, bf16[512,1024]{1,0:T(8,128)(2,1)S(1)} %collective-permute-done.32.refs_2_, bf16[512,1024]{1,0:T(8,128)(2,1)} %copy-done.24, ...), custom_call_target="tpu_custom_call", output_to_operand_aliasing={{}: (4, {})} | custom-call | flops 1 | bytes 1 | tf_op jit(solution)/shard_map/more_features/pallas_call | solution.py:344
  161.9 3.5 %collective-permute-done.30.refs_0_ = bf16[64,3584]{1,0:T(8,128)(2,1)S(1)} collective-permute-done((bf16[64,3584]{1,0:T(8,128)(2,1)}, bf16[64,3584]{1,0:T(8,128)(2,1)S(1)}, u32[]{:S(2)}, u32[]{:S(2)}) %collective-permute-start.30) | collective-permute-done | bytes 458784 | tf_op jit(solution)/shard_map/ppermute | solution.py:622
  166.2 1.7 collective-permute-start.34
  168.6 9.7 %mix_and_back.5 = (bf16[512,3584]{1,0:T(8,128)(2,1)}, bf16[1024,3584]{1,0:T(8,128)(2,1)}) custom-call(s32[49]{0:T(128)} %copy-done.13, bf16[512,4096]{1,0:T(8,128)(2,1)} %more_features.5.refs_2_.l_ref, bf16[64,3584]{1,0:T(8,128)(2,1)} %join.22.a_ref, bf16[64,3584]{1,0:T(8,128)(2,1)} %copy-done.28, ...), custom_call_target="tpu_custom_call", output_to_operand_aliasing={{1}: (22, {})} | custom-call | flops 1 | bytes 1 | tf_op jit(solution)/shard_map/mix_and_back/pallas_call | solution.py:491
  181.3 9.8 %mix_and_back.6 = (bf16[512,3584]{1,0:T(8,128)(2,1)}, bf16[1024,3584]{1,0:T(8,128)(2,1)}) custom-call(s32[49]{0:T(128)} %copy-done.13, bf16[512,4096]{1,0:T(8,128)(2,1)} %more_features.5.refs_2_.l_ref, bf16[64,3584]{1,0:T(8,128)(2,1)} %join.23.a_ref, bf16[64,3584]{1,0:T(8,128)(2,1)} %copy-done.26, ...), custom_call_target="tpu_custom_call", output_to_operand_aliasing={{1}: (22, {}), {0}: (23, {})} | custom-call | flops 1 | bytes 1 | tf_op jit(solution)/shard_map/mix_and_back/pallas_call | solution.py:491
  194.0 9.8 %mix_and_back.7 = (bf16[512,3584]{1,0:T(8,128)(2,1)}, bf16[1024,3584]{1,0:T(8,128)(2,1)}) custom-call(s32[49]{0:T(128)} %copy-done.13, bf16[512,4096]{1,0:T(8,128)(2,1)} %more_features.5.refs_2_.l_ref, bf16[64,3584]{1,0:T(8,128)(2,1)} %join.24.a_ref, bf16[64,3584]{1,0:T(8,128)(2,1)} %copy-done.25, ...), custom_call_target="tpu_custom_call", output_to_operand_aliasing={{1}: (22, {}), {0}: (23, {})} | custom-call | flops 1 | bytes 1 | tf_op jit(solution)/shard_map/mix_and_back/pallas_call | solution.py:491
  206.6 9.8 %mix_and_back.8 = (bf16[512,3584]{1,0:T(8,128)(2,1)}, bf16[1024,3584]{1,0:T(8,128)(2,1)}) custom-call(s32[49]{0:T(128)} %copy-done.13, bf16[512,4096]{1,0:T(8,128)(2,1)} %more_features.5.refs_2_.l_ref, bf16[64,3584]{1,0:T(8,128)(2,1)} %join.25.a_ref, bf16[64,3584]{1,0:T(8,128)(2,1)} %copy-done.29, ...), custom_call_target="tpu_custom_call", output_to_operand_aliasing={{1}: (22, {}), {0}: (23, {})} | custom-call | flops 1 | bytes 1 | tf_op jit(solution)/shard_map/mix_and_back/pallas_call | solution.py:491
  219.1 8.1 %mix_and_back.9 = (bf16[512,3584]{1,0:T(8,128)(2,1)}, bf16[1024,3584]{1,0:T(8,128)(2,1)}) custom-call(s32[49]{0:T(128)} %copy-done.13, bf16[512,4096]{1,0:T(8,128)(2,1)} %more_features.5.refs_2_.l_ref, bf16[64,3584]{1,0:T(8,128)(2,1)} %join.26.a_ref, bf16[64,3584]{1,0:T(8,128)(2,1)} %copy-done.30, ...), custom_call_target="tpu_custom_call", output_to_operand_aliasing={{1}: (22, {}), {0}: (23, {})} | custom-call | flops 1 | bytes 1 | tf_op jit(solution)/shard_map/mix_and_back/pallas_call | solution.py:491
  229.0 3.4 %mix_pair.3 = bf16[1024,3584]{1,0:T(8,128)(2,1)} custom-call(s32[49]{0:T(128)} %copy-done.13, bf16[64,3584]{1,0:T(8,128)(2,1)} %join.27.a_ref, bf16[64,3584]{1,0:T(8,128)(2,1)} %copy-done.27, bf16[512,3584]{1,0:T(8,128)(2,1)} %join.19.s_ref, bf16[1024,3584]{1,0:T(8,128)(2,1)} %get-tuple-element.54.refs_1_.held), custom_call_target="tpu_custom_call", output_to_operand_aliasing={{}: (4, {})} | custom-call | flops 1 | bytes 1 | tf_op jit(solution)/shard_map/mix_pair/pallas_call | solution.py:431
  (148 shorter events, 38.0 us)
Async XLA Ops:
  1.4 139.0 %copy-start.13 = (s32[49]{0:T(128)}, s32[49]{0:T(128)S(1)}, u32[]{:S(2)}) copy-start(s32[49]{0:T(128)S(1)} %stack.263.t) | copy-start | bytes 592
  6.6 8.6 %collective-permute-start = (bf16[128,512]{1,0:T(8,128)(2,1)S(1)}, bf16[128,512]{1,0:T(8,128)(2,1)S(1)}, u32[]{:S(2)}, u32[]{:S(2)}) collective-permute-start(bf16[128,512]{1,0:T(8,128)(2,1)S(1)} %partial_blocks.3), channel_id=1, source_target_pairs={{0,2},{1,3},{2,0},{3,1},{4,6},{5,7},{6,4},{7,5},{8,10},{9,11},{10,... | collective-permute-start | bytes 393224 | tf_op jit(solution)/shard_map/ppermute | solution.py:52
  15.2 10.6 %collective-permute-start.3 = (bf16[384,512]{1,0:T(8,128)(2,1)S(1)}, bf16[384,512]{1,0:T(8,128)(2,1)S(1)}, u32[]{:S(2)}, u32[]{:S(2)}) collective-permute-start(bf16[384,512]{1,0:T(8,128)(2,1)S(1)} %partial_blocks.4.refs_0_), channel_id=1, source_target_pairs={{0,2},{1,3},{2,0},{3,1},{4,6},{5,7},{6,4},{7,5},{8,10},{9,11},{10,... | collective-permute-start | bytes 1179656 | tf_op jit(solution)/shard_map/ppermute | solution.py:52
  15.3 10.5 %copy-start.1 = (bf16[1,1024,512]{2,1,0:T(8,128)(2,1)S(1)}, bf16[1,1024,512]{2,1,0:T(8,128)(2,1)}, u32[]{:S(2)}) copy-start(bf16[1,1024,512]{2,1,0:T(8,128)(2,1)} %param.7) | copy-start | bytes 3145732
  15.3 1.4 collective-permute-start.1
  22.4 17.8 %collective-permute-start.2 = (bf16[64,3584]{1,0:T(8,128)(2,1)S(1)}, bf16[64,3584]{1,0:T(8,128)(2,1)S(1)}, u32[]{:S(2)}, u32[]{:S(2)}) collective-permute-start(bf16[64,3584]{1,0:T(8,128)(2,1)S(1)} %get-tuple-element.31.refs_1_), channel_id=1, source_target_pairs={{0,8},{8,16},{16,24},{24,28},{28,20},{20,12},{12,4},{4,0},{1,9},{9... | collective-permute-start | bytes 1376264 | tf_op jit(solution)/shard_map/ppermute | solution.py:563
  24.4 15.8 %collective-permute-start.7 = (bf16[64,3584]{1,0:T(8,128)(2,1)S(1)}, bf16[64,3584]{1,0:T(8,128)(2,1)S(1)}, u32[]{:S(2)}, u32[]{:S(2)}) collective-permute-start(bf16[64,3584]{1,0:T(8,128)(2,1)S(1)} %get-tuple-element.32.refs_2_), channel_id=1, source_target_pairs={{8,0},{16,8},{24,16},{28,24},{20,28},{12,20},{4,12},{0,4},{9,1},{1... | collective-permute-start | bytes 1376264 | tf_op jit(solution)/shard_map/ppermute | solution.py:563
  24.5 8.9 %collective-permute-start.4 = (bf16[384,512]{1,0:T(8,128)(2,1)S(1)}, bf16[384,512]{1,0:T(8,128)(2,1)S(1)}, u32[]{:S(2)}, u32[]{:S(2)}) collective-permute-start(bf16[384,512]{1,0:T(8,128)(2,1)S(1)} %partial_blocks.4.refs_0_), channel_id=1, source_target_pairs={{0,1},{1,0},{2,3},{3,2},{4,5},{5,4},{6,7},{7,6},{8,9},{9,8},{10,11... | collective-permute-start | bytes 1179656 | tf_op jit(solution)/shard_map/ppermute | solution.py:52
  25.8 7.5 %collective-permute-start.5 = (bf16[384,512]{1,0:T(8,128)(2,1)S(1)}, bf16[384,512]{1,0:T(8,128)(2,1)S(1)}, u32[]{:S(2)}, u32[]{:S(2)}) collective-permute-start(bf16[384,512]{1,0:T(8,128)(2,1)S(1)} %collective-permute-done.3.refs_1_), channel_id=1, source_target_pairs={{0,1},{1,0},{2,3},{3,2},{4,5},{5,4},{6,7},{7,6},{8,9},{9,8},{10,11... | collective-permute-start | bytes 1179656 | tf_op jit(solution)/shard_map/ppermute | solution.py:52
  32.2 14.5 %collective-permute-start.9 = (bf16[512,512]{1,0:T(8,128)(2,1)S(1)}, bf16[512,512]{1,0:T(8,128)(2,1)}, u32[]{:S(2)}, u32[]{:S(2)}) collective-permute-start(bf16[512,512]{1,0:T(8,128)(2,1)S(1)} %partial_blocks.5.refs_4_.refs_0_), channel_id=1, source_target_pairs={{0,2},{1,3},{2,0},{3,1},{4,6},{5,7},{6,4},{7,5},{8,10},{9,11},{10,... | collective-permute-start | bytes 1572872 | tf_op jit(solution)/shard_map/ppermute | solution.py:52
  42.4 13.3 %collective-permute-start.12 = (bf16[64,3584]{1,0:T(8,128)(2,1)}, bf16[64,3584]{1,0:T(8,128)(2,1)}, u32[]{:S(2)}, u32[]{:S(2)}) collective-permute-start(bf16[64,3584]{1,0:T(8,128)(2,1)} %get-tuple-element.70.refs_1_), channel_id=1, source_target_pairs={{8,0},{16,8},{24,16},{28,24},{20,28},{12,20},{4,12},{0,4},{9,1},{1... | collective-permute-start | bytes 1376264 | tf_op jit(solution)/shard_map/ppermute | solution.py:563
  43.9 12.0 %collective-permute-start.6 = (bf16[64,3584]{1,0:T(8,128)(2,1)S(1)}, bf16[64,3584]{1,0:T(8,128)(2,1)}, u32[]{:S(2)}, u32[]{:S(2)}) collective-permute-start(bf16[64,3584]{1,0:T(8,128)(2,1)S(1)} %get-tuple-element.71.refs_0_), channel_id=1, source_target_pairs={{0,8},{8,16},{16,24},{24,28},{28,20},{20,12},{12,4},{4,0},{1,9},{9... | collective-permute-start | bytes 1376264 | tf_op jit(solution)/shard_map/ppermute | solution.py:563
  44.4 17.3 %collective-permute-start.10 = (bf16[512,512]{1,0:T(8,128)(2,1)S(1)}, bf16[512,512]{1,0:T(8,128)(2,1)}, u32[]{:S(2)}, u32[]{:S(2)}) collective-permute-start(bf16[512,512]{1,0:T(8,128)(2,1)S(1)} %partial_blocks.5.refs_4_.refs_0_), channel_id=1, source_target_pairs={{0,1},{1,0},{2,3},{3,2},{4,5},{5,4},{6,7},{7,6},{8,9},{9,8},{10,11... | collective-permute-start | bytes 1572872 | tf_op jit(solution)/shard_map/ppermute | solution.py:52
  46.7 15.1 %collective-permute-start.11 = (bf16[512,512]{1,0:T(8,128)(2,1)}, bf16[512,512]{1,0:T(8,128)(2,1)}, u32[]{:S(2)}, u32[]{:S(2)}) collective-permute-start(bf16[512,512]{1,0:T(8,128)(2,1)} %collective-permute-done.9.refs_1_), channel_id=1, source_target_pairs={{0,1},{1,0},{2,3},{3,2},{4,5},{5,4},{6,7},{7,6},{8,9},{9,8},{10,11... | collective-permute-start | bytes 1572872 | tf_op jit(solution)/shard_map/ppermute | solution.py:52
  58.3 13.5 %collective-permute-start.14 = (bf16[64,3584]{1,0:T(8,128)(2,1)}, bf16[64,3584]{1,0:T(8,128)(2,1)}, u32[]{:S(2)}, u32[]{:S(2)}) collective-permute-start(bf16[64,3584]{1,0:T(8,128)(2,1)} %get-tuple-element.68.refs_5_), channel_id=1, source_target_pairs={{8,0},{16,8},{24,16},{28,24},{20,28},{12,20},{4,12},{0,4},{9,1},{1... | collective-permute-start | bytes 1376264 | tf_op jit(solution)/shard_map/ppermute | solution.py:563
  60.0 12.8 %collective-permute-start.8 = (bf16[64,3584]{1,0:T(8,128)(2,1)S(1)}, bf16[64,3584]{1,0:T(8,128)(2,1)}, u32[]{:S(2)}, u32[]{:S(2)}) collective-permute-start(bf16[64,3584]{1,0:T(8,128)(2,1)S(1)} %get-tuple-element.69.refs_4_), channel_id=1, source_target_pairs={{0,8},{8,16},{16,24},{24,28},{28,20},{20,12},{12,4},{4,0},{1,9},{9... | collective-permute-start | bytes 1376264 | tf_op jit(solution)/shard_map/ppermute | solution.py:563
  60.4 26.1 %collective-permute-start.15 = (bf16[512,1024]{1,0:T(8,128)(2,1)S(1)}, bf16[512,1024]{1,0:T(8,128)(2,1)}, u32[]{:S(2)}, u32[]{:S(2)}) collective-permute-start(bf16[512,1024]{1,0:T(8,128)(2,1)S(1)} %copy-done.9), channel_id=1, source_target_pairs={{0,2},{1,3},{2,0},{3,1},{4,6},{5,7},{6,4},{7,5},{8,10},{9,11},{10,... | collective-permute-start | bytes 3145736 | tf_op jit(solution)/shard_map/ppermute | solution.py:52
  75.4 12.3 %collective-permute-start.13 = (bf16[64,3584]{1,0:T(8,128)(2,1)}, bf16[64,3584]{1,0:T(8,128)(2,1)}, u32[]{:S(2)}, u32[]{:S(2)}) collective-permute-start(bf16[64,3584]{1,0:T(8,128)(2,1)} %get-tuple-element.67.refs_0_), channel_id=1, source_target_pairs={{0,8},{8,16},{16,24},{24,28},{28,20},{20,12},{12,4},{4,0},{1,9},{9... | collective-permute-start | bytes 1376264 | tf_op jit(solution)/shard_map/ppermute | solution.py:563
  76.0 12.4 %collective-permute-start.17 = (bf16[64,3584]{1,0:T(8,128)(2,1)}, bf16[64,3584]{1,0:T(8,128)(2,1)}, u32[]{:S(2)}, u32[]{:S(2)}) collective-permute-start(bf16[64,3584]{1,0:T(8,128)(2,1)} %get-tuple-element.66.refs_1_), channel_id=1, source_target_pairs={{8,0},{16,8},{24,16},{28,24},{20,28},{12,20},{4,12},{0,4},{9,1},{1... | collective-permute-start | bytes 1376264 | tf_op jit(solution)/shard_map/ppermute | solution.py:563
  91.0 11.6 %collective-permute-start.16 = (bf16[64,3584]{1,0:T(8,128)(2,1)}, bf16[64,3584]{1,0:T(8,128)(2,1)}, u32[]{:S(2)}, u32[]{:S(2)}) collective-permute-start(bf16[64,3584]{1,0:T(8,128)(2,1)} %get-tuple-element.65.refs_0_), channel_id=1, source_target_pairs={{0,8},{8,16},{16,24},{24,28},{28,20},{20,12},{12,4},{4,0},{1,9},{9... | collective-permute-start | bytes 1376264 | tf_op jit(solution)/shard_map/ppermute | solution.py:563
  92.5 11.2 %collective-permute-start.21 = (bf16[64,3584]{1,0:T(8,128)(2,1)}, bf16[64,3584]{1,0:T(8,128)(2,1)}, u32[]{:S(2)}, u32[]{:S(2)}) collective-permute-start(bf16[64,3584]{1,0:T(8,128)(2,1)} %get-tuple-element.64.refs_1_), channel_id=1, source_target_pairs={{8,0},{16,8},{24,16},{28,24},{20,28},{12,20},{4,12},{0,4},{9,1},{1... | collective-permute-start | bytes 1376264 | tf_op jit(solution)/shard_map/ppermute | solution.py:563
  93.0 17.5 %collective-permute-start.19 = (bf16[512,1024]{1,0:T(8,128)(2,1)S(1)}, bf16[512,1024]{1,0:T(8,128)(2,1)}, u32[]{:S(2)}, u32[]{:S(2)}) collective-permute-start(bf16[512,1024]{1,0:T(8,128)(2,1)S(1)} %copy-done.9), channel_id=1, source_target_pairs={{0,1},{1,0},{2,3},{3,2},{4,5},{5,4},{6,7},{7,6},{8,9},{9,8},{10,11... | collective-permute-start | bytes 3145736 | tf_op jit(solution)/shard_map/ppermute | solution.py:52
  93.0 25.7 %collective-permute-start.22 = (bf16[512,1024]{1,0:T(8,128)(2,1)S(1)}, bf16[512,1024]{1,0:T(8,128)(2,1)}, u32[]{:S(2)}, u32[]{:S(2)}) collective-permute-start(bf16[512,1024]{1,0:T(8,128)(2,1)S(1)} %copy-done.6), channel_id=1, source_target_pairs={{0,2},{1,3},{2,0},{3,1},{4,6},{5,7},{6,4},{7,5},{8,10},{9,11},{10,... | collective-permute-start | bytes 3145736 | tf_op jit(solution)/shard_map/ppermute | solution.py:52
  102.1 8.5 %collective-permute-start.20 = (bf16[512,1024]{1,0:T(8,128)(2,1)}, bf16[512,1024]{1,0:T(8,128)(2,1)}, u32[]{:S(2)}, u32[]{:S(2)}) collective-permute-start(bf16[512,1024]{1,0:T(8,128)(2,1)} %collective-permute-done.15.refs_2_.refs_1_), channel_id=1, source_target_pairs={{0,1},{1,0},{2,3},{3,2},{4,5},{5,4},{6,7},{7,6},{8,9},{9,8},{10,11... | collective-permute-start | bytes 3145736 | tf_op jit(solution)/shard_map/ppermute | solution.py:52
  106.2 12.5 %collective-permute-start.18 = (bf16[64,3584]{1,0:T(8,128)(2,1)}, bf16[64,3584]{1,0:T(8,128)(2,1)}, u32[]{:S(2)}, u32[]{:S(2)}) collective-permute-start(bf16[64,3584]{1,0:T(8,128)(2,1)} %get-tuple-element.63.refs_3_), channel_id=1, source_target_pairs={{0,8},{8,16},{16,24},{24,28},{28,20},{20,12},{12,4},{4,0},{1,9},{9... | collective-permute-start | bytes 1376264 | tf_op jit(solution)/shard_map/ppermute | solution.py:563
  107.8 11.2 %collective-permute-start.26 = (bf16[64,3584]{1,0:T(8,128)(2,1)S(1)}, bf16[64,3584]{1,0:T(8,128)(2,1)}, u32[]{:S(2)}, u32[]{:S(2)}) collective-permute-start(bf16[64,3584]{1,0:T(8,128)(2,1)S(1)} %get-tuple-element.62.refs_4_), channel_id=1, source_target_pairs={{8,0},{16,8},{24,16},{28,24},{20,28},{12,20},{4,12},{0,4},{9,1},{1... | collective-permute-start | bytes 1376264 | tf_op jit(solution)/shard_map/ppermute | solution.py:563
  110.5 13.0 %collective-permute-start.24 = (bf16[512,1024]{1,0:T(8,128)(2,1)S(1)}, bf16[512,1024]{1,0:T(8,128)(2,1)}, u32[]{:S(2)}, u32[]{:S(2)}) collective-permute-start(bf16[512,1024]{1,0:T(8,128)(2,1)S(1)} %copy-done.6), channel_id=1, source_target_pairs={{0,1},{1,0},{2,3},{3,2},{4,5},{5,4},{6,7},{7,6},{8,9},{9,8},{10,11... | collective-permute-start | bytes 3145736 | tf_op jit(solution)/shard_map/ppermute | solution.py:52
  118.7 4.8 %collective-permute-start.25 = (bf16[512,1024]{1,0:T(8,128)(2,1)}, bf16[512,1024]{1,0:T(8,128)(2,1)}, u32[]{:S(2)}, u32[]{:S(2)}) collective-permute-start(bf16[512,1024]{1,0:T(8,128)(2,1)} %collective-permute-done.22.refs_2_.refs_1_), channel_id=1, source_target_pairs={{0,1},{1,0},{2,3},{3,2},{4,5},{5,4},{6,7},{7,6},{8,9},{9,8},{10,11... | collective-permute-start | bytes 3145736 | tf_op jit(solution)/shard_map/ppermute | solution.py:52
  121.5 12.9 %collective-permute-start.23 = (bf16[64,3584]{1,0:T(8,128)(2,1)}, bf16[64,3584]{1,0:T(8,128)(2,1)S(1)}, u32[]{:S(2)}, u32[]{:S(2)}) collective-permute-start(bf16[64,3584]{1,0:T(8,128)(2,1)} %get-tuple-element.61.refs_5_), channel_id=1, source_target_pairs={{0,8},{8,16},{16,24},{24,28},{28,20},{20,12},{12,4},{4,0},{1,9},{9... | collective-permute-start | bytes 1376264 | tf_op jit(solution)/shard_map/ppermute | solution.py:563
  123.1 12.7 %collective-permute-start.28 = (bf16[64,3584]{1,0:T(8,128)(2,1)}, bf16[64,3584]{1,0:T(8,128)(2,1)}, u32[]{:S(2)}, u32[]{:S(2)}) collective-permute-start(bf16[64,3584]{1,0:T(8,128)(2,1)} %get-tuple-element.60.refs_6_), channel_id=1, source_target_pairs={{8,0},{16,8},{24,16},{28,24},{20,28},{12,20},{4,12},{0,4},{9,1},{1... | collective-permute-start | bytes 1376264 | tf_op jit(solution)/shard_map/ppermute | solution.py:563
  126.6 9.2 %copy-start.7 = (f32[128,3584]{1,0:T(8,128)S(1)}, f32[128,3584]{1,0:T(8,128)}, u32[]{:S(2)}) copy-start(f32[128,3584]{1,0:T(8,128)} %g_ref.1) | copy-start | bytes 5505028
  126.6 25.6 %collective-permute-start.31 = (bf16[512,1024]{1,0:T(8,128)(2,1)S(1)}, bf16[512,1024]{1,0:T(8,128)(2,1)}, u32[]{:S(2)}, u32[]{:S(2)}) collective-permute-start(bf16[512,1024]{1,0:T(8,128)(2,1)S(1)} %copy-done.3), channel_id=1, source_target_pairs={{0,2},{1,3},{2,0},{3,1},{4,6},{5,7},{6,4},{7,5},{8,10},{9,11},{10,... | collective-permute-start | bytes 3145736 | tf_op jit(solution)/shard_map/ppermute | solution.py:52
  138.4 11.6 %collective-permute-start.27 = (bf16[64,3584]{1,0:T(8,128)(2,1)S(1)}, bf16[64,3584]{1,0:T(8,128)(2,1)S(1)}, u32[]{:S(2)}, u32[]{:S(2)}) collective-permute-start(bf16[64,3584]{1,0:T(8,128)(2,1)S(1)} %get-tuple-element.59.refs_0_), channel_id=1, source_target_pairs={{0,8},{8,16},{16,24},{24,28},{28,20},{20,12},{12,4},{4,0},{1,9},{9... | collective-permute-start | bytes 1376264 | tf_op jit(solution)/shard_map/ppermute | solution.py:622
  140.0 11.4 %collective-permute-start.29 = (bf16[64,3584]{1,0:T(8,128)(2,1)S(1)}, bf16[64,3584]{1,0:T(8,128)(2,1)S(1)}, u32[]{:S(2)}, u32[]{:S(2)}) collective-permute-start(bf16[64,3584]{1,0:T(8,128)(2,1)S(1)} %get-tuple-element.58.refs_1_), channel_id=1, source_target_pairs={{8,0},{16,8},{24,16},{28,24},{20,28},{12,20},{4,12},{0,4},{9,1},{1... | collective-permute-start | bytes 1376264 | tf_op jit(solution)/shard_map/ppermute | solution.py:622
  152.2 6.1 %collective-permute-start.32 = (bf16[512,1024]{1,0:T(8,128)(2,1)}, bf16[512,1024]{1,0:T(8,128)(2,1)S(1)}, u32[]{:S(2)}, u32[]{:S(2)}) collective-permute-start(bf16[512,1024]{1,0:T(8,128)(2,1)} %get-tuple-element.44.refs_0_), channel_id=1, source_target_pairs={{0,1},{1,0},{2,3},{3,2},{4,5},{5,4},{6,7},{7,6},{8,9},{9,8},{10,11... | collective-permute-start | bytes 3145736 | tf_op jit(solution)/shard_map/ppermute | solution.py:52
  152.2 6.1 %collective-permute-start.33 = (bf16[512,1024]{1,0:T(8,128)(2,1)}, bf16[512,1024]{1,0:T(8,128)(2,1)S(1)}, u32[]{:S(2)}, u32[]{:S(2)}) collective-permute-start(bf16[512,1024]{1,0:T(8,128)(2,1)} %get-tuple-element.45.refs_1_), channel_id=1, source_target_pairs={{0,1},{1,0},{2,3},{3,2},{4,5},{5,4},{6,7},{7,6},{8,9},{9,8},{10,11... | collective-permute-start | bytes 3145736 | tf_op jit(solution)/shard_map/ppermute | solution.py:52
  152.7 12.7 %collective-permute-start.30 = (bf16[64,3584]{1,0:T(8,128)(2,1)}, bf16[64,3584]{1,0:T(8,128)(2,1)S(1)}, u32[]{:S(2)}, u32[]{:S(2)}) collective-permute-start(bf16[64,3584]{1,0:T(8,128)(2,1)} %get-tuple-element.41.a_ref.refs_2_), channel_id=1, source_target_pairs={{0,8},{8,16},{16,24},{24,28},{28,20},{20,12},{12,4},{4,0},{1,9},{9... | collective-permute-start | bytes 1376264 | tf_op jit(solution)/shard_map/ppermute | solution.py:622
  154.3 13.5 %collective-permute-start.35 = (bf16[64,3584]{1,0:T(8,128)(2,1)}, bf16[64,3584]{1,0:T(8,128)(2,1)S(1)}, u32[]{:S(2)}, u32[]{:S(2)}) collective-permute-start(bf16[64,3584]{1,0:T(8,128)(2,1)} %get-tuple-element.42.b_ref.refs_3_), channel_id=1, source_target_pairs={{8,0},{16,8},{24,16},{28,24},{20,28},{12,20},{4,12},{0,4},{9,1},{1... | collective-permute-start | bytes 1376264 | tf_op jit(solution)/shard_map/ppermute | solution.py:622
  166.2 12.2 %collective-permute-start.34 = (bf16[64,3584]{1,0:T(8,128)(2,1)}, bf16[64,3584]{1,0:T(8,128)(2,1)S(1)}, u32[]{:S(2)}, u32[]{:S(2)}) collective-permute-start(bf16[64,3584]{1,0:T(8,128)(2,1)} %join.22.a_ref), channel_id=1, source_target_pairs={{0,8},{8,16},{16,24},{24,28},{28,20},{20,12},{12,4},{4,0},{1,9},{9... | collective-permute-start | bytes 1376264 | tf_op jit(solution)/shard_map/ppermute | solution.py:622
  167.8 12.7 %collective-permute-start.37 = (bf16[64,3584]{1,0:T(8,128)(2,1)S(1)}, bf16[64,3584]{1,0:T(8,128)(2,1)S(1)}, u32[]{:S(2)}, u32[]{:S(2)}) collective-permute-start(bf16[64,3584]{1,0:T(8,128)(2,1)S(1)} %collective-permute-done.35.b_ref), channel_id=1, source_target_pairs={{8,0},{16,8},{24,16},{28,24},{20,28},{12,20},{4,12},{0,4},{9,1},{1... | collective-permute-start | bytes 1376264 | tf_op jit(solution)/shard_map/ppermute | solution.py:622
  179.2 11.9 %collective-permute-start.36 = (bf16[64,3584]{1,0:T(8,128)(2,1)}, bf16[64,3584]{1,0:T(8,128)(2,1)S(1)}, u32[]{:S(2)}, u32[]{:S(2)}) collective-permute-start(bf16[64,3584]{1,0:T(8,128)(2,1)} %join.23.a_ref), channel_id=1, source_target_pairs={{0,8},{8,16},{16,24},{24,28},{28,20},{20,12},{12,4},{4,0},{1,9},{9... | collective-permute-start | bytes 1376264 | tf_op jit(solution)/shard_map/ppermute | solution.py:622
  180.5 12.7 %collective-permute-start.39 = (bf16[64,3584]{1,0:T(8,128)(2,1)S(1)}, bf16[64,3584]{1,0:T(8,128)(2,1)S(1)}, u32[]{:S(2)}, u32[]{:S(2)}) collective-permute-start(bf16[64,3584]{1,0:T(8,128)(2,1)S(1)} %collective-permute-done.37.b_ref), channel_id=1, source_target_pairs={{8,0},{16,8},{24,16},{28,24},{20,28},{12,20},{4,12},{0,4},{9,1},{1... | collective-permute-start | bytes 1376264 | tf_op jit(solution)/shard_map/ppermute | solution.py:622
  191.9 11.9 %collective-permute-start.38 = (bf16[64,3584]{1,0:T(8,128)(2,1)}, bf16[64,3584]{1,0:T(8,128)(2,1)S(1)}, u32[]{:S(2)}, u32[]{:S(2)}) collective-permute-start(bf16[64,3584]{1,0:T(8,128)(2,1)} %join.24.a_ref), channel_id=1, source_target_pairs={{0,8},{8,16},{16,24},{24,28},{28,20},{20,12},{12,4},{4,0},{1,9},{9... | collective-permute-start | bytes 1376264 | tf_op jit(solution)/shard_map/ppermute | solution.py:622
  193.2 12.6 %collective-permute-start.41 = (bf16[64,3584]{1,0:T(8,128)(2,1)S(1)}, bf16[64,3584]{1,0:T(8,128)(2,1)S(1)}, u32[]{:S(2)}, u32[]{:S(2)}) collective-permute-start(bf16[64,3584]{1,0:T(8,128)(2,1)S(1)} %collective-permute-done.39.b_ref), channel_id=1, source_target_pairs={{8,0},{16,8},{24,16},{28,24},{20,28},{12,20},{4,12},{0,4},{9,1},{1... | collective-permute-start | bytes 1376264 | tf_op jit(solution)/shard_map/ppermute | solution.py:622
  204.5 11.8 %collective-permute-start.40 = (bf16[64,3584]{1,0:T(8,128)(2,1)}, bf16[64,3584]{1,0:T(8,128)(2,1)S(1)}, u32[]{:S(2)}, u32[]{:S(2)}) collective-permute-start(bf16[64,3584]{1,0:T(8,128)(2,1)} %join.25.a_ref), channel_id=1, source_target_pairs={{0,8},{8,16},{16,24},{24,28},{28,20},{20,12},{12,4},{4,0},{1,9},{9... | collective-permute-start | bytes 1376264 | tf_op jit(solution)/shard_map/ppermute | solution.py:622
  205.8 12.6 %collective-permute-start.43 = (bf16[64,3584]{1,0:T(8,128)(2,1)S(1)}, bf16[64,3584]{1,0:T(8,128)(2,1)S(1)}, u32[]{:S(2)}, u32[]{:S(2)}) collective-permute-start(bf16[64,3584]{1,0:T(8,128)(2,1)S(1)} %collective-permute-done.41.b_ref), channel_id=1, source_target_pairs={{8,0},{16,8},{24,16},{28,24},{20,28},{12,20},{4,12},{0,4},{9,1},{1... | collective-permute-start | bytes 1376264 | tf_op jit(solution)/shard_map/ppermute | solution.py:622
  217.1 10.3 %collective-permute-start.42 = (bf16[64,3584]{1,0:T(8,128)(2,1)}, bf16[64,3584]{1,0:T(8,128)(2,1)S(1)}, u32[]{:S(2)}, u32[]{:S(2)}) collective-permute-start(bf16[64,3584]{1,0:T(8,128)(2,1)} %join.26.a_ref), channel_id=1, source_target_pairs={{0,8},{8,16},{16,24},{24,28},{28,20},{20,12},{12,4},{4,0},{1,9},{9... | collective-permute-start | bytes 1376264 | tf_op jit(solution)/shard_map/ppermute | solution.py:622
  218.3 9.9 %collective-permute-start.44 = (bf16[64,3584]{1,0:T(8,128)(2,1)S(1)}, bf16[64,3584]{1,0:T(8,128)(2,1)S(1)}, u32[]{:S(2)}, u32[]{:S(2)}) collective-permute-start(bf16[64,3584]{1,0:T(8,128)(2,1)S(1)} %collective-permute-done.43.b_ref), channel_id=1, source_target_pairs={{8,0},{16,8},{24,16},{28,24},{20,28},{12,20},{4,12},{0,4},{9,1},{1... | collective-permute-start | bytes 1376264 | tf_op jit(solution)/shard_map/ppermute | solution.py:622
  (28 other events, 45.4 us)
